TPU v7x, 128 devices: a whole 4x4x4 slice. The times are simulated.
128 devices in a mesh: ctx: 16 (over x_hi, y, core), shard: 8 (over x_lo, z).
Axes of the slice: x: 4 (x_hi: 2, x_lo: 2; x = x_hi * 2 + x_lo), y: 4, z: 4, core: 2. Of those that a mesh axis runs over, the one named last changes fastest.
Arguments:
- tokens: bfloat16 [8, 4096, 1024], P('shard', 'ctx'), may hold values from -6 to 6
- cotangent: bfloat16 [8, 4096, 1024], P('shard', 'ctx'), may hold values from -6 to 6
- segments: int32 [8, 4096], P('shard'), may hold values from 0 to 13, as said below
- positions: int32 [8, 4096], P('shard', 'ctx'), may hold values from 0 to 2303, as said below
- pad_mask: int32 [8, 4096], P('shard'), may hold values from 0 to 1, as said below
- w_in: float32 [1024, 10240], P(('ctx', 'shard')), may hold values from -0.1875 to 0.1875
- w_out: float32 [5120, 1024], P(('ctx', 'shard'))
- gains: float32 [2304], P(('ctx', 'shard')), may hold values from 0.5 to 1.5
- first_in: float32 [1024, 10240], P(('ctx', 'shard'))
- first_out: float32 [5120, 1024], P(('ctx', 'shard'))
- first_gains: float32 [2304], P(('ctx', 'shard'))
- second_in: float32 [1024, 10240], P(('ctx', 'shard')), as said below
- second_out: float32 [5120, 1024], P(('ctx', 'shard')), as said below
- second_gains: float32 [2304], P(('ctx', 'shard')), as said below
Outputs:
- output: float32 [8, 4096, 1024], P('shard', 'ctx')
- input_grad: float32 [8, 4096, 1024], P('shard', 'ctx')
- new_first_in: float32 [1024, 10240], P(('ctx', 'shard'))
- new_first_out: float32 [5120, 1024], P(('ctx', 'shard'))
- new_first_gains: float32 [2304], P(('ctx', 'shard'))
- new_second_in: float32 [1024, 10240], P(('ctx', 'shard'))
- new_second_out: float32 [5120, 1024], P(('ctx', 'shard'))
- new_second_gains: float32 [2304], P(('ctx', 'shard'))
- new_master_in: float32 [1024, 10240], P(('ctx', 'shard'))
- new_master_out: float32 [5120, 1024], P(('ctx', 'shard'))
- new_master_gains: float32 [2304], P(('ctx', 'shard'))
- copy_in: bfloat16 [1024, 10240], P(('ctx', 'shard'))
- copy_out: bfloat16 [5120, 1024], P(('ctx', 'shard'))
Inputs may be any that keep to these rules, and one draw needn't show every extreme that they name: `segments`: along the sequence index, segment numbers never fall; the last segment, of one token or more, is padding and has the number 16 / 2 + 5; a segment of 2048 tokens or more begins within the first 128 tokens of the sequence. `positions`: a token's index within its segment. `pad_mask`: 1 exactly on the tokens of all segments but the last. `second_in`: positive. `second_out`: positive. `second_gains`: positive.
All inputs are finite; a program needn't handle non-finite values.
Results may differ from a plain program's by a relative error of at most 0.02.
Values may be sent and summed in bfloat16 or wider, within the bound.
No kernel may reach another device: no remote copies, remote signals or barrier semaphores. Data moves between devices by JAX's collectives and lax.ppermute only.
A program may use at most 320 MiB of HBM per device.

v0:
```python
import math

import jax
import jax.numpy as jnp
from jax import lax
from jax.sharding import PartitionSpec as P

H_Q = 16
H_KV = 8
HD = 128
FF = 3072
STEP = 5


NORM_EPS = 1e-06
ROPE_BASE = 1000000.0
BETA_ONE = 0.5
BETA_TWO = 0.5
ADAM_EPS = 1e-08
WEIGHT_DECAY = 0.1
RATE_MATRIX = 0.03
RATE_GAIN = 0.25
MASKED = -1e30


def rms_norm(values, weight):
    return values * lax.rsqrt(jnp.mean(values * values, axis=-1, keepdims=True) + NORM_EPS) * weight


def rms_back(values, weight, upstream):
    inverse = lax.rsqrt(jnp.mean(values * values, axis=-1, keepdims=True) + NORM_EPS)
    normed = values * inverse
    scaled = upstream * weight
    grad_values = inverse * (scaled - normed * jnp.mean(scaled * normed, axis=-1, keepdims=True))
    return (grad_values, upstream * normed)


def angles(places):
    halves = jnp.arange(HD // 2, dtype=jnp.float32)
    inverse = ROPE_BASE ** (-2.0 * halves / HD)
    phase_angle = places.astype(jnp.float32)[:, None] * inverse[None, :]
    phase_angle = jnp.concatenate([phase_angle, phase_angle], axis=-1)
    return (jnp.cos(phase_angle)[:, None, :], jnp.sin(phase_angle)[:, None, :])


def rotate(values, cosine_table, sine_table):
    half_width = values.shape[-1] // 2
    turned = jnp.concatenate([-values[..., half_width:], values[..., :half_width]], axis=-1)
    return values * cosine_table + turned * sine_table


def rotate_back(upstream, cosine_table, sine_table):
    half_width = upstream.shape[-1] // 2
    turned_in = upstream * sine_table
    return upstream * cosine_table + jnp.concatenate(
        [turned_in[..., half_width:], -turned_in[..., :half_width]], axis=-1
    )


def seq_order(row_ids, half_rows, n_ctx):
    block_ids = row_ids // half_rows
    owner_dev = block_ids // 2
    place_ids = jnp.where(block_ids % 2 == 0, owner_dev, 2 * n_ctx - 1 - owner_dev)
    return place_ids * half_rows + row_ids % half_rows


def adam_step(master, first_old, second_old, gradient, rate):
    first_new = BETA_ONE * first_old + (1.0 - BETA_ONE) * gradient
    second_new = BETA_TWO * second_old + (1.0 - BETA_TWO) * gradient * gradient
    first_hat = first_new / (1.0 - BETA_ONE**STEP)
    second_hat = second_new / (1.0 - BETA_TWO**STEP)
    master_new = master - rate * (
        first_hat / (jnp.sqrt(second_hat) + ADAM_EPS) + WEIGHT_DECAY * master
    )
    return (first_new, second_new, master_new)


def body(
    tokens,
    cotangent,
    segments,
    positions,
    pad_mask,
    w_in,
    w_out,
    gains,
    first_in,
    first_out,
    first_gains,
    second_in,
    second_out,
    second_gains,
):
    tok_rows = tokens.shape[1]
    model_width = tokens.shape[2]
    key_span = segments.shape[1]
    half_rows = tok_rows // 2
    q_width = H_Q * HD
    kv_width = H_KV * HD
    attn_cols = q_width + 2 * kv_width
    repeat = H_Q // H_KV
    score_scale = 1.0 / math.sqrt(HD)
    bf16 = jnp.bfloat16
    f32 = jnp.float32
    own_in = w_in.astype(bf16)
    own_out = w_out.astype(bf16)
    own_gains = gains.astype(bf16)
    full_in, full_out, full_gains = (
        lax.all_gather(own_in, ("ctx", "shard"), axis=0, tiled=True),
        lax.all_gather(own_out, ("ctx", "shard"), axis=0, tiled=True),
        lax.all_gather(own_gains, ("ctx", "shard"), axis=0, tiled=True),
    )
    gain_vals = full_gains.astype(f32)
    gain_one = gain_vals[:model_width]
    gain_two = gain_vals[model_width : 2 * model_width]
    gain_query = gain_vals[2 * model_width : 2 * model_width + HD]
    gain_key = gain_vals[2 * model_width + HD :]
    attn_in = full_in[:, :attn_cols]
    ffn_in = full_in[:, attn_cols:]
    attn_out = full_out[:q_width]
    ffn_out = full_out[q_width:]
    inputs = tokens[0].astype(f32)
    cosine_table, sine_table = angles(positions[0])
    n_ctx = lax.axis_size("ctx")
    ctx_index = lax.axis_index("ctx")
    offset = ctx_index * tok_rows
    doc_ids = segments[0]
    live_keys = pad_mask[0]
    own_docs = lax.dynamic_slice_in_dim(doc_ids, offset, tok_rows)
    own_ids = seq_order(offset + jnp.arange(tok_rows, dtype=jnp.int32), half_rows, n_ctx)
    own_places = (ctx_index, 2 * n_ctx - 1 - ctx_index)
    normed_in = rms_norm(inputs, gain_one).astype(bf16)
    projected = jnp.dot(normed_in, attn_in, preferred_element_type=f32)
    query_raw = projected[:, :q_width].reshape(tok_rows, H_Q, HD)
    key_raw = projected[:, q_width : q_width + kv_width].reshape(tok_rows, H_KV, HD)
    value_low = projected[:, q_width + kv_width :].astype(bf16)
    query_low = (
        rotate(rms_norm(query_raw, gain_query), cosine_table, sine_table)
        .astype(bf16)
        .reshape(tok_rows, q_width)
    )
    key_low = (
        rotate(rms_norm(key_raw, gain_key), cosine_table, sine_table)
        .astype(bf16)
        .reshape(tok_rows, kv_width)
    )
    keys_full, values_full = (
        lax.all_gather(key_low, "ctx", axis=0, tiled=True),
        lax.all_gather(value_low, "ctx", axis=0, tiled=True),
    )

    def block_scores(query_block, query_ids, query_docs, key_place):
        start_row = (
            jnp.where(key_place < n_ctx, 2 * key_place, 4 * n_ctx - 1 - 2 * key_place) * half_rows
        )
        key_block = lax.dynamic_slice_in_dim(keys_full, start_row, half_rows, 0).reshape(
            half_rows, H_KV, HD
        )
        value_block = lax.dynamic_slice_in_dim(values_full, start_row, half_rows, 0).reshape(
            half_rows, H_KV, HD
        )
        key_ids = key_place * half_rows + jnp.arange(half_rows, dtype=jnp.int32)
        key_docs = lax.dynamic_slice_in_dim(doc_ids, start_row, half_rows)
        key_live = lax.dynamic_slice_in_dim(live_keys, start_row, half_rows)
        allowed = (
            (key_ids[None, :] <= query_ids[:, None])
            & (key_docs[None, :] == query_docs[:, None])
            & ((key_live[None, :] == 1) | (key_ids[None, :] == query_ids[:, None]))
        )
        scores = (
            jnp.einsum("tgre,kge->tgrk", query_block, key_block, preferred_element_type=f32)
            * score_scale
        )
        return (
            jnp.where(allowed[:, None, None, :], scores, MASKED),
            key_block,
            value_block,
            start_row,
        )

    sides = []
    for side_index in range(2):
        rows_from = side_index * half_rows
        query_block = query_low[rows_from : rows_from + half_rows].reshape(
            half_rows, H_KV, repeat, HD
        )
        sides.append(
            (
                query_block,
                own_ids[rows_from : rows_from + half_rows],
                own_docs[rows_from : rows_from + half_rows],
                own_places[side_index],
            )
        )

    def block_probs(side, key_place, row_max, row_sum):
        scores, key_block, value_block, start_row = block_scores(
            side[0], side[1], side[2], key_place
        )
        probs = jnp.exp(scores - row_max[..., None]) / row_sum[..., None]
        return (probs, key_block, value_block, start_row)

    side_stats = []
    mixed_sides = []
    for side in sides:

        def stat_step(key_place, carry):
            row_max, row_sum = carry
            scores = block_scores(side[0], side[1], side[2], key_place)[0]
            new_max = jnp.maximum(row_max, jnp.max(scores, axis=-1))
            new_sum = row_sum * jnp.exp(row_max - new_max) + jnp.sum(
                jnp.exp(scores - new_max[..., None]), axis=-1
            )
            return (new_max, new_sum)

        stat_start = (
            jnp.full((half_rows, H_KV, repeat), MASKED, f32),
            jnp.zeros((half_rows, H_KV, repeat), f32),
        )
        stat_carry = lax.fori_loop(jnp.int32(0), side[3], stat_step, stat_start)
        row_max, row_sum = stat_step(side[3], stat_carry)

        def mix_step(key_place, total):
            probs, key_block, value_block, start_row = block_probs(
                side, key_place, row_max, row_sum
            )
            return total + jnp.einsum(
                "tgrk,kge->tgre", probs.astype(bf16), value_block, preferred_element_type=f32
            )

        mixed = lax.fori_loop(
            jnp.int32(0), side[3], mix_step, jnp.zeros((half_rows, H_KV, repeat, HD), f32)
        )
        mixed = mix_step(side[3], mixed)
        side_stats.append((row_max, row_sum))
        mixed_sides.append(mixed.reshape(half_rows, q_width))
    attn_low = jnp.concatenate(mixed_sides, axis=0).astype(bf16)
    residual = inputs + jnp.dot(attn_low, attn_out, preferred_element_type=f32)
    normed_mid = rms_norm(residual, gain_two).astype(bf16)
    gate_up = jnp.dot(normed_mid, ffn_in, preferred_element_type=f32)
    gate_pre = gate_up[:, :FF]
    up_pre = gate_up[:, FF:]
    sigmoid_gate = jax.nn.sigmoid(gate_pre)
    activated = gate_pre * sigmoid_gate
    hidden_low = (activated * up_pre).astype(bf16)
    output = residual + jnp.dot(hidden_low, ffn_out, preferred_element_type=f32)
    upstream = cotangent[0]
    grad_hidden = jnp.einsum("td,fd->tf", upstream, ffn_out, preferred_element_type=f32)
    grad_gate_up = jnp.concatenate(
        [
            grad_hidden * up_pre * sigmoid_gate * (1.0 + gate_pre * (1.0 - sigmoid_gate)),
            grad_hidden * activated,
        ],
        axis=1,
    ).astype(bf16)
    grad_mid = jnp.einsum("tc,dc->td", grad_gate_up, ffn_in, preferred_element_type=f32)
    grad_resid_part, gain_two_terms = rms_back(residual, gain_two, grad_mid)
    grad_residual = upstream.astype(f32) + grad_resid_part
    resid_low = grad_residual.astype(bf16)
    grad_attn = jnp.einsum("td,qd->tq", resid_low, attn_out, preferred_element_type=f32).astype(
        bf16
    )

    def add_rows(total, start_row, piece):
        current = lax.dynamic_slice_in_dim(total, start_row, half_rows, 0)
        return lax.dynamic_update_slice_in_dim(total, current + piece, start_row, 0)

    key_acc = jnp.zeros((key_span, kv_width), f32)
    value_acc = jnp.zeros((key_span, kv_width), f32)
    query_sides = []
    for side_index in range(2):
        side = sides[side_index]
        row_max, row_sum = side_stats[side_index]
        rows_from = side_index * half_rows
        grad_block = grad_attn[rows_from : rows_from + half_rows].reshape(
            half_rows, H_KV, repeat, HD
        )

        def delta_step(key_place, total):
            probs, key_block, value_block, start_row = block_probs(
                side, key_place, row_max, row_sum
            )
            grad_probs = jnp.einsum(
                "tgre,kge->tgrk", grad_block, value_block, preferred_element_type=f32
            )
            return total + jnp.sum(probs * grad_probs, axis=-1)

        row_delta = lax.fori_loop(
            jnp.int32(0), side[3], delta_step, jnp.zeros((half_rows, H_KV, repeat), f32)
        )
        row_delta = delta_step(side[3], row_delta)

        def grad_step(key_place, carry):
            query_part, key_part, value_part = carry
            probs, key_block, value_block, start_row = block_probs(
                side, key_place, row_max, row_sum
            )
            grad_probs = jnp.einsum(
                "tgre,kge->tgrk", grad_block, value_block, preferred_element_type=f32
            )
            grad_scores = (probs * (grad_probs - row_delta[..., None])).astype(bf16)
            query_part = (
                query_part
                + jnp.einsum("tgrk,kge->tgre", grad_scores, key_block, preferred_element_type=f32)
                * score_scale
            )
            key_piece = (
                jnp.einsum("tgrk,tgre->kge", grad_scores, side[0], preferred_element_type=f32)
                * score_scale
            )
            value_piece = jnp.einsum(
                "tgrk,tgre->kge", probs.astype(bf16), grad_block, preferred_element_type=f32
            )
            key_part = add_rows(key_part, start_row, key_piece.reshape(half_rows, kv_width))
            value_part = add_rows(value_part, start_row, value_piece.reshape(half_rows, kv_width))
            return (query_part, key_part, value_part)

        grad_start = (jnp.zeros((half_rows, H_KV, repeat, HD), f32), key_acc, value_acc)
        grad_carry = lax.fori_loop(jnp.int32(0), side[3], grad_step, grad_start)
        query_part, key_acc, value_acc = grad_step(side[3], grad_carry)
        query_sides.append(query_part.reshape(half_rows, H_Q, HD))
    grad_keys, grad_values = (
        lax.psum_scatter(
            key_acc.astype(jnp.bfloat16), "ctx", scatter_dimension=0, tiled=True
        ).astype(jnp.float32),
        lax.psum_scatter(
            value_acc.astype(jnp.bfloat16), "ctx", scatter_dimension=0, tiled=True
        ).astype(jnp.float32),
    )
    grad_query = jnp.concatenate(query_sides, axis=0)
    query_back, gain_query_terms = rms_back(
        query_raw, gain_query, rotate_back(grad_query, cosine_table, sine_table)
    )
    key_back, gain_key_terms = rms_back(
        key_raw,
        gain_key,
        rotate_back(grad_keys.reshape(tok_rows, H_KV, HD), cosine_table, sine_table),
    )
    grad_projected = jnp.concatenate(
        [query_back.reshape(tok_rows, q_width), key_back.reshape(tok_rows, kv_width), grad_values],
        axis=1,
    ).astype(bf16)
    grad_normed_in = jnp.einsum("tc,dc->td", grad_projected, attn_in, preferred_element_type=f32)
    grad_in_part, gain_one_terms = rms_back(inputs, gain_one, grad_normed_in)
    input_grad = grad_residual + grad_in_part
    grad_w_in = jnp.concatenate(
        [
            jnp.einsum("td,tc->dc", normed_in, grad_projected, preferred_element_type=f32),
            jnp.einsum("td,tc->dc", normed_mid, grad_gate_up, preferred_element_type=f32),
        ],
        axis=1,
    )
    grad_w_out = jnp.concatenate(
        [
            jnp.einsum("tq,td->qd", attn_low, resid_low, preferred_element_type=f32),
            jnp.einsum("tf,td->fd", hidden_low, upstream, preferred_element_type=f32),
        ],
        axis=0,
    )
    grad_gains = jnp.concatenate(
        [
            jnp.sum(gain_one_terms, axis=0),
            jnp.sum(gain_two_terms, axis=0),
            jnp.sum(gain_query_terms, axis=(0, 1)),
            jnp.sum(gain_key_terms, axis=(0, 1)),
        ]
    )
    owned_in, owned_out, owned_gains = (
        lax.psum_scatter(grad_w_in, ("ctx", "shard"), scatter_dimension=0, tiled=True),
        lax.psum_scatter(grad_w_out, ("ctx", "shard"), scatter_dimension=0, tiled=True),
        lax.psum_scatter(grad_gains, ("ctx", "shard"), scatter_dimension=0, tiled=True),
    )
    new_first_in, new_second_in, new_master_in = adam_step(
        w_in, first_in, second_in, owned_in, RATE_MATRIX
    )
    new_first_out, new_second_out, new_master_out = adam_step(
        w_out, first_out, second_out, owned_out, RATE_MATRIX
    )
    new_first_gains, new_second_gains, new_master_gains = adam_step(
        gains, first_gains, second_gains, owned_gains, RATE_GAIN
    )
    return (
        output[None],
        input_grad[None],
        new_first_in,
        new_first_out,
        new_first_gains,
        new_second_in,
        new_second_out,
        new_second_gains,
        new_master_in,
        new_master_out,
        new_master_gains,
        new_master_in.astype(bf16),
        new_master_out.astype(bf16),
    )


def solution(mesh):
    in_specs = (
        P("shard", "ctx", None),
        P("shard", "ctx", None),
        P("shard", None),
        P("shard", "ctx"),
        P("shard", None),
        P(("ctx", "shard"), None),
        P(("ctx", "shard"), None),
        P(("ctx", "shard")),
        P(("ctx", "shard"), None),
        P(("ctx", "shard"), None),
        P(("ctx", "shard")),
        P(("ctx", "shard"), None),
        P(("ctx", "shard"), None),
        P(("ctx", "shard")),
    )
    out_specs = (
        P("shard", "ctx", None),
        P("shard", "ctx", None),
        P(("ctx", "shard"), None),
        P(("ctx", "shard"), None),
        P(("ctx", "shard")),
        P(("ctx", "shard"), None),
        P(("ctx", "shard"), None),
        P(("ctx", "shard")),
        P(("ctx", "shard"), None),
        P(("ctx", "shard"), None),
        P(("ctx", "shard")),
        P(("ctx", "shard"), None),
        P(("ctx", "shard"), None),
    )
    return jax.shard_map(body, mesh=mesh, in_specs=in_specs, out_specs=out_specs, check_vma=False)
```

profile of v0, /device:TPU:96, one launch (start us, length us, event | category | flops | bytes accessed | tf_op | source)
XLA Modules:
  0.0 3022.8 jit_solution(15351358783828262563)
XLA Ops:
  9.8 64.9 %all-reduce = bf16[2304]{0:T(1024)(128)(2,1)S(1)} all-reduce(bf16[2304]{0:T(1024)(128)(2,1)S(1)} %dynamic-update-slice), channel_id=1, replica_groups=mesh['ctx'=16,'shard'=8] {'ctx','shard'}, use_global_device_ids=true, to_apply=%add | all-reduce | flops 2304 | bytes 9216
  76.0 268.7 %all-gather.5.cloned.1.call-done = bf16[1024,10240]{1,0:T(8,128)(2,1)} async-done(((bf16[8,10240]{1,0:T(8,128)(2,1)}), bf16[1024,10240]{1,0:T(8,128)(2,1)}) %all-gather.5.cloned.1.call-update) | async-done | bytes 20971536 | tf_op jit(solution)/shard_map/all_gather | solution.py:109
  344.8 6.0 fusion.78
  373.9 54.1 %all-gather.7.cloned.1.call-done = bf16[4096,1024]{1,0:T(8,128)(2,1)} async-done(((bf16[256,1024]{1,0:T(8,128)(2,1)}), bf16[4096,1024]{1,0:T(8,128)(2,1)}) %all-gather.7.cloned.1.call-update) | async-done | bytes 8388624 | tf_op jit(solution)/shard_map/all_gather | solution.py:149
  428.0 73.8 %all-gather.9.cloned.1.call-done = bf16[4096,1024]{1,0:T(8,128)(2,1)} async-done(((bf16[256,1024]{1,0:T(8,128)(2,1)}), bf16[4096,1024]{1,0:T(8,128)(2,1)}) %all-gather.9.cloned.1.call-update) | async-done | bytes 8388624 | tf_op jit(solution)/shard_map/all_gather | solution.py:148
  505.1 11.7 copy.334
  517.2 101.3 %while.94 = (s32[]{:T(128)}, f32[128,8,2]{0,2,1:T(2,128)S(1)}, f32[128,8,2]{0,2,1:T(2,128)S(1)}, s32[]{:T(128)}, s32[128]{0:T(128)S(1)}, /*index=5*/s32[4096]{0:...) while((s32[]{:T(128)}, f32[128,8,2]{0,2,1:T(2,128)S(1)}, ...), condition=%wide.region_14.15_spmd, body=%wide.region_11.14_spmd.sunk | while | flops 68522248 | bytes 3551773 | solution.py:220
  620.0 11.8 copy.333
  633.3 198.8 %while.95 = (s32[]{:T(128)}, f32[128,8,2,128]{0,3,2,1:T(8,128)}, s32[]{:T(128)}, bf16[4096,1024]{0,1:T(8,128)(2,1)}, s32[128]{0:T(128)S(1)}, /*index=5*/s32[4096...) while((s32[]{:T(128)}, f32[128,8,2,128]{0,3,2,1:T(8,128)}, ...), condition=%wide.region_18.19_spmd, body=%wide.region_17.18_spmd.sunk | while | flops 135889168 | bytes 4248109 | solution.py:231
  655.9 3.0 fusion.322
  662.4 3.0 fusion.322
  675.2 3.0 fusion.322
  688.0 3.0 fusion.322
  707.2 3.0 fusion.322
  713.7 3.0 fusion.322
  720.1 3.0 fusion.322
  739.3 3.0 fusion.322
  745.7 3.0 fusion.322
  752.1 3.0 fusion.322
  771.4 3.0 fusion.322
  777.8 3.0 fusion.322
  803.4 3.0 fusion.322
  809.9 3.0 fusion.322
  838.5 4.1 multiply_reduce_fusion.9
  842.6 11.1 fusion.74
  853.7 6.1 multiply_convert_fusion.1
  859.8 8.4 multiply_reduce_fusion.4
  868.6 3.9 fusion.89
  888.6 7.9 broadcast.898
  896.4 7.9 broadcast.898.clone
  907.3 195.0 %while.98 = (s32[]{:T(128)}, f32[128,8,2]{0,2,1:T(2,128)S(1)}, s32[]{:T(128)}, s32[128]{0:T(128)S(1)}, s32[4096]{0:T(1024)}, /*index=5*/s32[128]{0:T(128)S(1)}, ...) while((s32[]{:T(128)}, f32[128,8,2]{0,2,1:T(2,128)S(1)}, ...), condition=%wide.region_29.30_spmd, body=%wide.region_27.29_spmd.sunk | while | flops 135889152 | bytes 4805173 | solution.py:288
  1106.6 272.1 %while.99 = (s32[]{:T(128)}, f32[128,8,2,128]{0,3,2,1:T(8,128)S(1)}, f32[4096,1024]{0,1:T(8,128)}, f32[4096,1024]{0,1:T(8,128)}, s32[]{:T(128)}, /*index=5*/bf16...) while((s32[]{:T(128)}, ...), condition=%wide.region_32.33_spmd, body=%wide.region_31.32_spmd.sunk | while | flops 338657536 | bytes 17101424 | solution.py:319
  1378.8 17.4 copy.377
  1402.3 9.1 convert_element_type.125
  1411.5 18.0 copy.382
  1433.4 9.3 convert_element_type.127
  1448.3 12.2 pad_maximum_fusion.1
  1481.8 5.1 multiply_reduce_fusion
  1487.0 10.8 fusion.97
  1497.8 14.1 reduce-scatter.5.cloned.1.call-done
  1518.6 98.5 %reduce-scatter.7.cloned.1.call-done = bf16[256,1024]{1,0:T(8,128)(2,1)} async-done(((bf16[4096,1024]{1,0:T(8,128)(2,1)}), bf16[256,1024]{1,0:T(8,128)(2,1)}) %reduce-scatter.7.cloned.1.call-update) | async-done | bytes 524304 | tf_op jit(solution)/shard_map/reduce_scatter | solution.py:326
  1617.1 9.3 fusion.144
  1626.4 28.6 pad_maximum_fusion
  1655.1 6.2 fusion.116
  1661.4 6.9 fusion.132
  1668.4 65.4 %all-reduce.1 = f32[2304]{0:T(1024)S(1)} all-reduce(f32[2304]{0:T(1024)S(1)} %pad_maximum_fusion.15), channel_id=6, replica_groups=mesh['ctx'=16,'shard'=8] {'ctx','shard'}, use_global_device_ids=true, to_apply=%region_46.47.clone | all-reduce | flops 2304 | bytes 18432
  1736.9 549.5 %reduce-scatter.11.cloned.1.call-done = f32[40,1024]{1,0:T(8,128)} async-done(((f32[5120,1024]{1,0:T(8,128)}), f32[40,1024]{1,0:T(8,128)}) %reduce-scatter.11.cloned.1.call-update) | async-done | bytes 163856 | tf_op jit(solution)/shard_map/reduce_scatter | solution.py:370
  2288.2 725.4 %reduce-scatter.9.cloned.1.call-done = f32[8,10240]{1,0:T(8,128)} async-done(((f32[1024,10240]{1,0:T(8,128)}), f32[8,10240]{1,0:T(8,128)}) %reduce-scatter.9.cloned.1.call-update) | async-done | bytes 327696 | tf_op jit(solution)/shard_map/reduce_scatter | solution.py:369
  (1474 shorter events, 833.3 us)
Async XLA Ops:
  7.2 337.6 %all-gather.5.cloned.1.call-start = ((), (), s32[]{:S(2)}) async-start(), calls=%async_computation.4 | async-start | bytes 21135360 | tf_op jit(solution)/shard_map/all_gather | solution.py:109
  8.9 419.1 %all-gather.7.cloned.1.call-start = ((), (), s32[]{:S(2)}) async-start(), calls=%async_computation.5 | async-start | bytes 8912896 | tf_op jit(solution)/shard_map/all_gather | solution.py:149
  76.0 274.8 %copy-start.68 = (f32[256]{0:T(256)}, f32[256]{0:T(256)S(1)}, u32[]{:S(2)}) copy-start(f32[256]{0:T(256)S(1)} %add_rsqrt_fusion.3) | copy-start | bytes 3076
  76.0 274.8 %copy-start.55 = (f32[1024]{0:T(1024)}, f32[1024]{0:T(1024)S(1)}, u32[]{:S(2)}) copy-start(f32[1024]{0:T(1024)S(1)} %get-tuple-element.1328) | copy-start | bytes 12292
  76.0 792.2 %copy-start.57 = (f32[1024]{0:T(1024)}, f32[1024]{0:T(1024)S(1)}, u32[]{:S(2)}) copy-start(f32[1024]{0:T(1024)S(1)} %get-tuple-element.1327) | copy-start | bytes 12292
  344.8 9.0 copy-start.75
  353.7 148.0 %all-gather.9.cloned.1.call-start = ((), (), s32[]{:S(2)}) async-start(), calls=%async_computation.6 | async-start | bytes 8912896 | tf_op jit(solution)/shard_map/all_gather | solution.py:148
  354.4 15.0 copy-start.20
  354.5 15.0 copy-start.35
  354.5 14.9 copy-start.70
  362.3 476.2 %all-gather.11.cloned.1.call-start = ((), (), s32[]{:S(2)}) async-start(), calls=%async_computation.7 | async-start | bytes 10567680 | tf_op jit(solution)/shard_map/all_gather | solution.py:110
  363.0 1148.8 %reduce-scatter.5.cloned.1.call-start = ((), (), s32[]{:S(2)}) async-start(), calls=%async_computation.8 | async-start | bytes 8912896 | tf_op jit(solution)/shard_map/reduce_scatter | solution.py:323
  503.2 13.6 copy-start.39
  504.2 114.4 %copy-start.37 = (bf16[128,1024]{0,1:T(8,128)(2,1)}, bf16[128,1024]{0,1:T(8,128)(2,1)S(1)}, u32[]{:S(2)}) copy-start(bf16[128,1024]{0,1:T(8,128)(2,1)S(1)} %copy.331) | copy-start | bytes 786436
  517.2 366.3 %copy-start.8 = (f32[128,8,2,128]{0,3,2,1:T(8,128)}, f32[128,8,2,128]{0,3,2,1:T(8,128)S(1)}, u32[]{:S(2)}) copy-start(f32[128,8,2,128]{0,3,2,1:T(8,128)S(1)} %get-tuple-element.1334) | copy-start | bytes 3145732
  620.0 12.0 copy-start.9
  838.4 15.3 slice-start
  842.6 25.7 copy-start.27
  842.6 25.7 copy-start.66
  842.6 11.1 copy-start.43
  842.6 11.1 slice-start.1
  842.6 11.1 slice-start.2
  859.8 8.4 copy-start.46
  859.8 8.4 copy-start.48
  875.2 8.3 copy-start.61
  1411.5 205.6 %reduce-scatter.7.cloned.1.call-start = ((), (), s32[]{:S(2)}) async-start(), calls=%async_computation.9 | async-start | bytes 8912896 | tf_op jit(solution)/shard_map/reduce_scatter | solution.py:326
  1442.7 843.7 %reduce-scatter.11.cloned.1.call-start = ((), (), s32[]{:S(2)}) async-start(), calls=%async_computation.11 | async-start | bytes 21135360 | tf_op jit(solution)/shard_map/reduce_scatter | solution.py:370
  1460.6 6.0 copy-start.23
  1460.6 5.9 copy-start.38
  1460.6 1553.1 %reduce-scatter.9.cloned.1.call-start = ((), (), s32[]{:S(2)}) async-start(), calls=%async_computation.10 | async-start | bytes 42270720 | tf_op jit(solution)/shard_map/reduce_scatter | solution.py:369
  1463.8 6.8 copy-start.10
  1516.0 101.1 %copy-start.26 = (bf16[1,256,1024]{2,1,0:T(8,128)(2,1)S(1)}, bf16[1,256,1024]{2,1,0:T(8,128)(2,1)}, u32[]{:S(2)}) copy-start(bf16[1,256,1024]{2,1,0:T(8,128)(2,1)} %param.30) | copy-start | bytes 1572868
  1516.0 101.1 %copy-start.31 = (bf16[256,2048]{1,0:T(8,128)(2,1)S(1)}, bf16[256,2048]{1,0:T(8,128)(2,1)}, u32[]{:S(2)}) copy-start(bf16[256,2048]{1,0:T(8,128)(2,1)} %get-tuple-element.1297) | copy-start | bytes 3145732
  1516.0 101.1 %copy-start.56 = (f32[1024]{0:T(1024)S(1)}, f32[1024]{0:T(1024)}, u32[]{:S(2)}) copy-start(f32[1024]{0:T(1024)} %copy-done.55) | copy-start | bytes 12292
  1516.0 101.1 %copy-start.69 = (f32[256]{0:T(256)S(1)}, f32[256]{0:T(256)}, u32[]{:S(2)}) copy-start(f32[256]{0:T(256)} %copy-done.68) | copy-start | bytes 3076
  1655.1 6.3 copy-start.32
  1655.1 6.3 copy-start.53
  1661.4 7.0 copy-start.74
  1661.4 72.4 %copy-start.76 = (f32[18]{0:T(128)S(1)}, f32[18]{0:T(128)}, u32[]{:S(2)}) copy-start(f32[18]{0:T(128)} %param.37) | copy-start | bytes 220
  1661.4 72.4 %copy-start.77 = (f32[18]{0:T(128)S(1)}, f32[18]{0:T(128)}, u32[]{:S(2)}) copy-start(f32[18]{0:T(128)} %param.43) | copy-start | bytes 220
  1661.4 72.4 %copy-start.78 = (f32[18]{0:T(128)S(1)}, f32[18]{0:T(128)}, u32[]{:S(2)}) copy-start(f32[18]{0:T(128)} %param.40) | copy-start | bytes 220
  1661.4 73.0 %copy-start.19 = (f32[256,1024]{1,0:T(8,128)S(1)}, f32[256,1024]{1,0:T(8,128)}, u32[]{:S(2)}) copy-start(f32[256,1024]{1,0:T(8,128)} %copy-done.18) | copy-start | bytes 3145732
  1668.3 618.1 %copy-start.52 = (f32[40,1024]{1,0:T(8,128)S(1)}, f32[40,1024]{1,0:T(8,128)}, u32[]{:S(2)}) copy-start(f32[40,1024]{1,0:T(8,128)} %param.36) | copy-start | bytes 491524
  1668.3 618.1 %copy-start.62 = (f32[40,1024]{1,0:T(8,128)S(1)}, f32[40,1024]{1,0:T(8,128)}, u32[]{:S(2)}) copy-start(f32[40,1024]{1,0:T(8,128)} %param.42) | copy-start | bytes 491524
  1668.3 618.1 %copy-start.63 = (f32[40,1024]{1,0:T(8,128)S(1)}, f32[40,1024]{1,0:T(8,128)}, u32[]{:S(2)}) copy-start(f32[40,1024]{1,0:T(8,128)} %param.39) | copy-start | bytes 491524
  1668.3 1345.4 %copy-start.50 = (f32[8,10240]{1,0:T(8,128)S(1)}, f32[8,10240]{1,0:T(8,128)}, u32[]{:S(2)}) copy-start(f32[8,10240]{1,0:T(8,128)} %param.35) | copy-start | bytes 983044
  1668.3 1345.3 %copy-start.59 = (f32[8,10240]{1,0:T(8,128)S(1)}, f32[8,10240]{1,0:T(8,128)}, u32[]{:S(2)}) copy-start(f32[8,10240]{1,0:T(8,128)} %param.41) | copy-start | bytes 983044
  1668.3 1345.3 %copy-start.60 = (f32[8,10240]{1,0:T(8,128)S(1)}, f32[8,10240]{1,0:T(8,128)}, u32[]{:S(2)}) copy-start(f32[8,10240]{1,0:T(8,128)} %param.38) | copy-start | bytes 983044
  (71 other events, 134.2 us)
Sparse Core Ops, SparseCore 0:
  10.3 334.4 all-gather.4
  353.8 74.1 all-gather.6
  431.0 70.6 all-gather.8
  503.9 315.6 all-gather.10
  1411.6 100.2 reduce-scatter.4
  1516.0 101.0 reduce-scatter.6
  1619.5 666.9 reduce-scatter.10
  2288.8 724.7 reduce-scatter.8
where the time goes:
time: 3060 us; the launch traced here: 3020 us
  waiting for transfers between devices  1780 us (58%)
  local copies, waits for them, and re-layouts  414 us (14%)
  matrix products  376 us (12%)
  other arithmetic  295 us (10%)
  blocking collectives  130 us (4%)
    reduce_scatter x1, waiting for transfers between devices, body(): lax.psum_scatter(grad_w_in, ('ctx', 'shard'), scatter_dimension=0, tiled=...  725 us
    reduce_scatter x1, waiting for transfers between devices, body(): lax.psum_scatter(grad_w_out, ('ctx', 'shard'), scatter_dimension=0, tiled...  550 us
    all_gather x1, waiting for transfers between devices, body(): lax.all_gather(own_in, ('ctx', 'shard'), axis=0, tiled=True)  269 us
    unnamed x2, blocking collectives  130 us
    dynamic_slice x95, local copies, waits for them, and re-layouts, block_scores(): lax.dynamic_slice_in_dim(keys_full, start_row, half_rows, 0)  116 us
    dot_general x95, matrix products, block_scores(): jnp.einsum('tgre,kge->tgrk', query_block, key_block, preferred_element_ty...  103 us
    reduce_scatter x1, waiting for transfers between devices, body(): lax.psum_scatter(value_acc.astype(jnp.bfloat16), 'ctx', scatter_dimension...  98.5 us
    dot_general x33, matrix products, mix_step(): jnp.einsum('tgrk,kge->tgre', probs.astype(bf16), value_block, preferred_e...  97.2 us
  transfers between devices with their start and end apart: 8, of which 7 were waited for; matrix products, arithmetic and copies ran while one was open for 16% of the time, Pallas kernels for 0%

commit v1 on v0

v1 whole, which is shorter than its diff:
```python
import functools
import math

import jax
import jax.numpy as jnp
from jax import lax
from jax.experimental import pallas as pl
from jax.experimental.pallas import tpu as pltpu
from jax.sharding import Mesh
from jax.sharding import PartitionSpec as P

H_Q = 16
H_KV = 8
HD = 128
FF = 3072
STEP = 5

NORM_EPS = 1e-06
ROPE_BASE = 1000000.0
BETA_ONE = 0.5
BETA_TWO = 0.5
ADAM_EPS = 1e-08
WEIGHT_DECAY = 0.1
RATE_MATRIX = 0.03
RATE_GAIN = 0.25

CTX = ("xh", "y", "core")
SHARD = ("xl", "z")
EVERY = CTX + SHARD
AXIS_X = ("xh", "xl")
AXIS_YZ = ("y", "z", "core")
SIZES = {"xh": 2, "y": 4, "core": 2, "xl": 2, "z": 4}

LOG2_E = 1.4426950408889634
SCORE_SCALE = 1.0 / math.sqrt(HD)
BQ = 256
BK = 512
VMEM_BYTES = 48 * 1024 * 1024

bf16 = jnp.bfloat16
f32 = jnp.float32


def rms_norm(values, weight):
    return values * lax.rsqrt(jnp.mean(values * values, axis=-1, keepdims=True) + NORM_EPS) * weight


def rms_back(values, weight, upstream):
    inverse = lax.rsqrt(jnp.mean(values * values, axis=-1, keepdims=True) + NORM_EPS)
    normed = values * inverse
    scaled = upstream * weight
    grad_values = inverse * (scaled - normed * jnp.mean(scaled * normed, axis=-1, keepdims=True))
    return (grad_values, upstream * normed)


def dot_nt(a, b):
    return lax.dot_general(a, b, (((1,), (1,)), ((), ())), preferred_element_type=f32)


def dot_tn(a, b):
    return lax.dot_general(a, b, (((0,), (0,)), ((), ())), preferred_element_type=f32)


def dot_nn(a, b):
    return lax.dot_general(a, b, (((1,), (0,)), ((), ())), preferred_element_type=f32)


def project_kernel(a_ref, w_ref, cos_ref, sin_ref, gq_ref, gk_ref, send_ref, qraw_ref, kraw_ref):
    prod = dot_nn(a_ref[...], w_ref[...])
    cos = cos_ref[...]
    sin = sin_ref[...]

    def roped(raw, gain):
        normed = rms_norm(raw, gain)
        return normed * cos + pltpu.roll(normed, HD // 2, 1) * sin

    key_raw = prod[:, 2 * HD : 3 * HD]
    key = roped(key_raw, gk_ref[...]).astype(bf16)
    value = prod[:, 3 * HD :].astype(bf16)
    kraw_ref[0] = key_raw
    for r in range(2):
        raw = prod[:, r * HD : (r + 1) * HD]
        qraw_ref[r] = raw
        send_ref[r, 0] = (roped(raw, gq_ref[...]) * (SCORE_SCALE * LOG2_E)).astype(bf16)
        send_ref[r, 1] = key
        send_ref[r, 2] = value


def project(a, w, cos, sin, gq, gk):
    rows, width = a.shape
    whole = lambda j: (0, 0)
    return pl.pallas_call(
        project_kernel,
        grid=(H_KV,),
        in_specs=[
            pl.BlockSpec((rows, width), whole),
            pl.BlockSpec((width, 4 * HD), lambda j: (0, j)),
            pl.BlockSpec((rows, HD), whole),
            pl.BlockSpec((rows, HD), whole),
            pl.BlockSpec((1, HD), whole),
            pl.BlockSpec((1, HD), whole),
        ],
        out_specs=[
            pl.BlockSpec((2, 3, rows, HD), lambda j: (j, 0, 0, 0)),
            pl.BlockSpec((2, rows, HD), lambda j: (j, 0, 0)),
            pl.BlockSpec((1, rows, HD), lambda j: (j, 0, 0)),
        ],
        out_shape=[
            jax.ShapeDtypeStruct((H_Q, 3, rows, HD), bf16),
            jax.ShapeDtypeStruct((H_Q, rows, HD), f32),
            jax.ShapeDtypeStruct((H_KV, rows, HD), f32),
        ],
        compiler_params=pltpu.CompilerParams(vmem_limit_bytes=VMEM_BYTES),
        name="project",
    )(a, w, cos, sin, gq, gk)


def project_back_kernel(
    recv_ref, qraw_ref, kraw_ref, cos_ref, sin_ref, gq_ref, gk_ref, w_ref, at_ref, dw_ref, da_ref, dg_ref
):
    step = pl.program_id(0)
    cos = cos_ref[...]
    sin = sin_ref[...]

    def back(raw, gain, grad):
        unrot = grad * cos + pltpu.roll(grad * sin, HD // 2, 1)
        return rms_back(raw, gain, unrot)

    pieces = []
    gq_terms = jnp.zeros((1, HD), f32)
    for r in range(2):
        grad, terms = back(qraw_ref[r], gq_ref[...], recv_ref[r, 0].astype(f32))
        pieces.append(grad.astype(bf16))
        gq_terms = gq_terms + jnp.sum(terms, axis=0, keepdims=True)
    grad_key = recv_ref[0, 1].astype(f32) + recv_ref[1, 1].astype(f32)
    grad, terms = back(kraw_ref[0], gk_ref[...], grad_key)
    gk_terms = jnp.sum(terms, axis=0, keepdims=True)
    pieces.append(grad.astype(bf16))
    pieces.append((recv_ref[0, 2].astype(f32) + recv_ref[1, 2].astype(f32)).astype(bf16))
    dproj = jnp.concatenate(pieces, axis=1)
    dw_ref[...] = dot_nn(at_ref[...], dproj).astype(bf16)
    part = dot_nt(dproj, w_ref[...])
    both = jnp.concatenate([gq_terms, gk_terms, jnp.zeros((6, HD), f32)], axis=0)

    @pl.when(step == 0)
    def _():
        da_ref[...] = part
        dg_ref[...] = both

    @pl.when(step > 0)
    def _():
        da_ref[...] += part
        dg_ref[...] += both


def project_back(recv, qraw, kraw, cos, sin, gq, gk, w, at):
    width, rows = at.shape
    whole = lambda j: (0, 0)
    return pl.pallas_call(
        project_back_kernel,
        grid=(H_KV,),
        in_specs=[
            pl.BlockSpec((2, 3, rows, HD), lambda j: (j, 0, 0, 0)),
            pl.BlockSpec((2, rows, HD), lambda j: (j, 0, 0)),
            pl.BlockSpec((1, rows, HD), lambda j: (j, 0, 0)),
            pl.BlockSpec((rows, HD), whole),
            pl.BlockSpec((rows, HD), whole),
            pl.BlockSpec((1, HD), whole),
            pl.BlockSpec((1, HD), whole),
            pl.BlockSpec((width, 4 * HD), lambda j: (0, j)),
            pl.BlockSpec((width, rows), whole),
        ],
        out_specs=[
            pl.BlockSpec((width, 4 * HD), lambda j: (0, j)),
            pl.BlockSpec((rows, width), whole),
            pl.BlockSpec((8, HD), whole),
        ],
        out_shape=[
            jax.ShapeDtypeStruct((width, 4 * HD * H_KV), bf16),
            jax.ShapeDtypeStruct((rows, width), f32),
            jax.ShapeDtypeStruct((8, HD), f32),
        ],
        compiler_params=pltpu.CompilerParams(vmem_limit_bytes=VMEM_BYTES),
        name="project_back",
    )(recv, qraw, kraw, cos, sin, gq, gk, w, at)


def dealt_slot(place, n_dev):
    if place < n_dev:
        return place, 0
    return 2 * n_dev - 1 - place, 1


def key_mask(len_row, offset):
    ahead = (
        lax.broadcasted_iota(jnp.int32, (BK, BQ), 1)
        - lax.broadcasted_iota(jnp.int32, (BK, BQ), 0)
        + offset
    )
    return (ahead >= 0) & (ahead <= len_row)


def attend_kernel(klo_ref, x_ref, len_ref, osend_ref, onat_ref, linv_ref, qn, kn, vt):
    n_dev = x_ref.shape[0]
    half = x_ref.shape[2] // 2
    span = qn.shape[0]
    for place in range(2 * n_dev):
        dev, side = dealt_slot(place, n_dev)
        rows = slice(side * half, (side + 1) * half)
        to = slice(place * half, (place + 1) * half)
        qn[to, :] = x_ref[dev, 0, rows, :]
        kn[to, :] = x_ref[dev, 1, rows, :]
        vt[:, to] = x_ref[dev, 2, rows, :].astype(f32).T.astype(bf16)

    def q_step(qb, _):
        q_at = pl.multiple_of(qb * BQ, BQ)
        q_blk = qn[pl.ds(q_at, BQ), :]
        len_row = len_ref[pl.ds(qb, 1), :]

        def k_step(kb, carry):
            acc, total = carry
            k_at = pl.multiple_of(kb * BK, BK)
            s = dot_nt(kn[pl.ds(k_at, BK), :], q_blk)
            p = jnp.where(key_mask(len_row, q_at - k_at), jnp.exp2(s), 0.0)
            total = total + jnp.sum(p.reshape(BK // 8, 8, BQ), axis=0)
            acc = acc + dot_nn(vt[:, pl.ds(k_at, BK)], p.astype(bf16))
            return acc, total

        acc, total = lax.fori_loop(
            klo_ref[qb],
            (q_at + BQ - 1) // BK + 1,
            k_step,
            (jnp.zeros((HD, BQ), f32), jnp.zeros((8, BQ), f32)),
        )
        inverse = 1.0 / jnp.sum(total, axis=0, keepdims=True)
        linv_ref[pl.ds(qb, 1), :] = inverse
        out = (acc * inverse).T
        onat_ref[pl.ds(q_at, BQ), :] = out
        return 0

    lax.fori_loop(0, span // BQ, q_step, 0)
    for place in range(2 * n_dev):
        dev, side = dealt_slot(place, n_dev)
        osend_ref[dev, side * half : (side + 1) * half, :] = onat_ref[
            place * half : (place + 1) * half, :
        ].astype(bf16)


def vmem():
    return pl.BlockSpec(memory_space=pltpu.VMEM)


def attend(klo, x, lens):
    n_dev, _, rows, _ = x.shape
    span = n_dev * rows
    return pl.pallas_call(
        attend_kernel,
        in_specs=[pl.BlockSpec(memory_space=pltpu.SMEM), vmem(), vmem()],
        out_specs=[vmem(), vmem(), vmem()],
        out_shape=[
            jax.ShapeDtypeStruct((n_dev, rows, HD), bf16),
            jax.ShapeDtypeStruct((span, HD), f32),
            jax.ShapeDtypeStruct((span // BQ, BQ), f32),
        ],
        scratch_shapes=[
            pltpu.VMEM((span, HD), bf16),
            pltpu.VMEM((span, HD), bf16),
            pltpu.VMEM((HD, span), bf16),
        ],
        compiler_params=pltpu.CompilerParams(vmem_limit_bytes=VMEM_BYTES),
        name="attend",
    )(klo, x, lens)


def attend_back_kernel(
    klo_ref, x_ref, do_ref, onat_ref, linv_ref, len_ref, send_ref, qn, kn, vn, kt, don, dq, dk, dv
):
    n_dev = x_ref.shape[0]
    half = x_ref.shape[2] // 2
    span = qn.shape[0]
    for place in range(2 * n_dev):
        dev, side = dealt_slot(place, n_dev)
        rows = slice(side * half, (side + 1) * half)
        to = slice(place * half, (place + 1) * half)
        qn[to, :] = x_ref[dev, 0, rows, :]
        key = x_ref[dev, 1, rows, :]
        kn[to, :] = key
        kt[:, to] = key.astype(f32).T.astype(bf16)
        vn[to, :] = x_ref[dev, 2, rows, :]
        don[to, :] = do_ref[dev, rows, :]
    dk[...] = jnp.zeros_like(dk)
    dv[...] = jnp.zeros_like(dv)

    def q_step(qb, _):
        q_at = pl.multiple_of(qb * BQ, BQ)
        q_blk = qn[pl.ds(q_at, BQ), :]
        do_blk = don[pl.ds(q_at, BQ), :]
        len_row = len_ref[pl.ds(qb, 1), :]
        inverse = linv_ref[pl.ds(qb, 1), :]
        mixed = (do_blk.astype(f32) * onat_ref[pl.ds(q_at, BQ), :]).T
        delta = jnp.sum(mixed, axis=0, keepdims=True)

        def k_step(kb, acc):
            k_at = pl.multiple_of(kb * BK, BK)
            here = pl.ds(k_at, BK)
            s = dot_nt(kn[here, :], q_blk)
            p = jnp.where(key_mask(len_row, q_at - k_at), jnp.exp2(s) * inverse, 0.0)
            dp = dot_nt(vn[here, :], do_blk)
            ds = (p * (dp - delta)).astype(bf16)
            dv[here, :] += dot_nn(p.astype(bf16), do_blk)
            dk[here, :] += dot_nn(ds, q_blk)
            return acc + dot_nn(kt[:, here], ds)

        acc = lax.fori_loop(
            klo_ref[qb], (q_at + BQ - 1) // BK + 1, k_step, jnp.zeros((HD, BQ), f32)
        )
        dq[pl.ds(q_at, BQ), :] = (acc * SCORE_SCALE).T
        return 0

    lax.fori_loop(0, span // BQ, q_step, 0)
    for place in range(2 * n_dev):
        dev, side = dealt_slot(place, n_dev)
        rows = slice(side * half, (side + 1) * half)
        at = slice(place * half, (place + 1) * half)
        send_ref[dev, 0, rows, :] = dq[at, :].astype(bf16)
        send_ref[dev, 1, rows, :] = (dk[at, :] * (1.0 / LOG2_E)).astype(bf16)
        send_ref[dev, 2, rows, :] = dv[at, :].astype(bf16)


def attend_back(klo, x, do, onat, linv, lens):
    n_dev, _, rows, _ = x.shape
    span = n_dev * rows
    return pl.pallas_call(
        attend_back_kernel,
        in_specs=[pl.BlockSpec(memory_space=pltpu.SMEM)] + [vmem()] * 5,
        out_specs=vmem(),
        out_shape=jax.ShapeDtypeStruct((n_dev, 3, rows, HD), bf16),
        scratch_shapes=[
            pltpu.VMEM((span, HD), bf16),
            pltpu.VMEM((span, HD), bf16),
            pltpu.VMEM((span, HD), bf16),
            pltpu.VMEM((HD, span), bf16),
            pltpu.VMEM((span, HD), bf16),
            pltpu.VMEM((span, HD), f32),
            pltpu.VMEM((span, HD), f32),
            pltpu.VMEM((span, HD), f32),
        ],
        compiler_params=pltpu.CompilerParams(vmem_limit_bytes=VMEM_BYTES),
        name="attend_back",
    )(klo, x, do, onat, linv, lens)


OUT_ROWS = 160
CHUNK_ROWS = 32
N_CHUNKS = 3
CHUNK = FF // N_CHUNKS


def middle_kernel(
    full_ref,
    mixed_ref,
    tok_ref,
    cot_ref,
    gain_ref,
    shuffle_ref,
    gate_ref,
    up_ref,
    out_ref,
    dres_ref,
    dob_ref,
    feat_ref,
    drb_ref,
    grad_ref,
    dgain_ref,
    w_out,
    resid,
    mid_low,
    grad_mid,
    grad_up,
    sems,
):
    step = pl.program_id(0)
    q_width = H_Q * HD
    width = tok_ref.shape[1]

    def fetch(i):
        return pltpu.make_async_copy(
            full_ref.at[i, pl.ds(0, OUT_ROWS), :],
            w_out.at[pl.ds(i * OUT_ROWS, OUT_ROWS), :],
            sems.at[i],
        )

    n_fetch = full_ref.shape[0]
    n_first = -(-q_width // OUT_ROWS)

    @pl.when(step == 0)
    def _():
        for i in range(n_fetch):
            fetch(i).start()
        for h in range(H_Q):
            feat_ref[:, h * HD : (h + 1) * HD] = mixed_ref[h]
        for i in range(n_first):
            fetch(i).wait()
        residual = tok_ref[...].astype(f32) + dot_nn(feat_ref[:, :q_width], w_out[:q_width, :])
        resid[...] = residual
        out_ref[...] = residual
        normed = rms_norm(residual, gain_ref[...]).astype(bf16)
        mid_low[...] = dot_nn(normed, shuffle_ref[...]).astype(bf16)
        grad_mid[...] = jnp.zeros_like(grad_mid)
        for i in range(n_first, n_fetch):
            fetch(i).wait()

    @pl.when((step > 0) & (step < 2 * N_CHUNKS + 1) & (step % 2 == 1))
    def _():
        at = pl.multiple_of(q_width + ((step - 1) // 2) * CHUNK, CHUNK)
        gate_w = gate_ref[...].reshape(width, CHUNK)
        gate = dot_nn(mid_low[...], gate_w)
        up = dot_nn(mid_low[...], up_ref[...].reshape(width, CHUNK))
        sigmoid_gate = 1.0 / (1.0 + jnp.exp(-gate))
        activated = gate * sigmoid_gate
        hidden = (activated * up).astype(bf16)
        feat_ref[:, pl.ds(at, CHUNK)] = hidden
        down_w = w_out[pl.ds(at, CHUNK), :]
        out_ref[...] += dot_nn(hidden, down_w)
        grad_hidden = dot_nt(cot_ref[...], down_w)
        grad_up[...] = (grad_hidden * activated).astype(bf16)
        grad_gate = (
            grad_hidden * up * sigmoid_gate * (1.0 + gate * (1.0 - sigmoid_gate))
        ).astype(bf16)
        grad_mid[...] += dot_nt(grad_gate, gate_w)
        grad_ref[...] = dot_tn(mid_low[...], grad_gate).astype(bf16).reshape(grad_ref.shape)

    @pl.when((step > 0) & (step < 2 * N_CHUNKS + 1) & (step % 2 == 0))
    def _():
        grad_mid[...] += dot_nt(grad_up[...], up_ref[...].reshape(width, CHUNK))
        grad_ref[...] = dot_tn(mid_low[...], grad_up[...]).astype(bf16).reshape(grad_ref.shape)

    @pl.when(step == 2 * N_CHUNKS + 1)
    def _():
        grad = dot_nt(grad_mid[...].astype(bf16), shuffle_ref[...])
        part, terms = rms_back(resid[...], gain_ref[...], grad)
        dgain_ref[...] = jnp.sum(terms, axis=0, keepdims=True)
        dres = cot_ref[...].astype(f32) + part
        dres_ref[...] = dres
        low = dres.astype(bf16)
        drb_ref[...] = low
        for c in range(4):
            piece = dot_nt(low, w_out[c * 4 * HD : (c + 1) * 4 * HD, :]).astype(bf16)
            for h in range(4):
                dob_ref[4 * c + h] = piece[:, h * HD : (h + 1) * HD]


def middle(full, mixed, tok, cot, gain, shuffle):
    rows, width = tok.shape
    n_blocks = full.shape[0]
    first = OUT_ROWS // CHUNK_ROWS
    q_width = H_Q * HD

    def chunk_of(i):
        return jnp.clip((i - 1) // 2, 0, N_CHUNKS - 1)

    def grad_at(i):
        i = jnp.clip(i, 1, 2 * N_CHUNKS)
        return (0, first + N_CHUNKS * ((i - 1) % 2) + (i - 1) // 2, 0)

    def whole(shape):
        return pl.BlockSpec(shape, lambda i: (0,) * len(shape))

    return pl.pallas_call(
        middle_kernel,
        grid=(2 * N_CHUNKS + 2,),
        in_specs=[
            pl.BlockSpec(memory_space=pl.ANY),
            whole((H_Q, rows, HD)),
            whole((rows, width)),
            whole((rows, width)),
            whole((1, width)),
            whole((width, width)),
            pl.BlockSpec((n_blocks, CHUNK_ROWS, CHUNK), lambda i: (0, first + chunk_of(i), 0)),
            pl.BlockSpec(
                (n_blocks, CHUNK_ROWS, CHUNK), lambda i: (0, first + N_CHUNKS + chunk_of(i), 0)
            ),
        ],
        out_specs=[
            whole((rows, width)),
            whole((rows, width)),
            whole((H_Q, rows, HD)),
            whole((rows, q_width + FF)),
            whole((rows, width)),
            pl.BlockSpec((n_blocks, CHUNK_ROWS, CHUNK), grad_at),
            whole((1, width)),
        ],
        out_shape=[
            jax.ShapeDtypeStruct((rows, width), f32),
            jax.ShapeDtypeStruct((rows, width), f32),
            jax.ShapeDtypeStruct((H_Q, rows, HD), bf16),
            jax.ShapeDtypeStruct((rows, q_width + FF), bf16),
            jax.ShapeDtypeStruct((rows, width), bf16),
            jax.ShapeDtypeStruct(full.shape, bf16),
            jax.ShapeDtypeStruct((1, width), f32),
        ],
        scratch_shapes=[
            pltpu.VMEM((q_width + FF, width), bf16),
            pltpu.VMEM((rows, width), f32),
            pltpu.VMEM((rows, width), bf16),
            pltpu.VMEM((rows, width), f32),
            pltpu.VMEM((rows, CHUNK), bf16),
            pltpu.SemaphoreType.DMA((n_blocks,)),
        ],
        compiler_params=pltpu.CompilerParams(vmem_limit_bytes=VMEM_BYTES),
        name="middle",
    )(full, mixed, tok, cot, gain, shuffle, full, full)


def grad_out_kernel(feat_ref, drb_ref, cot_ref, grads_ref, out_ref):
    step = pl.program_id(0)
    q_width = H_Q * HD
    block = feat_ref.shape[1]
    both = q_width // block
    cut = q_width % block

    def store(value):
        out_ref[...] = value.astype(bf16).reshape(out_ref.shape)

    @pl.when(step < both)
    def _():
        store(dot_tn(feat_ref[...], drb_ref[...]))

    @pl.when(step == both)
    def _():
        upper = dot_tn(feat_ref[:, :cut], drb_ref[...])
        lower = dot_tn(feat_ref[:, cut:], cot_ref[...])
        store(jnp.concatenate([upper, lower], axis=0))

    @pl.when(step > both)
    def _():
        store(dot_tn(feat_ref[...], cot_ref[...]))


def grad_out(feat, drb, cot, grads):
    rows, n_features = feat.shape
    width = drb.shape[1]
    blocks = 4
    return pl.pallas_call(
        grad_out_kernel,
        grid=(grads.shape[0] // blocks,),
        in_specs=[
            pl.BlockSpec((rows, blocks * OUT_ROWS), lambda i: (0, i)),
            pl.BlockSpec((rows, width), lambda i: (0, 0)),
            pl.BlockSpec((rows, width), lambda i: (0, 0)),
            pl.BlockSpec(memory_space=pl.ANY),
        ],
        out_specs=pl.BlockSpec((blocks, OUT_ROWS, width), lambda i: (i, 0, 0)),
        out_shape=jax.ShapeDtypeStruct(grads.shape, bf16),
        input_output_aliases={3: 0},
        compiler_params=pltpu.CompilerParams(vmem_limit_bytes=VMEM_BYTES),
        name="grad_out",
    )(feat, drb, cot, grads)


def adam_step(master, first_old, second_old, gradient, rate):
    first_new = BETA_ONE * first_old + (1.0 - BETA_ONE) * gradient
    second_new = BETA_TWO * second_old + (1.0 - BETA_TWO) * gradient * gradient
    first_hat = first_new / (1.0 - BETA_ONE**STEP)
    second_hat = second_new / (1.0 - BETA_TWO**STEP)
    master_new = master - rate * (
        first_hat / (jnp.sqrt(second_hat) + ADAM_EPS) + WEIGHT_DECAY * master
    )
    return (first_new, second_new, master_new)


def gathered(x):
    return lax.all_gather(x, AXIS_YZ, axis=0, tiled=True)


def sum_over_x(blocks):
    me = lax.axis_index(AXIS_X)
    n = blocks.shape[0]

    def block(i):
        return lax.dynamic_index_in_dim(blocks, lax.rem(i, n), 0, keepdims=False)

    total = block(me).astype(f32)
    for shift in range(1, n):
        pairs = [(i, (i + shift) % n) for i in range(n)]
        total = total + lax.ppermute(block(me + shift), AXIS_X, pairs).astype(f32)
    return total


def natural_of_permuted(x):
    tail = x.shape[1:]
    x = x.reshape((4, 4, 2, 2, 2) + tail)
    x = x.transpose((3, 0, 2, 4, 1) + tuple(range(5, 5 + len(tail))))
    return x.reshape((128,) + tail)


def owner_pairs():
    pairs = []
    for n in range(128):
        z = n % 4
        xl = (n // 4) % 2
        core = (n // 8) % 2
        y = (n // 16) % 4
        xh = n // 64
        pairs.append((n, (((y * 4 + z) * 2 + core) * 2 + xh) * 2 + xl))
    return pairs


def body(
    tokens,
    cotangent,
    segments,
    positions,
    pad_mask,
    w_in,
    w_out,
    gains,
    first_in,
    first_out,
    first_gains,
    second_in,
    second_out,
    second_gains,
):
    rows = tokens.shape[1]
    width = tokens.shape[2]
    span = segments.shape[1]
    half = rows // 2
    n_ctx = span // rows
    q_width = H_Q * HD
    kv_width = H_KV * HD
    attn_cols = q_width + 2 * kv_width
    owned = w_in.shape[0]
    owned_gains = gains.shape[0]

    low_in = w_in.astype(bf16)
    own_qkv = jnp.concatenate(
        [
            low_in[:, :q_width].reshape(owned, H_KV, 2 * HD),
            low_in[:, q_width : q_width + kv_width].reshape(owned, H_KV, HD),
            low_in[:, q_width + kv_width : attn_cols].reshape(owned, H_KV, HD),
        ],
        axis=2,
    ).reshape(owned, attn_cols)
    own_gains = jnp.pad(gains.astype(bf16)[None, :], ((0, owned - 1), (0, HD - owned_gains)))
    packed = jnp.concatenate([own_qkv, own_gains, low_in[:, attn_cols:]], axis=1)
    packed = lax.all_gather(packed, AXIS_X, axis=0, tiled=True)
    w_qkv = gathered(packed[:, : attn_cols + HD])
    pairs = owner_pairs()
    own_out = lax.ppermute(w_out.astype(bf16), EVERY, [(p, n) for n, p in pairs])
    own_out = lax.all_gather(own_out, AXIS_X, axis=0, tiled=True)
    own_ffn = packed[:, attn_cols + HD :].reshape(CHUNK_ROWS, 2 * N_CHUNKS, CHUNK)
    own_ffn = own_ffn.transpose(1, 0, 2).reshape(2 * N_CHUNKS * CHUNK_ROWS, CHUNK)
    full = gathered(jnp.concatenate([own_out, own_ffn], axis=0)[None])

    gain_rows = w_qkv[:, attn_cols:].reshape(width // owned, owned, HD)[:, 0, :owned_gains]
    gain_vals = natural_of_permuted(gain_rows).reshape(-1).astype(f32)
    gain_one = gain_vals[:width]
    gain_two = gain_vals[width : 2 * width]
    gain_query = gain_vals[2 * width : 2 * width + HD].reshape(1, HD)
    gain_key = gain_vals[2 * width + HD :].reshape(1, HD)

    order = natural_of_permuted(jnp.arange(width, dtype=jnp.int32).reshape(width // owned, owned)).reshape(-1)
    shuffle = (order[:, None] == jnp.arange(width, dtype=jnp.int32)[None, :]).astype(bf16)

    inputs = tokens[0].astype(f32)
    halves = jnp.arange(HD // 2, dtype=f32)
    inverse = ROPE_BASE ** (-2.0 * halves / HD)
    angle = positions[0].astype(f32)[:, None] * inverse[None, :]
    cos_half = jnp.cos(angle)
    sin_half = jnp.sin(angle)
    cos = jnp.concatenate([cos_half, cos_half], axis=1)
    sin = jnp.concatenate([-sin_half, sin_half], axis=1)

    def natural(x):
        x = x.reshape(n_ctx, 2, half)
        return jnp.concatenate([x[:, 0], x[::-1, 1]], axis=0)

    docs = natural(segments[0])
    live = natural(pad_mask[0])
    at = jnp.arange(span, dtype=jnp.int32).reshape(2 * n_ctx, half)
    start = jnp.zeros_like(docs)
    for number in range(1, 14):
        before = jnp.sum((docs < number).astype(jnp.int32))
        start = jnp.where(docs == number, before, start)
    lens = jnp.where(live == 1, at - start, 0)
    klo = jnp.min((at - lens).reshape(span // BQ, BQ), axis=1) // BK
    lens = lens.reshape(span // BQ, BQ)

    a = rms_norm(inputs, gain_one).astype(bf16)
    a_perm = dot_nn(a, shuffle).astype(bf16)
    send, query_raw, key_raw = project(a_perm, w_qkv, cos, sin, gain_query, gain_key)
    x = lax.all_to_all(send, CTX, 0, 0, tiled=True)
    o_send, o_nat, l_inv = attend(klo, x, lens)
    mixed = lax.all_to_all(o_send, CTX, 0, 0, tiled=True)

    output, grad_residual, do_send, features, resid_low, grads, gain_two_terms = middle(
        full, mixed, tokens[0], cotangent[0], gain_two.reshape(1, width), shuffle
    )
    do = lax.all_to_all(do_send, CTX, 0, 0, tiled=True)
    grads = grad_out(features, resid_low, cotangent[0], grads)
    do, grads = lax.optimization_barrier((do, grads))
    grads = lax.psum_scatter(grads, AXIS_YZ, scatter_dimension=0, tiled=True)[0]
    n_x = 4

    d_send = attend_back(klo, x, do, o_nat, l_inv, lens)
    d_recv = lax.all_to_all(d_send, CTX, 0, 0, tiled=True)
    grad_w_qkv, da_perm, gain_qk = project_back(
        d_recv, query_raw, key_raw, cos, sin, gain_query, gain_key, w_qkv, a_perm.T
    )
    grad_w_qkv, grads = lax.optimization_barrier((grad_w_qkv, grads))
    out_part = grads[:OUT_ROWS].reshape(n_x, OUT_ROWS // n_x, width)
    ffn_part = grads[OUT_ROWS:].reshape(2 * N_CHUNKS, n_x, owned, CHUNK)
    ffn_part = ffn_part.transpose(1, 0, 2, 3).reshape(n_x, 2 * N_CHUNKS * owned, CHUNK)
    grads = sum_over_x(jnp.concatenate([out_part, ffn_part], axis=1))
    owned_out = lax.ppermute(grads[: OUT_ROWS // n_x], EVERY, pairs)
    owned_ffn = grads[OUT_ROWS // n_x :].reshape(2 * N_CHUNKS, owned, CHUNK)
    owned_ffn = owned_ffn.transpose(1, 0, 2).reshape(owned, 2 * FF)
    grad_w_qkv = lax.psum_scatter(grad_w_qkv, AXIS_YZ, scatter_dimension=0, tiled=True)
    grad_a = dot_nt(da_perm.astype(bf16), shuffle)
    grad_in_part, gain_one_terms = rms_back(inputs, gain_one, grad_a)
    input_grad = grad_residual + grad_in_part
    grad_gains = jnp.concatenate(
        [jnp.sum(gain_one_terms, axis=0), gain_two_terms[0], gain_qk[0], gain_qk[1]]
    )
    owned_gain_grad = lax.psum_scatter(grad_gains, EVERY, scatter_dimension=0, tiled=True)
    grad_w_qkv, owned_gain_grad = lax.optimization_barrier((grad_w_qkv, owned_gain_grad))
    owned_qkv = sum_over_x(grad_w_qkv.reshape(n_x, owned, attn_cols)).reshape(owned, H_KV, 4 * HD)
    owned_in = jnp.concatenate(
        [
            owned_qkv[:, :, : 2 * HD].reshape(owned, q_width),
            owned_qkv[:, :, 2 * HD : 3 * HD].reshape(owned, kv_width),
            owned_qkv[:, :, 3 * HD :].reshape(owned, kv_width),
            owned_ffn,
        ],
        axis=1,
    )
    new_first_in, new_second_in, new_master_in = adam_step(
        w_in, first_in, second_in, owned_in, RATE_MATRIX
    )
    new_first_out, new_second_out, new_master_out = adam_step(
        w_out, first_out, second_out, owned_out, RATE_MATRIX
    )
    new_first_gains, new_second_gains, new_master_gains = adam_step(
        gains, first_gains, second_gains, owned_gain_grad, RATE_GAIN
    )
    return (
        output[None],
        input_grad[None],
        new_first_in,
        new_first_out,
        new_first_gains,
        new_second_in,
        new_second_out,
        new_second_gains,
        new_master_in,
        new_master_out,
        new_master_gains,
        new_master_in.astype(bf16),
        new_master_out.astype(bf16),
    )


def solution(mesh):
    cut = Mesh(mesh.devices.reshape(tuple(SIZES[name] for name in EVERY)), EVERY)
    weights = P(EVERY, None)
    vector = P(EVERY)
    acts = P(SHARD, CTX, None)
    in_specs = (
        acts,
        acts,
        P(SHARD, None),
        P(SHARD, CTX),
        P(SHARD, None),
    ) + (weights, weights, vector) * 3
    out_specs = (acts, acts) + (weights, weights, vector) * 3 + (weights, weights)
    return jax.shard_map(body, mesh=cut, in_specs=in_specs, out_specs=out_specs, check_vma=False)
```

time: 3060 us -> 538 us (0.18); the launches traced: 3020 us -> 535 us
  waiting for transfers between devices: 1780 us -> 186 us
  local copies, waits for them, and re-layouts: 414 us -> 16.3 us
  matrix products: 376 us -> 3.75 us
  other arithmetic: 295 us -> 21.8 us
  Pallas kernels: 0 us -> 123 us
  starting transfers between devices: 0.95 us -> 31.9 us
    reduce_scatter x4 -> x2, waiting for transfers between devices: 1390 us -> 58.6 us  [the longest x1 52.1 us: body(): grads = lax.psum_scatter(grads, AXIS_YZ, scatter_dimension=0, tiled=True)[0]]
    dot_general x303 -> x2, matrix products: 376 us -> 3.75 us  [the longest x1 2.28 us: dot_nt(): lax.dot_general(a, b, (((1,), (1,)), ((), ())), preferred_element_type=f32)]
    all_gather x4 -> x2, waiting for transfers between devices: 397 us -> 37.1 us  [gathered(): return lax.all_gather(x, AXIS_YZ, axis=0, tiled=True)]
    dynamic_slice x284 -> x0, local copies, waits for them, and re-layouts: 299 us -> none  [the longest x95 116 us: block_scores(): lax.dynamic_slice_in_dim(keys_full, start_row, half_rows, 0)]
    pallas_call x0 -> x6, Pallas kernels: none -> 123 us  [the longest x1 32.1 us: middle(): pl.pallas_call(middle_kernel, grid=(2 * N_CHUNKS + 2,), in_specs=[pl.Bloc...]
    eq x124 -> x0, other arithmetic: 94.5 us -> none  [block_scores(): key_live[None, :] == 1]
    dynamic_update_slice x35 -> x0, other arithmetic: 80.2 us -> none  [add_rows(): return lax.dynamic_update_slice_in_dim(total, current + piece, start_row, 0)]
    unnamed x2 -> x1, blocking collectives: 130 us -> 64.1 us
  transfers between devices with their start and end apart: 8 -> 15, of which waited for: 7 -> 14; matrix products, arithmetic and copies ran while one was open for 16% -> 5% of each run, Pallas kernels for 0% -> 17%
where the time goes in v1:
time: 538 us; the launch traced here: 535 us
  waiting for transfers between devices  186 us (35%)
  blocking collectives  138 us (26%)
  Pallas kernels  123 us (23%)
  starting transfers between devices  31.9 us (6%)
  other arithmetic  21.8 us (4%)
  local copies, waits for them, and re-layouts  16.3 us (3%)
  between operations  14.4 us (3%)
    unnamed x1, blocking collectives  64.1 us
    reduce_scatter x1, waiting for transfers between devices, body(): grads = lax.psum_scatter(grads, AXIS_YZ, scatter_dimension=0, tiled=True)[0]  52.1 us
    all_to_all x1, blocking collectives, body(): d_recv = lax.all_to_all(d_send, CTX, 0, 0, tiled=True)  48.1 us
    all_to_all x1, waiting for transfers between devices, body(): x = lax.all_to_all(send, CTX, 0, 0, tiled=True)  38.1 us
    all_gather x2, waiting for transfers between devices, gathered(): return lax.all_gather(x, AXIS_YZ, axis=0, tiled=True)  37.1 us
    pallas_call x1, Pallas kernels, middle(): pl.pallas_call(middle_kernel, grid=(2 * N_CHUNKS + 2,), in_specs=[pl.Bloc...  32.1 us
    pallas_call x1, Pallas kernels, attend_back(): pl.pallas_call(attend_back_kernel, in_specs=[pl.BlockSpec(memory_space=pl...  31.2 us
    pallas_call x1, Pallas kernels, attend(): pl.pallas_call(attend_kernel, in_specs=[pl.BlockSpec(memory_space=pltpu.S...  23.9 us
  transfers between devices with their start and end apart: 15, of which 14 were waited for; matrix products, arithmetic and copies ran while one was open for 5% of the time, Pallas kernels for 17%

profile of v1, /device:TPU:96, one launch (start us, length us, event | category | flops | bytes accessed | tf_op | source)
XLA Modules:
  0.0 534.9 jit_solution(10464223356672217303)
XLA Ops:
  7.2 1.0 convert_element_type.126
  9.0 13.6 %all_gather.13 = bf16[32,10368]{1,0:T(8,128)(2,1)S(1)} all-gather(bf16[8,10368]{1,0:T(8,128)(2,1)S(1)} %fusion.36), channel_id=1, replica_groups=mesh['xh'=2,'y'=4,'core'=2,'xl'=2,'z'=4] {'xh','xl'}, dimensions={0}, use_global_device_ids=true | all-gather | bytes 829440 | tf_op jit(solution)/shard_map/all_gather | solution.py:647
  24.3 3.7 collective-permute-start
  28.7 4.8 collective-permute-done
  33.5 12.4 %all_gather.12 = bf16[160,1024]{1,0:T(8,128)(2,1)S(1)} all-gather(bf16[40,1024]{1,0:T(8,128)(2,1)S(1)} %collective-permute-done), channel_id=1, replica_groups=mesh['xh'=2,'y'=4,'core'=2,'xl'=2,'z'=4] {'xh','xl'}, dimensions={0}, use_global_device_ids=true | all-gather | bytes 409600 | tf_op jit(solution)/shard_map/all_gather | solution.py:651
  47.8 30.3 %all-gather.4.cloned.1.call-done.w_ref = bf16[1024,4224]{1,0:T(8,128)(2,1)} async-done(((bf16[32,4224]{1,0:T(8,128)(2,1)}), bf16[1024,4224]{1,0:T(8,128)(2,1)}) %all-gather.4.cloned.1.call-update) | async-done | bytes 8650768 | tf_op jit(solution)/shard_map/all_gather | solution.py:573
  79.4 1.5 fusion.9
  81.1 9.7 %project.1 = (bf16[16,3,256,128]{3,2,1,0:T(8,128)(2,1)}, f32[16,256,128]{2,1,0:T(8,128)S(1)}, f32[8,256,128]{2,1,0:T(8,128)S(1)}) custom-call(bf16[256,1024]{1,0:T(8,128)(2,1)S(1)} %copy.61.a_ref, bf16[1024,4224]{1,0:T(8,128)(2,1)} %all-gather.4.cloned.1.call-done.w_ref, f32[256,128]{1,0:T(8,128)S(1)} %get-tuple-element.119.cos_ref, ...), custom_call_target="tpu_custom_call" | custom-call | tf_op jit(solution)/shard_map/project/pallas_call | solution.py:92
  90.8 1.3 copy-done.3
  93.1 5.2 all-to-all-start
  99.4 8.6 %subtract_reduce_fusion = (s32[32]{0:T(128)S(1)}, s32[32,128]{1,0:T(8,128)S(1)}, pred[32,128]{1,0:T(8,128)(4,1)S(1)}) fusion(s32[32]{0:T(128)S(1)} %reshape.272, s32[]{:T(128)} %get-tuple-element.103, s32[]{:T(128)} %get-tuple-element.99, s32[]{:T(128)} %get-tuple-element.71, s32[]{:T(128)} %get-tuple-element.69, s32[]{:T(128)} %get-tuple-element.101, ...), kind=kLoop, calls=%fused_computation.84 | loop fusion | flops 139232 | bytes 53556 | tf_op jit(solution)/shard_map/reduce_min | solution.py:687
  108.4 38.1 %all-to-all-done.x_ref = bf16[16,3,256,128]{3,2,1,0:T(8,128)(2,1)} async-done(((bf16[16,3,256,128]{3,2,1,0:T(8,128)(2,1)}), bf16[16,3,256,128]{3,2,1,0:T(8,128)(2,1)}, u32[]{:S(2)}, u32[]{:S(2)}) %all-to-all-start) | async-done | bytes 3145760 | tf_op jit(solution)/shard_map/all_to_all | solution.py:693
  146.5 23.9 %attend.1 = (bf16[16,256,128]{2,1,0:T(8,128)(2,1)S(1)}, f32[4096,128]{1,0:T(8,128)S(1)}, f32[16,256]{1,0:T(8,128)S(1)}) custom-call(s32[16]{0:T(128)S(1)} %and_select_fusion.klo_ref, bf16[16,3,256,128]{3,2,1,0:T(8,128)(2,1)} %all-to-all-done.x_ref, s32[16,256]{1,0:T(8,128)S(1)} %fusion.42.len_ref), custom_call_target="tpu_custom_call" | custom-call | tf_op jit(solution)/shard_map/attend/pallas_call | solution.py:256
  170.4 1.3 copy-done.5
  171.7 1.0 copy-done.10
  172.7 5.6 %all-to-all-start.1 = ((bf16[16,256,128]{2,1,0:T(8,128)(2,1)}), bf16[16,256,128]{2,1,0:T(8,128)(2,1)S(1)}, u32[]{:S(2)}, u32[]{:S(2)}) async-start(bf16[16,256,128]{2,1,0:T(8,128)(2,1)} %copy-done.10), calls=%async_computation.1 | async-start | bytes 2097152 | tf_op jit(solution)/shard_map/all_to_all | solution.py:695
  178.3 1.7 fusion.1.shuffle_ref
  180.0 18.7 %all-to-all-done.1.mixed_ref = bf16[16,256,128]{2,1,0:T(8,128)(2,1)S(1)} async-done(((bf16[16,256,128]{2,1,0:T(8,128)(2,1)}), bf16[16,256,128]{2,1,0:T(8,128)(2,1)S(1)}, u32[]{:S(2)}, u32[]{:S(2)}) %all-to-all-start.1) | async-done | bytes 1048608 | tf_op jit(solution)/shard_map/all_to_all | solution.py:695
  198.7 6.8 %all-gather.6.cloned.1.call-done = bf16[11264,1024]{1,0:T(8,128)(2,1)} async-done(((bf16[352,1024]{1,0:T(8,128)(2,1)}), bf16[11264,1024]{1,0:T(8,128)(2,1)}) %all-gather.6.cloned.1.call-update) | async-done | bytes 23068688 | tf_op jit(solution)/shard_map/all_gather | solution.py:573
  205.5 32.1 %middle.1 = (f32[256,1024]{1,0:T(8,128)}, f32[256,1024]{1,0:T(8,128)S(1)}, bf16[16,256,128]{2,1,0:T(8,128)(2,1)S(1)}, bf16[256,5120]{1,0:T(8,128)(2,1)}, bf16[25...) custom-call(bf16[32,352,1024]{2,1,0:T(8,128)(2,1)} %bitcast.109, ...), custom_call_target="tpu_custom_call" | custom-call | tf_op jit(solution)/shard_map/middle/pallas_call | solution.py:469
  237.7 1.0 copy-done.9
  238.6 1.0 copy-done.11
  239.6 5.0 all-to-all-start.2
  244.7 1.7 copy-done.1
  246.4 7.3 %grad_out.1 = bf16[32,352,1024]{2,1,0:T(8,128)(2,1)} custom-call(bf16[256,5120]{1,0:T(8,128)(2,1)S(1)} %copy-done.1, bf16[256,1024]{1,0:T(8,128)(2,1)S(1)} %get-tuple-element.41.drb_ref, bf16[256,1024]{1,0:T(8,128)(2,1)S(1)} %bitcast.105, bf16[32,352,1024]{2,1,0:T(8,128)(2,1)} %get-tuple-element.42.grads_ref), custom_call_target="tpu_custom_call", output_to_operand_aliasing={{}: (3, {})} | custom-call | tf_op jit(solution)/shard_map/grad_out/pallas_call | solution.py:544
  253.7 8.9 %all-to-all-done.2.do_ref = bf16[16,256,128]{2,1,0:T(8,128)(2,1)S(1)} async-done(((bf16[16,256,128]{2,1,0:T(8,128)(2,1)}), bf16[16,256,128]{2,1,0:T(8,128)(2,1)S(1)}, u32[]{:S(2)}, u32[]{:S(2)}) %all-to-all-start.2) | async-done | bytes 1048608 | tf_op jit(solution)/shard_map/all_to_all | solution.py:700
  262.9 1.6 copy-done.6
  264.5 31.2 %attend_back.1 = bf16[16,3,256,128]{3,2,1,0:T(8,128)(2,1)} custom-call(s32[16]{0:T(128)S(1)} %and_select_fusion.klo_ref, bf16[16,3,256,128]{3,2,1,0:T(8,128)(2,1)} %all-to-all-done.x_ref, bf16[16,256,128]{2,1,0:T(8,128)(2,1)S(1)} %all-to-all-done.2.do_ref, f32[4096,128]{1,0:T(8,128)S(1)} %copy-done.6, f32[16,256]{1,0:T(8,128)S(1)} %get-tuple-element.45.linv_ref, ...), custom_call_target="tpu_custom_call" | custom-call | tf_op jit(solution)/shard_map/attend_back/pallas_call | solution.py:333
  295.7 48.1 %all_to_all.20.recv_ref = bf16[16,3,256,128]{3,2,1,0:T(8,128)(2,1)} all-to-all(bf16[16,3,256,128]{3,2,1,0:T(8,128)(2,1)} %attend_back.1), channel_id=1, replica_groups=mesh['xh'=2,'y'=4,'core'=2,'xl'=2,'z'=4] {'xh','y','core'}, dimensions={0} | all-to-all | bytes 6291456 | tf_op jit(solution)/shard_map/all_to_all | solution.py:707
  343.8 18.6 %project_back.1 = (bf16[1024,4096]{1,0:T(8,128)(2,1)}, f32[256,1024]{1,0:T(8,128)S(1)}, f32[8,128]{1,0:T(8,128)S(1)}) custom-call(bf16[16,3,256,128]{3,2,1,0:T(8,128)(2,1)} %all_to_all.20.recv_ref, f32[16,256,128]{2,1,0:T(8,128)S(1)} %copy-done.4, f32[8,256,128]{2,1,0:T(8,128)S(1)} %copy-done.8, f32[256,128]{1,0:T(8,128)S(1)} %get-tuple-element.119.cos_ref, ...), custom_call_target="tpu_custom_call" | custom-call | tf_op jit(solution)/shard_map/project_back/pallas_call | solution.py:159
  362.5 52.1 %reduce-scatter.3.cloned.1.call-done = bf16[1,352,1024]{2,1,0:T(8,128)(2,1)} async-done(((bf16[32,352,1024]{2,1,0:T(8,128)(2,1)}), bf16[1,352,1024]{2,1,0:T(8,128)(2,1)}) %reduce-scatter.3.cloned.1.call-update) | async-done | bytes 720912 | tf_op jit(solution)/shard_map/reduce_scatter | solution.py:703
  414.6 2.3 fusion.16
  416.9 64.1 %all-reduce.1 = f32[2304]{0:T(1024)S(1)} all-reduce(f32[2304]{0:T(1024)S(1)} %pad_maximum_fusion.5), channel_id=5, replica_groups=mesh['xh'=2,'y'=4,'core'=2,'xl'=2,'z'=4] {'xh','y','core','xl','z'}, use_global_device_ids=true, to_apply=%region_20.21.clone | all-reduce | flops 2304 | bytes 18432
  481.1 1.0 slice.97
  482.1 1.0 slice.96
  483.3 1.0 collective-permute-start.4
  484.3 2.6 collective-permute-start.5
  487.4 4.5 collective-permute-done.4
  491.9 2.9 collective-permute-done.5
  495.3 1.9 collective-permute-start.7
  497.2 1.3 fusion.15
  498.5 9.1 %collective-permute-done.7 = f32[40,1024]{1,0:T(8,128)S(1)} collective-permute-done((f32[40,1024]{1,0:T(8,128)S(1)}, f32[40,1024]{1,0:T(8,128)S(1)}, u32[]{:S(2)}, u32[]{:S(2)}) %collective-permute-start.7) | collective-permute-done | bytes 163872 | tf_op jit(solution)/shard_map/ppermute | solution.py:716
  508.5 6.5 %reduce-scatter.5.cloned.1.call-done = bf16[32,4096]{1,0:T(8,128)(2,1)} async-done(((bf16[1024,4096]{1,0:T(8,128)(2,1)}), bf16[32,4096]{1,0:T(8,128)(2,1)}) %reduce-scatter.5.cloned.1.call-update) | async-done | bytes 262160 | tf_op jit(solution)/shard_map/reduce_scatter | solution.py:719
  516.0 1.7 collective-permute-start.1
  517.7 3.3 collective-permute-start.2
  522.5 1.4 collective-permute-done.2
  523.9 1.3 collective-permute-done.3
  526.2 2.2 fusion.47
  (112 shorter events, 14.6 us)
Async XLA Ops:
  7.2 39.7 %copy-start.20 = (s32[1,256]{1,0:T(1,128)S(1)}, s32[1,256]{1,0:T(1,128)}, u32[]{:S(2)}) copy-start(s32[1,256]{1,0:T(1,128)} %param.17) | copy-start | bytes 3076
  7.2 71.0 %all-gather.4.cloned.1.call-start = ((), (), s32[]{:S(2)}) async-start(), calls=%async_computation.6 | async-start | bytes 8921088 | tf_op jit(solution)/shard_map/all_gather | solution.py:573
  9.0 38.7 %copy-start = (bf16[1,256,1024]{2,1,0:T(8,128)(2,1)S(1)}, bf16[1,256,1024]{2,1,0:T(8,128)(2,1)}, u32[]{:S(2)}) copy-start(bf16[1,256,1024]{2,1,0:T(8,128)(2,1)} %param.14) | copy-start | bytes 1572868
  23.3 182.2 %all-gather.6.cloned.1.call-start = ((), (), s32[]{:S(2)}) async-start(), calls=%async_computation.9 | async-start | bytes 23789568 | tf_op jit(solution)/shard_map/all_gather | solution.py:573
  24.3 9.2 %collective-permute-start = (bf16[40,1024]{1,0:T(8,128)(2,1)S(1)}, bf16[40,1024]{1,0:T(8,128)(2,1)S(1)}, u32[]{:S(2)}, u32[]{:S(2)}) collective-permute-start(bf16[40,1024]{1,0:T(8,128)(2,1)S(1)} %convert_element_type.125), channel_id=1, source_target_pairs={{0,0},{8,1},{16,2},{24,3},{1,4},{9,5},{17,6},{25,7},{4,8},{12,9},{... | collective-permute-start | bytes 245768 | tf_op jit(solution)/shard_map/ppermute | solution.py:650
  90.8 1.3 copy-start.3
  92.1 1.0 copy-start.7
  92.1 6.2 %copy-start.18 = (s32[1,4096]{1,0:T(1,128)S(1)}, s32[1,4096]{1,0:T(1,128)}, u32[]{:S(2)}) copy-start(s32[1,4096]{1,0:T(1,128)} %param.16) | copy-start | bytes 49156
  92.1 6.3 %copy-start.19 = (s32[1,4096]{1,0:T(1,128)S(1)}, s32[1,4096]{1,0:T(1,128)}, u32[]{:S(2)}) copy-start(s32[1,4096]{1,0:T(1,128)} %param.18) | copy-start | bytes 49156
  93.1 53.4 %all-to-all-start = ((bf16[16,3,256,128]{3,2,1,0:T(8,128)(2,1)}), bf16[16,3,256,128]{3,2,1,0:T(8,128)(2,1)}, u32[]{:S(2)}, u32[]{:S(2)}) async-start(bf16[16,3,256,128]{3,2,1,0:T(8,128)(2,1)} %get-tuple-element.35), calls=%async_computation | async-start | bytes 6291456 | tf_op jit(solution)/shard_map/all_to_all | solution.py:693
  98.3 107.2 %copy-start.2 = (bf16[1,256,1024]{2,1,0:T(8,128)(2,1)S(1)}, bf16[1,256,1024]{2,1,0:T(8,128)(2,1)}, u32[]{:S(2)}) copy-start(bf16[1,256,1024]{2,1,0:T(8,128)(2,1)} %param.15) | copy-start | bytes 1572868
  170.4 1.3 copy-start.5
  171.7 1.0 copy-start.10
  172.7 26.0 %all-to-all-start.1 = ((bf16[16,256,128]{2,1,0:T(8,128)(2,1)}), bf16[16,256,128]{2,1,0:T(8,128)(2,1)S(1)}, u32[]{:S(2)}, u32[]{:S(2)}) async-start(bf16[16,256,128]{2,1,0:T(8,128)(2,1)} %copy-done.10), calls=%async_computation.1 | async-start | bytes 2097152 | tf_op jit(solution)/shard_map/all_to_all | solution.py:695
  237.7 1.0 copy-start.9
  238.6 1.0 copy-start.11
  239.6 23.0 %all-to-all-start.2 = ((bf16[16,256,128]{2,1,0:T(8,128)(2,1)}), bf16[16,256,128]{2,1,0:T(8,128)(2,1)S(1)}, u32[]{:S(2)}, u32[]{:S(2)}) async-start(bf16[16,256,128]{2,1,0:T(8,128)(2,1)} %copy-done.9), calls=%async_computation.2 | async-start | bytes 2097152 | tf_op jit(solution)/shard_map/all_to_all | solution.py:700
  244.6 169.9 %reduce-scatter.3.cloned.1.call-start = ((), (), s32[]{:S(2)}) async-start(), calls=%async_computation.7 | async-start | bytes 23789568 | tf_op jit(solution)/shard_map/reduce_scatter | solution.py:703
  244.7 1.7 copy-start.1
  262.7 252.4 %reduce-scatter.5.cloned.1.call-start = ((), (), s32[]{:S(2)}) async-start(), calls=%async_computation.8 | async-start | bytes 8650752 | tf_op jit(solution)/shard_map/reduce_scatter | solution.py:719
  262.9 1.6 copy-start.6
  295.7 48.1 %copy-start.4 = (f32[16,256,128]{2,1,0:T(8,128)S(1)}, f32[16,256,128]{2,1,0:T(8,128)}, u32[]{:S(2)}) copy-start(f32[16,256,128]{2,1,0:T(8,128)} %copy-done.3) | copy-start | bytes 6291460
  295.7 48.1 %copy-start.8 = (f32[8,256,128]{2,1,0:T(8,128)S(1)}, f32[8,256,128]{2,1,0:T(8,128)}, u32[]{:S(2)}) copy-start(f32[8,256,128]{2,1,0:T(8,128)} %copy-done.7) | copy-start | bytes 3145732
  414.6 82.6 %copy-start.12 = (f32[256,1024]{1,0:T(8,128)S(1)}, f32[256,1024]{1,0:T(8,128)}, u32[]{:S(2)}) copy-start(f32[256,1024]{1,0:T(8,128)} %copy-done.11) | copy-start | bytes 3145732
  416.9 80.3 %copy-start.14 = (f32[256,1024]{1,0:T(8,128)S(1)}, f32[256,1024]{1,0:T(8,128)}, u32[]{:S(2)}) copy-start(f32[256,1024]{1,0:T(8,128)} %get-tuple-element.118) | copy-start | bytes 3145732
  483.1 24.5 %copy-start.15 = (f32[40,1024]{1,0:T(8,128)S(1)}, f32[40,1024]{1,0:T(8,128)}, u32[]{:S(2)}) copy-start(f32[40,1024]{1,0:T(8,128)} %param.20) | copy-start | bytes 491524
  483.1 24.5 %copy-start.16 = (f32[40,1024]{1,0:T(8,128)S(1)}, f32[40,1024]{1,0:T(8,128)}, u32[]{:S(2)}) copy-start(f32[40,1024]{1,0:T(8,128)} %param.26) | copy-start | bytes 491524
  483.2 24.5 %copy-start.17 = (f32[40,1024]{1,0:T(8,128)S(1)}, f32[40,1024]{1,0:T(8,128)}, u32[]{:S(2)}) copy-start(f32[40,1024]{1,0:T(8,128)} %param.23) | copy-start | bytes 491524
  483.2 38.7 %copy-start.21 = (f32[18]{0:T(128)S(1)}, f32[18]{0:T(128)}, u32[]{:S(2)}) copy-start(f32[18]{0:T(128)} %param.21) | copy-start | bytes 220
  483.2 38.7 %copy-start.22 = (f32[18]{0:T(128)S(1)}, f32[18]{0:T(128)}, u32[]{:S(2)}) copy-start(f32[18]{0:T(128)} %param.27) | copy-start | bytes 220
  483.2 38.7 %copy-start.23 = (f32[18]{0:T(128)S(1)}, f32[18]{0:T(128)}, u32[]{:S(2)}) copy-start(f32[18]{0:T(128)} %param.24) | copy-start | bytes 220
  483.3 42.9 %copy-start.13 = (f32[8,10240]{1,0:T(8,128)S(1)}, f32[8,10240]{1,0:T(8,128)}, u32[]{:S(2)}) copy-start(f32[8,10240]{1,0:T(8,128)} %param.19) | copy-start | bytes 983044
  483.3 8.6 %collective-permute-start.4 = (bf16[88,1024]{1,0:T(8,128)(2,1)S(1)}, bf16[88,1024]{1,0:T(8,128)(2,1)S(1)}, u32[]{:S(2)}, u32[]{:S(2)}) collective-permute-start(bf16[88,1024]{1,0:T(8,128)(2,1)S(1)} %get-tuple-element.86), channel_id=1, source_target_pairs={{0,4},{4,64},{64,68},{68,0},{1,5},{5,65},{65,69},{69,1},{2,6},{6,6... | collective-permute-start | bytes 540680 | tf_op jit(solution)/shard_map/ppermute | solution.py:586
  484.3 10.5 %collective-permute-start.5 = (bf16[88,1024]{1,0:T(8,128)(2,1)S(1)}, bf16[88,1024]{1,0:T(8,128)(2,1)S(1)}, u32[]{:S(2)}, u32[]{:S(2)}) collective-permute-start(bf16[88,1024]{1,0:T(8,128)(2,1)S(1)} %get-tuple-element.87), channel_id=1, source_target_pairs={{0,64},{4,68},{64,0},{68,4},{1,65},{5,69},{65,1},{69,5},{2,66},{6,... | collective-permute-start | bytes 540680 | tf_op jit(solution)/shard_map/ppermute | solution.py:586
  486.9 8.2 %collective-permute-start.6 = (bf16[88,1024]{1,0:T(8,128)(2,1)S(1)}, bf16[88,1024]{1,0:T(8,128)(2,1)S(1)}, u32[]{:S(2)}, u32[]{:S(2)}) collective-permute-start(bf16[88,1024]{1,0:T(8,128)(2,1)S(1)} %get-tuple-element.88), channel_id=1, source_target_pairs={{0,68},{4,0},{64,4},{68,64},{1,69},{5,1},{65,5},{69,65},{2,70},{6,... | collective-permute-start | bytes 540680 | tf_op jit(solution)/shard_map/ppermute | solution.py:586
  495.3 12.3 %collective-permute-start.7 = (f32[40,1024]{1,0:T(8,128)S(1)}, f32[40,1024]{1,0:T(8,128)S(1)}, u32[]{:S(2)}, u32[]{:S(2)}) collective-permute-start(f32[40,1024]{1,0:T(8,128)S(1)} %slice.120), channel_id=1, source_target_pairs={{0,0},{1,8},{2,16},{3,24},{4,1},{5,9},{6,17},{7,25},{8,4},{9,12},{... | collective-permute-start | bytes 491528 | tf_op jit(solution)/shard_map/ppermute | solution.py:716
  516.0 6.5 %collective-permute-start.1 = (bf16[8,4096]{1,0:T(8,128)(2,1)S(1)}, bf16[8,4096]{1,0:T(8,128)(2,1)S(1)}, u32[]{:S(2)}, u32[]{:S(2)}) collective-permute-start(bf16[8,4096]{1,0:T(8,128)(2,1)S(1)} %get-tuple-element.89), channel_id=1, source_target_pairs={{0,4},{4,64},{64,68},{68,0},{1,5},{5,65},{65,69},{69,1},{2,6},{6,6... | collective-permute-start | bytes 196616 | tf_op jit(solution)/shard_map/ppermute | solution.py:586
  517.7 6.2 %collective-permute-start.2 = (bf16[8,4096]{1,0:T(8,128)(2,1)S(1)}, bf16[8,4096]{1,0:T(8,128)(2,1)S(1)}, u32[]{:S(2)}, u32[]{:S(2)}) collective-permute-start(bf16[8,4096]{1,0:T(8,128)(2,1)S(1)} %get-tuple-element.91), channel_id=1, source_target_pairs={{0,64},{4,68},{64,0},{68,4},{1,65},{5,69},{65,1},{69,5},{2,66},{6,... | collective-permute-start | bytes 196616 | tf_op jit(solution)/shard_map/ppermute | solution.py:586
  521.0 4.3 collective-permute-start.3
Sparse Core Ops, SparseCore 0:
  23.4 54.7 all-gather.3
  81.0 124.4 all-gather.5
  262.8 151.7 reduce-scatter.2
  418.6 96.4 reduce-scatter.4

commit v2 on v1

--- a/solution.py
+++ b/solution.py
@@ -36,6 +36,7 @@
 BQ = 256
 BK = 512
 VMEM_BYTES = 48 * 1024 * 1024
+BIG_VMEM_BYTES = 60 * 1024 * 1024
 
 bf16 = jnp.bfloat16
 f32 = jnp.float32
@@ -65,124 +66,169 @@
     return lax.dot_general(a, b, (((1,), (0,)), ((), ())), preferred_element_type=f32)
 
 
-def project_kernel(a_ref, w_ref, cos_ref, sin_ref, gq_ref, gk_ref, send_ref, qraw_ref, kraw_ref):
-    prod = dot_nn(a_ref[...], w_ref[...])
-    cos = cos_ref[...]
-    sin = sin_ref[...]
-
-    def roped(raw, gain):
-        normed = rms_norm(raw, gain)
-        return normed * cos + pltpu.roll(normed, HD // 2, 1) * sin
-
-    key_raw = prod[:, 2 * HD : 3 * HD]
-    key = roped(key_raw, gk_ref[...]).astype(bf16)
-    value = prod[:, 3 * HD :].astype(bf16)
-    kraw_ref[0] = key_raw
-    for r in range(2):
-        raw = prod[:, r * HD : (r + 1) * HD]
-        qraw_ref[r] = raw
-        send_ref[r, 0] = (roped(raw, gq_ref[...]) * (SCORE_SCALE * LOG2_E)).astype(bf16)
-        send_ref[r, 1] = key
-        send_ref[r, 2] = value
-
-
-def project(a, w, cos, sin, gq, gk):
-    rows, width = a.shape
-    whole = lambda j: (0, 0)
+N_GROUPS = 4
+GROUP = 8
+HALF = 128
+STEP_BLOCKS = 4
+STEPS = GROUP // STEP_BLOCKS
+HEAD_COLS = 3 * HD
+PAD_COLS = 4 * HD
+
+
+def block_spec(width, first, count):
+    return pl.BlockSpec(
+        (STEP_BLOCKS, HALF, width), lambda i, place: (jnp.clip(i - first, 0, count - 1), 0, 0)
+    )
+
+
+def group_specs(width):
+    return [block_spec(width, k * STEPS, STEPS) for k in range(N_GROUPS)]
+
+
+def fixed(shape):
+    return pl.BlockSpec(shape, lambda i, place: (0,) * len(shape))
+
+
+def rows_of(place_ref, step, i):
+    return pl.ds(pl.multiple_of(place_ref[step * STEP_BLOCKS + i] * HALF, HALF), HALF)
+
+
+def project_kernel(
+    place_ref, x0, x1, x2, x3, w_ref, cos_ref, sin_ref, gq_ref, gk_ref,
+    q_ref, k_ref, v_ref, qraw_ref, kraw_ref, inv_ref,
+):
+    step = pl.program_id(0)
+
+    def run(x):
+        wide = x.astype(f32)
+        inverse = lax.rsqrt(jnp.mean(wide * wide, axis=-1, keepdims=True) + NORM_EPS)
+        prod = dot_nn(x, w_ref[...]) * inverse
+        for i in range(STEP_BLOCKS):
+            at = rows_of(place_ref, step, i)
+            part = slice(i * HALF, (i + 1) * HALF)
+            cos = cos_ref[at, :]
+            sin = sin_ref[at, :]
+
+            def roped(raw, gain, cos=cos, sin=sin):
+                normed = rms_norm(raw, gain)
+                return normed * cos + pltpu.roll(normed, HD // 2, 1) * sin
+
+            query = prod[part, :HD]
+            key = prod[part, HD : 2 * HD]
+            inv_ref[at, :] = jnp.broadcast_to(inverse[part], (HALF, HD))
+            qraw_ref[at, :] = query
+            kraw_ref[at, :] = key
+            q_ref[at, :] = (roped(query, gq_ref[...]) * (SCORE_SCALE * LOG2_E)).astype(bf16)
+            k_ref[at, :] = roped(key, gk_ref[...]).astype(bf16)
+            v_ref[at, :] = prod[part, 2 * HD :].astype(bf16)
+
+    for k, x_ref in enumerate((x0, x1, x2, x3)):
+
+        @pl.when(step // STEPS == k)
+        def _(x_ref=x_ref):
+            run(x_ref[...].reshape(STEP_BLOCKS * HALF, x_ref.shape[2]))
+
+
+def project(place, groups, w, cos, sin, gq, gk):
+    width = w.shape[0]
+    span = cos.shape[0]
+    low = jax.ShapeDtypeStruct((span, HD), bf16)
+    wide = jax.ShapeDtypeStruct((span, HD), f32)
+    whole = fixed((span, HD))
     return pl.pallas_call(
         project_kernel,
-        grid=(H_KV,),
-        in_specs=[
-            pl.BlockSpec((rows, width), whole),
-            pl.BlockSpec((width, 4 * HD), lambda j: (0, j)),
-            pl.BlockSpec((rows, HD), whole),
-            pl.BlockSpec((rows, HD), whole),
-            pl.BlockSpec((1, HD), whole),
-            pl.BlockSpec((1, HD), whole),
-        ],
-        out_specs=[
-            pl.BlockSpec((2, 3, rows, HD), lambda j: (j, 0, 0, 0)),
-            pl.BlockSpec((2, rows, HD), lambda j: (j, 0, 0)),
-            pl.BlockSpec((1, rows, HD), lambda j: (j, 0, 0)),
-        ],
-        out_shape=[
-            jax.ShapeDtypeStruct((H_Q, 3, rows, HD), bf16),
-            jax.ShapeDtypeStruct((H_Q, rows, HD), f32),
-            jax.ShapeDtypeStruct((H_KV, rows, HD), f32),
-        ],
+        grid_spec=pltpu.PrefetchScalarGridSpec(
+            num_scalar_prefetch=1,
+            grid=(N_GROUPS * STEPS,),
+            in_specs=group_specs(width)
+            + [fixed((width, HEAD_COLS)), whole, whole, fixed((1, HD)), fixed((1, HD))],
+            out_specs=[whole] * 6,
+        ),
+        out_shape=[low, low, low, wide, wide, wide],
         compiler_params=pltpu.CompilerParams(vmem_limit_bytes=VMEM_BYTES),
         name="project",
-    )(a, w, cos, sin, gq, gk)
+    )(place, *groups, w, cos, sin, gq, gk)
 
 
 def project_back_kernel(
-    recv_ref, qraw_ref, kraw_ref, cos_ref, sin_ref, gq_ref, gk_ref, w_ref, at_ref, dw_ref, da_ref, dg_ref
+    place_ref, x0, x1, x2, x3, dq_ref, dk_ref, dv_ref, qraw_ref, kraw_ref, inv_ref, cos_ref, sin_ref,
+    gq_ref, gk_ref, w_ref, near_ref, far_ref, dw_ref, dg_ref, grads, scaled,
 ):
     step = pl.program_id(0)
-    cos = cos_ref[...]
-    sin = sin_ref[...]
-
-    def back(raw, gain, grad):
-        unrot = grad * cos + pltpu.roll(grad * sin, HD // 2, 1)
-        return rms_back(raw, gain, unrot)
-
-    pieces = []
-    gq_terms = jnp.zeros((1, HD), f32)
-    for r in range(2):
-        grad, terms = back(qraw_ref[r], gq_ref[...], recv_ref[r, 0].astype(f32))
-        pieces.append(grad.astype(bf16))
-        gq_terms = gq_terms + jnp.sum(terms, axis=0, keepdims=True)
-    grad_key = recv_ref[0, 1].astype(f32) + recv_ref[1, 1].astype(f32)
-    grad, terms = back(kraw_ref[0], gk_ref[...], grad_key)
-    gk_terms = jnp.sum(terms, axis=0, keepdims=True)
-    pieces.append(grad.astype(bf16))
-    pieces.append((recv_ref[0, 2].astype(f32) + recv_ref[1, 2].astype(f32)).astype(bf16))
-    dproj = jnp.concatenate(pieces, axis=1)
-    dw_ref[...] = dot_nn(at_ref[...], dproj).astype(bf16)
-    part = dot_nt(dproj, w_ref[...])
-    both = jnp.concatenate([gq_terms, gk_terms, jnp.zeros((6, HD), f32)], axis=0)
 
     @pl.when(step == 0)
     def _():
-        da_ref[...] = part
-        dg_ref[...] = both
-
-    @pl.when(step > 0)
-    def _():
-        da_ref[...] += part
-        dg_ref[...] += both
-
-
-def project_back(recv, qraw, kraw, cos, sin, gq, gk, w, at):
-    width, rows = at.shape
-    whole = lambda j: (0, 0)
+        dw_ref[...] = jnp.zeros_like(dw_ref)
+        dg_ref[...] = jnp.zeros_like(dg_ref)
+
+    def run(x, da_ref):
+        q_sum = jnp.zeros((1, HD), f32)
+        k_sum = jnp.zeros((1, HD), f32)
+        for i in range(STEP_BLOCKS):
+            at = rows_of(place_ref, step, i)
+            part = slice(i * HALF, (i + 1) * HALF)
+            cos = cos_ref[at, :]
+            sin = sin_ref[at, :]
+
+            def back(raw, gain, grad, cos=cos, sin=sin):
+                unrot = grad * cos + pltpu.roll(grad * sin, HD // 2, 1)
+                return rms_back(raw, gain, unrot)
+
+            grad_q, q_terms = back(qraw_ref[at, :], gq_ref[...], dq_ref[at, :])
+            grad_k, k_terms = back(kraw_ref[at, :], gk_ref[...], dk_ref[at, :])
+            inverse = inv_ref[at, :]
+            for c, grad in enumerate((grad_q, grad_k, dv_ref[at, :])):
+                grads[part, c * HD : (c + 1) * HD] = grad.astype(bf16)
+                scaled[part, c * HD : (c + 1) * HD] = (grad * inverse).astype(bf16)
+            q_sum = q_sum + jnp.sum(q_terms, axis=0, keepdims=True)
+            k_sum = k_sum + jnp.sum(k_terms, axis=0, keepdims=True)
+        da_ref[...] = dot_nt(grads[...], w_ref[...]).astype(bf16).reshape(da_ref.shape)
+        dw_ref[...] += dot_tn(x, scaled[...])
+        dg_ref[0:1, :] += q_sum
+        dg_ref[1:2, :] += k_sum
+
+    for k, x_ref in enumerate((x0, x1, x2, x3)):
+
+        @pl.when(step // STEPS == k)
+        def _(k=k, x_ref=x_ref):
+            da_ref = near_ref if k < N_GROUPS // 2 else far_ref
+            run(x_ref[...].reshape(STEP_BLOCKS * HALF, x_ref.shape[2]), da_ref)
+
+
+def project_back(place, groups, grads, raws, cos, sin, gq, gk, w):
+    width = w.shape[0]
+    span = cos.shape[0]
+    whole = fixed((span, HD))
+    n_half = N_GROUPS // 2
+    da = jax.ShapeDtypeStruct((n_half * GROUP, HALF, width), bf16)
     return pl.pallas_call(
         project_back_kernel,
-        grid=(H_KV,),
-        in_specs=[
-            pl.BlockSpec((2, 3, rows, HD), lambda j: (j, 0, 0, 0)),
-            pl.BlockSpec((2, rows, HD), lambda j: (j, 0, 0)),
-            pl.BlockSpec((1, rows, HD), lambda j: (j, 0, 0)),
-            pl.BlockSpec((rows, HD), whole),
-            pl.BlockSpec((rows, HD), whole),
-            pl.BlockSpec((1, HD), whole),
-            pl.BlockSpec((1, HD), whole),
-            pl.BlockSpec((width, 4 * HD), lambda j: (0, j)),
-            pl.BlockSpec((width, rows), whole),
-        ],
-        out_specs=[
-            pl.BlockSpec((width, 4 * HD), lambda j: (0, j)),
-            pl.BlockSpec((rows, width), whole),
-            pl.BlockSpec((8, HD), whole),
-        ],
+        grid_spec=pltpu.PrefetchScalarGridSpec(
+            num_scalar_prefetch=1,
+            grid=(N_GROUPS * STEPS,),
+            in_specs=group_specs(width)
+            + [whole] * 8
+            + [fixed((1, HD)), fixed((1, HD)), fixed((width, HEAD_COLS))],
+            out_specs=[
+                block_spec(width, 0, n_half * STEPS),
+                block_spec(width, n_half * STEPS, n_half * STEPS),
+                fixed((width, HEAD_COLS)),
+                fixed((8, HD)),
+            ],
+            scratch_shapes=[
+                pltpu.VMEM((STEP_BLOCKS * HALF, HEAD_COLS), bf16),
+                pltpu.VMEM((STEP_BLOCKS * HALF, HEAD_COLS), bf16),
+            ],
+        ),
         out_shape=[
-            jax.ShapeDtypeStruct((width, 4 * HD * H_KV), bf16),
-            jax.ShapeDtypeStruct((rows, width), f32),
+            da,
+            da,
+            jax.ShapeDtypeStruct((width, HEAD_COLS), f32),
             jax.ShapeDtypeStruct((8, HD), f32),
         ],
-        compiler_params=pltpu.CompilerParams(vmem_limit_bytes=VMEM_BYTES),
+        compiler_params=pltpu.CompilerParams(vmem_limit_bytes=BIG_VMEM_BYTES),
         name="project_back",
-    )(recv, qraw, kraw, cos, sin, gq, gk, w, at)
+    )(place, *groups, *grads, *raws, cos, sin, gq, gk, w)
 
 
 def dealt_slot(place, n_dev):
@@ -200,27 +246,23 @@
     return (ahead >= 0) & (ahead <= len_row)
 
 
-def attend_kernel(klo_ref, x_ref, len_ref, osend_ref, onat_ref, linv_ref, qn, kn, vt):
-    n_dev = x_ref.shape[0]
-    half = x_ref.shape[2] // 2
-    span = qn.shape[0]
-    for place in range(2 * n_dev):
-        dev, side = dealt_slot(place, n_dev)
-        rows = slice(side * half, (side + 1) * half)
-        to = slice(place * half, (place + 1) * half)
-        qn[to, :] = x_ref[dev, 0, rows, :]
-        kn[to, :] = x_ref[dev, 1, rows, :]
-        vt[:, to] = x_ref[dev, 2, rows, :].astype(f32).T.astype(bf16)
+def attend_kernel(klo_ref, q_ref, k_ref, v_ref, len_ref, osend_ref, onat_ref, linv_ref, vt):
+    n_dev, rows, _ = osend_ref.shape
+    half = rows // 2
+    span = q_ref.shape[0]
+    for c in range(span // BQ):
+        to = slice(c * BQ, (c + 1) * BQ)
+        vt[:, to] = v_ref[to, :].astype(f32).T.astype(bf16)
 
     def q_step(qb, _):
         q_at = pl.multiple_of(qb * BQ, BQ)
-        q_blk = qn[pl.ds(q_at, BQ), :]
+        q_blk = q_ref[pl.ds(q_at, BQ), :]
         len_row = len_ref[pl.ds(qb, 1), :]
 
         def k_step(kb, carry):
             acc, total = carry
             k_at = pl.multiple_of(kb * BK, BK)
-            s = dot_nt(kn[pl.ds(k_at, BK), :], q_blk)
+            s = dot_nt(k_ref[pl.ds(k_at, BK), :], q_blk)
             p = jnp.where(key_mask(len_row, q_at - k_at), jnp.exp2(s), 0.0)
             total = total + jnp.sum(p.reshape(BK // 8, 8, BQ), axis=0)
             acc = acc + dot_nn(vt[:, pl.ds(k_at, BK)], p.astype(bf16))
@@ -234,8 +276,7 @@
         )
         inverse = 1.0 / jnp.sum(total, axis=0, keepdims=True)
         linv_ref[pl.ds(qb, 1), :] = inverse
-        out = (acc * inverse).T
-        onat_ref[pl.ds(q_at, BQ), :] = out
+        onat_ref[pl.ds(q_at, BQ), :] = (acc * inverse).T
         return 0
 
     lax.fori_loop(0, span // BQ, q_step, 0)
@@ -250,50 +291,40 @@
     return pl.BlockSpec(memory_space=pltpu.VMEM)
 
 
-def attend(klo, x, lens):
-    n_dev, _, rows, _ = x.shape
-    span = n_dev * rows
+def attend(klo, q, k, v, lens, rows):
+    span = q.shape[0]
     return pl.pallas_call(
         attend_kernel,
-        in_specs=[pl.BlockSpec(memory_space=pltpu.SMEM), vmem(), vmem()],
+        in_specs=[pl.BlockSpec(memory_space=pltpu.SMEM)] + [vmem()] * 4,
         out_specs=[vmem(), vmem(), vmem()],
         out_shape=[
-            jax.ShapeDtypeStruct((n_dev, rows, HD), bf16),
+            jax.ShapeDtypeStruct((span // rows, rows, HD), bf16),
             jax.ShapeDtypeStruct((span, HD), f32),
             jax.ShapeDtypeStruct((span // BQ, BQ), f32),
         ],
-        scratch_shapes=[
-            pltpu.VMEM((span, HD), bf16),
-            pltpu.VMEM((span, HD), bf16),
-            pltpu.VMEM((HD, span), bf16),
-        ],
+        scratch_shapes=[pltpu.VMEM((HD, span), bf16)],
         compiler_params=pltpu.CompilerParams(vmem_limit_bytes=VMEM_BYTES),
         name="attend",
-    )(klo, x, lens)
+    )(klo, q, k, v, lens)
 
 
 def attend_back_kernel(
-    klo_ref, x_ref, do_ref, onat_ref, linv_ref, len_ref, send_ref, qn, kn, vn, kt, don, dq, dk, dv
+    klo_ref, q_ref, k_ref, v_ref, do_ref, onat_ref, linv_ref, len_ref, dq, dk, dv, kt, don
 ):
-    n_dev = x_ref.shape[0]
-    half = x_ref.shape[2] // 2
-    span = qn.shape[0]
+    n_dev, rows, _ = do_ref.shape
+    half = rows // 2
+    span = q_ref.shape[0]
     for place in range(2 * n_dev):
         dev, side = dealt_slot(place, n_dev)
-        rows = slice(side * half, (side + 1) * half)
         to = slice(place * half, (place + 1) * half)
-        qn[to, :] = x_ref[dev, 0, rows, :]
-        key = x_ref[dev, 1, rows, :]
-        kn[to, :] = key
-        kt[:, to] = key.astype(f32).T.astype(bf16)
-        vn[to, :] = x_ref[dev, 2, rows, :]
-        don[to, :] = do_ref[dev, rows, :]
+        don[to, :] = do_ref[dev, side * half : (side + 1) * half, :]
+        kt[:, to] = k_ref[to, :].astype(f32).T.astype(bf16)
     dk[...] = jnp.zeros_like(dk)
     dv[...] = jnp.zeros_like(dv)
 
     def q_step(qb, _):
         q_at = pl.multiple_of(qb * BQ, BQ)
-        q_blk = qn[pl.ds(q_at, BQ), :]
+        q_blk = q_ref[pl.ds(q_at, BQ), :]
         do_blk = don[pl.ds(q_at, BQ), :]
         len_row = len_ref[pl.ds(qb, 1), :]
         inverse = linv_ref[pl.ds(qb, 1), :]
@@ -303,9 +334,9 @@
         def k_step(kb, acc):
             k_at = pl.multiple_of(kb * BK, BK)
             here = pl.ds(k_at, BK)
-            s = dot_nt(kn[here, :], q_blk)
+            s = dot_nt(k_ref[here, :], q_blk)
             p = jnp.where(key_mask(len_row, q_at - k_at), jnp.exp2(s) * inverse, 0.0)
-            dp = dot_nt(vn[here, :], do_blk)
+            dp = dot_nt(v_ref[here, :], do_blk)
             ds = (p * (dp - delta)).astype(bf16)
             dv[here, :] += dot_nn(p.astype(bf16), do_blk)
             dk[here, :] += dot_nn(ds, q_blk)
@@ -318,36 +349,20 @@
         return 0
 
     lax.fori_loop(0, span // BQ, q_step, 0)
-    for place in range(2 * n_dev):
-        dev, side = dealt_slot(place, n_dev)
-        rows = slice(side * half, (side + 1) * half)
-        at = slice(place * half, (place + 1) * half)
-        send_ref[dev, 0, rows, :] = dq[at, :].astype(bf16)
-        send_ref[dev, 1, rows, :] = (dk[at, :] * (1.0 / LOG2_E)).astype(bf16)
-        send_ref[dev, 2, rows, :] = dv[at, :].astype(bf16)
-
-
-def attend_back(klo, x, do, onat, linv, lens):
-    n_dev, _, rows, _ = x.shape
-    span = n_dev * rows
+    dk[...] = dk[...] * (1.0 / LOG2_E)
+
+
+def attend_back(klo, q, k, v, do, onat, linv, lens):
+    span = q.shape[0]
     return pl.pallas_call(
         attend_back_kernel,
-        in_specs=[pl.BlockSpec(memory_space=pltpu.SMEM)] + [vmem()] * 5,
-        out_specs=vmem(),
-        out_shape=jax.ShapeDtypeStruct((n_dev, 3, rows, HD), bf16),
-        scratch_shapes=[
-            pltpu.VMEM((span, HD), bf16),
-            pltpu.VMEM((span, HD), bf16),
-            pltpu.VMEM((span, HD), bf16),
-            pltpu.VMEM((HD, span), bf16),
-            pltpu.VMEM((span, HD), bf16),
-            pltpu.VMEM((span, HD), f32),
-            pltpu.VMEM((span, HD), f32),
-            pltpu.VMEM((span, HD), f32),
-        ],
+        in_specs=[pl.BlockSpec(memory_space=pltpu.SMEM)] + [vmem()] * 7,
+        out_specs=[vmem()] * 3,
+        out_shape=[jax.ShapeDtypeStruct((span, HD), f32)] * 3,
+        scratch_shapes=[pltpu.VMEM((HD, span), bf16), pltpu.VMEM((span, HD), bf16)],
         compiler_params=pltpu.CompilerParams(vmem_limit_bytes=VMEM_BYTES),
         name="attend_back",
-    )(klo, x, do, onat, linv, lens)
+    )(klo, q, k, v, do, onat, linv, lens)
 
 
 OUT_ROWS = 160
@@ -587,6 +602,81 @@
     return total
 
 
+def shift(x, axis, step):
+    n = SIZES[axis]
+    return lax.ppermute(x, axis, [(i, (i + step) % n) for i in range(n)])
+
+
+def first_moves(x):
+    first, second = x[None, :HALF], x[None, HALF:]
+    pair = jnp.concatenate([first, shift(first, "xh", 1)], axis=0)
+    ring = jnp.concatenate([second] + [shift(second, "y", b) for b in (1, 2, 3)], axis=0)
+    return pair, ring
+
+
+def second_moves(pair, ring):
+    one = jnp.concatenate([pair] + [shift(pair, "y", b) for b in (1, 2, 3)], axis=0)
+    two = jnp.concatenate([ring, shift(ring, "xh", 1)], axis=0)
+    return [one, two, shift(one, "core", 1), shift(two, "core", 1)]
+
+
+def places_of_groups():
+    xh, y, core = (lax.axis_index(name) for name in CTX)
+    places = []
+    for other in range(2):
+        for side in range(2):
+            for i in range(GROUP):
+                b, a = (i // 2, i % 2) if side == 0 else (i % 4, i // 4)
+                dev = (((xh + a) % 2) * 4 + (y - b) % 4) * 2 + (core + other) % 2
+                places.append(dev if side == 0 else 31 - dev)
+    return jnp.stack(places).astype(jnp.int32)
+
+
+def sum_over_core(near, far):
+    return (near.astype(f32) + shift(far, "core", 1).astype(f32)).astype(bf16)
+
+
+def first_sums(plane):
+    one = plane[:GROUP].reshape((4, 2) + plane.shape[1:])
+    two = plane[GROUP:].reshape((2, 4) + plane.shape[1:])
+    two = (two[0].astype(f32) + shift(two[1], "xh", 1).astype(f32)).astype(bf16)
+    one = sum((shift(one[b], "y", -b).astype(f32) for b in (1, 2, 3)), one[0].astype(f32))
+    return one.astype(bf16), two
+
+
+def second_sums(one, two):
+    two = sum((shift(two[b], "y", -b).astype(f32) for b in (1, 2, 3)), two[0].astype(f32))
+    one = one[0].astype(f32) + shift(one[1], "xh", 1).astype(f32)
+    return jnp.concatenate([one, two], axis=0)
+
+
+def pick(v, i, n, axis):
+    return lax.dynamic_index_in_dim(v, lax.rem(i, n), axis, keepdims=False)
+
+
+def sum_over_xl(x):
+    xl = lax.axis_index("xl")
+    return pick(x, xl, 2, 1).astype(f32) + shift(pick(x, xl + 1, 2, 1), "xl", 1).astype(f32)
+
+
+def sum_over_z(x):
+    z = lax.axis_index("z")
+    low = x.astype(bf16)
+    total = pick(x, z, 4, 1)
+    for step in (1, 2, 3):
+        total = total + shift(pick(low, z + step, 4, 1), "z", step).astype(f32)
+    return total
+
+
+def gather_shard(x):
+    z = lax.axis_index("z")
+    xl = lax.axis_index("xl")
+    ring = [x] + [shift(x, "z", -step) for step in (1, 2, 3)]
+    ring = lax.dynamic_slice_in_dim(jnp.stack(ring + ring[:3]), lax.rem(4 - z, 4), 4, 0)
+    other = shift(ring, "xl", 1)
+    return jnp.stack([jnp.where(xl == 0, ring, other), jnp.where(xl == 0, other, ring)])
+
+
 def natural_of_permuted(x):
     tail = x.shape[1:]
     x = x.reshape((4, 4, 2, 2, 2) + tail)
@@ -633,44 +723,48 @@
     owned = w_in.shape[0]
     owned_gains = gains.shape[0]
 
+    n_x = 4
     low_in = w_in.astype(bf16)
-    own_qkv = jnp.concatenate(
+    n_dev = width // owned
+
+    own_head = jnp.concatenate(
         [
-            low_in[:, :q_width].reshape(owned, H_KV, 2 * HD),
-            low_in[:, q_width : q_width + kv_width].reshape(owned, H_KV, HD),
-            low_in[:, q_width + kv_width : attn_cols].reshape(owned, H_KV, HD),
+            low_in[:, :q_width].reshape(owned, H_Q, HD),
+            jnp.repeat(low_in[:, q_width : q_width + kv_width].reshape(owned, H_KV, HD), 2, axis=1),
+            jnp.repeat(low_in[:, q_width + kv_width : attn_cols].reshape(owned, H_KV, HD), 2, axis=1),
+            jnp.broadcast_to(
+                jnp.pad(gains.astype(bf16)[None, None], ((0, owned - 1), (0, 0), (0, HD - owned_gains))),
+                (owned, H_Q, HD),
+            ),
         ],
         axis=2,
-    ).reshape(owned, attn_cols)
-    own_gains = jnp.pad(gains.astype(bf16)[None, :], ((0, owned - 1), (0, HD - owned_gains)))
-    packed = jnp.concatenate([own_qkv, own_gains, low_in[:, attn_cols:]], axis=1)
-    packed = lax.all_gather(packed, AXIS_X, axis=0, tiled=True)
-    w_qkv = gathered(packed[:, : attn_cols + HD])
+    ).transpose(1, 0, 2)
+    pair, ring = first_moves(tokens[0])
     pairs = owner_pairs()
     own_out = lax.ppermute(w_out.astype(bf16), EVERY, [(p, n) for n, p in pairs])
-    own_out = lax.all_gather(own_out, AXIS_X, axis=0, tiled=True)
-    own_ffn = packed[:, attn_cols + HD :].reshape(CHUNK_ROWS, 2 * N_CHUNKS, CHUNK)
-    own_ffn = own_ffn.transpose(1, 0, 2).reshape(2 * N_CHUNKS * CHUNK_ROWS, CHUNK)
-    full = gathered(jnp.concatenate([own_out, own_ffn], axis=0)[None])
-
-    gain_rows = w_qkv[:, attn_cols:].reshape(width // owned, owned, HD)[:, 0, :owned_gains]
-    gain_vals = natural_of_permuted(gain_rows).reshape(-1).astype(f32)
+    own_ffn = low_in[:, attn_cols:].reshape(owned, 2 * N_CHUNKS, CHUNK)
+    own_ffn = own_ffn.transpose(1, 0, 2).reshape(2 * N_CHUNKS * owned, CHUNK)
+    own_rest = jnp.concatenate([own_out, own_ffn], axis=0)
+    own_rest = lax.all_gather(own_rest, AXIS_X, axis=0, tiled=False)
+    own_head, own_rest, pair, ring = lax.optimization_barrier((own_head, own_rest, pair, ring))
+    head = gather_shard(lax.all_to_all(own_head, CTX, 0, 0, tiled=True))
+    head = head.transpose(2, 0, 1, 3, 4)
+    gain_vals = head[:, :, :, 0, HEAD_COLS : HEAD_COLS + owned_gains].reshape(-1).astype(f32)
+    w_head = head[..., :HEAD_COLS].reshape(width, HEAD_COLS)
     gain_one = gain_vals[:width]
     gain_two = gain_vals[width : 2 * width]
     gain_query = gain_vals[2 * width : 2 * width + HD].reshape(1, HD)
     gain_key = gain_vals[2 * width + HD :].reshape(1, HD)
-
-    order = natural_of_permuted(jnp.arange(width, dtype=jnp.int32).reshape(width // owned, owned)).reshape(-1)
+    w_scaled = (w_head.astype(f32) * gain_one[:, None]).astype(bf16)
+
+    n_out = w_out.shape[0]
+    part_out = own_rest[:, :n_out].reshape(n_x * n_out, width)
+    part_ffn = own_rest[:, n_out:].reshape(n_x, 2 * N_CHUNKS, owned, CHUNK).transpose(1, 0, 2, 3)
+    part_ffn = part_ffn.reshape(2 * N_CHUNKS * CHUNK_ROWS, CHUNK)
+    full = gathered(jnp.concatenate([part_out, part_ffn], axis=0)[None])
+
+    order = natural_of_permuted(jnp.arange(width, dtype=jnp.int32).reshape(n_dev, owned)).reshape(-1)
     shuffle = (order[:, None] == jnp.arange(width, dtype=jnp.int32)[None, :]).astype(bf16)
-
-    inputs = tokens[0].astype(f32)
-    halves = jnp.arange(HD // 2, dtype=f32)
-    inverse = ROPE_BASE ** (-2.0 * halves / HD)
-    angle = positions[0].astype(f32)[:, None] * inverse[None, :]
-    cos_half = jnp.cos(angle)
-    sin_half = jnp.sin(angle)
-    cos = jnp.concatenate([cos_half, cos_half], axis=1)
-    sin = jnp.concatenate([-sin_half, sin_half], axis=1)
 
     def natural(x):
         x = x.reshape(n_ctx, 2, half)
@@ -683,15 +777,24 @@
     for number in range(1, 14):
         before = jnp.sum((docs < number).astype(jnp.int32))
         start = jnp.where(docs == number, before, start)
-    lens = jnp.where(live == 1, at - start, 0)
+    place_in = at - start
+    lens = jnp.where(live == 1, place_in, 0)
     klo = jnp.min((at - lens).reshape(span // BQ, BQ), axis=1) // BK
     lens = lens.reshape(span // BQ, BQ)
-
-    a = rms_norm(inputs, gain_one).astype(bf16)
-    a_perm = dot_nn(a, shuffle).astype(bf16)
-    send, query_raw, key_raw = project(a_perm, w_qkv, cos, sin, gain_query, gain_key)
-    x = lax.all_to_all(send, CTX, 0, 0, tiled=True)
-    o_send, o_nat, l_inv = attend(klo, x, lens)
+    halves = jnp.arange(HD // 2, dtype=f32)
+    inverse = ROPE_BASE ** (-2.0 * halves / HD)
+    angle = place_in.reshape(span, 1).astype(f32) * inverse[None, :]
+    cos_half = jnp.cos(angle)
+    sin_half = jnp.sin(angle)
+    cos = jnp.concatenate([cos_half, cos_half], axis=1)
+    sin = jnp.concatenate([-sin_half, sin_half], axis=1)
+
+    groups = second_moves(pair, ring)
+    place = places_of_groups()
+    q, k, v, query_raw, key_raw, inv = project(
+        place, groups, w_scaled, cos, sin, gain_query, gain_key
+    )
+    o_send, o_nat, l_inv = attend(klo, q, k, v, lens, rows)
     mixed = lax.all_to_all(o_send, CTX, 0, 0, tiled=True)
 
     output, grad_residual, do_send, features, resid_low, grads, gain_two_terms = middle(
@@ -701,37 +804,50 @@
     grads = grad_out(features, resid_low, cotangent[0], grads)
     do, grads = lax.optimization_barrier((do, grads))
     grads = lax.psum_scatter(grads, AXIS_YZ, scatter_dimension=0, tiled=True)[0]
-    n_x = 4
-
-    d_send = attend_back(klo, x, do, o_nat, l_inv, lens)
-    d_recv = lax.all_to_all(d_send, CTX, 0, 0, tiled=True)
-    grad_w_qkv, da_perm, gain_qk = project_back(
-        d_recv, query_raw, key_raw, cos, sin, gain_query, gain_key, w_qkv, a_perm.T
-    )
-    grad_w_qkv, grads = lax.optimization_barrier((grad_w_qkv, grads))
+
+    head_grads = attend_back(klo, q, k, v, do, o_nat, l_inv, lens)
+    da_near, da_far, dw_head, gain_qk = project_back(
+        place, groups, head_grads, (query_raw, key_raw, inv), cos, sin, gain_query, gain_key, w_head
+    )
+
+    gain_one_grad = jnp.sum(dw_head * w_head.astype(f32), axis=1)
+    grad_gains = jnp.concatenate([gain_one_grad, gain_two_terms[0], gain_qk[0], gain_qk[1]])
+    grad_gains = jnp.pad(
+        grad_gains.reshape(n_dev, 1, owned_gains), ((0, 0), (0, owned - 1), (0, HD - owned_gains))
+    )
+    dw_head = (dw_head * gain_one[:, None]).reshape(n_dev, owned, HEAD_COLS)
+    dw_head = jnp.concatenate([dw_head, grad_gains], axis=2).astype(bf16)
+    dw_head = sum_over_xl(dw_head.reshape(n_ctx, 2, 4, owned, PAD_COLS))
+    plane = sum_over_core(da_near, da_far)
+    dw_head, plane = lax.optimization_barrier((dw_head, plane))
+    dw_head = sum_over_z(dw_head).astype(bf16)
+    one, two = first_sums(plane)
+    dw_head, one, two = lax.optimization_barrier((dw_head, one, two))
+    dw_head = lax.all_to_all(dw_head, CTX, 0, 0, tiled=True).astype(f32)
+
+    grad_a = second_sums(one, two)
+    inputs = tokens[0].astype(f32)
+    input_grad = grad_residual + rms_back(inputs, gain_one, grad_a)[0]
+    owned_gain_grad = jnp.sum(dw_head[:, 0, HEAD_COLS : HEAD_COLS + owned_gains], axis=0)
+
+    def columns(x):
+        return x.transpose(1, 0, 2).reshape(owned, -1)
+
+    def over_pair(x):
+        return columns(jnp.sum(x.reshape(H_KV, 2, owned, HD), axis=1))
+
     out_part = grads[:OUT_ROWS].reshape(n_x, OUT_ROWS // n_x, width)
     ffn_part = grads[OUT_ROWS:].reshape(2 * N_CHUNKS, n_x, owned, CHUNK)
     ffn_part = ffn_part.transpose(1, 0, 2, 3).reshape(n_x, 2 * N_CHUNKS * owned, CHUNK)
     grads = sum_over_x(jnp.concatenate([out_part, ffn_part], axis=1))
     owned_out = lax.ppermute(grads[: OUT_ROWS // n_x], EVERY, pairs)
     owned_ffn = grads[OUT_ROWS // n_x :].reshape(2 * N_CHUNKS, owned, CHUNK)
-    owned_ffn = owned_ffn.transpose(1, 0, 2).reshape(owned, 2 * FF)
-    grad_w_qkv = lax.psum_scatter(grad_w_qkv, AXIS_YZ, scatter_dimension=0, tiled=True)
-    grad_a = dot_nt(da_perm.astype(bf16), shuffle)
-    grad_in_part, gain_one_terms = rms_back(inputs, gain_one, grad_a)
-    input_grad = grad_residual + grad_in_part
-    grad_gains = jnp.concatenate(
-        [jnp.sum(gain_one_terms, axis=0), gain_two_terms[0], gain_qk[0], gain_qk[1]]
-    )
-    owned_gain_grad = lax.psum_scatter(grad_gains, EVERY, scatter_dimension=0, tiled=True)
-    grad_w_qkv, owned_gain_grad = lax.optimization_barrier((grad_w_qkv, owned_gain_grad))
-    owned_qkv = sum_over_x(grad_w_qkv.reshape(n_x, owned, attn_cols)).reshape(owned, H_KV, 4 * HD)
     owned_in = jnp.concatenate(
         [
-            owned_qkv[:, :, : 2 * HD].reshape(owned, q_width),
-            owned_qkv[:, :, 2 * HD : 3 * HD].reshape(owned, kv_width),
-            owned_qkv[:, :, 3 * HD :].reshape(owned, kv_width),
-            owned_ffn,
+            columns(dw_head[:, :, :HD]),
+            over_pair(dw_head[:, :, HD : 2 * HD]),
+            over_pair(dw_head[:, :, 2 * HD : HEAD_COLS]),
+            columns(owned_ffn),
         ],
         axis=1,
     )

time: 538 us -> 482 us (0.90)
  the two profiles are of different devices: /device:TPU:96 before, /device:TPU:103 now
where the time goes in v2:
time: 482 us; the launch traced here: 475 us
  waiting for transfers between devices  153 us (32%)
  Pallas kernels  153 us (32%)
  starting transfers between devices  64.1 us (13%)
  other arithmetic  50.2 us (10%)
  local copies, waits for them, and re-layouts  27.6 us (6%)
  between operations  15.3 us (3%)
  blocking collectives  12.1 us (3%)
    ppermute x27, waiting for transfers between devices, shift(): return lax.ppermute(x, axis, [(i, (i + step) % n) for i in range(n)])  86.9 us
    pallas_call x1, Pallas kernels, attend_back(): pl.pallas_call(attend_back_kernel, in_specs=[pl.BlockSpec(memory_space=pl...  35.5 us
    pallas_call x1, Pallas kernels, project_back(): pl.pallas_call(project_back_kernel, grid_spec=pltpu.PrefetchScalarGridSpe...  33.1 us
    pallas_call x1, Pallas kernels, middle(): pl.pallas_call(middle_kernel, grid=(2 * N_CHUNKS + 2,), in_specs=[pl.Bloc...  32.3 us
    ppermute x27, starting transfers between devices, shift(): return lax.ppermute(x, axis, [(i, (i + step) % n) for i in range(n)])  28.5 us
    pallas_call x1, Pallas kernels, attend(): pl.pallas_call(attend_kernel, in_specs=[pl.BlockSpec(memory_space=pltpu.S...  26.6 us
    pallas_call x1, Pallas kernels, project(): pl.pallas_call(project_kernel, grid_spec=pltpu.PrefetchScalarGridSpec(num...  18.6 us
    all_to_all x1, waiting for transfers between devices, body(): head = gather_shard(lax.all_to_all(own_head, CTX, 0, 0, tiled=True))  17.2 us
  transfers between devices with their start and end apart: 38, of which 21 were waited for; matrix products, arithmetic and copies ran while one was open for 13% of the time, Pallas kernels for 25%

profile of v2, /device:TPU:103, one launch (start us, length us, event | category | flops | bytes accessed | tf_op | source)
XLA Modules:
  0.0 475.5 jit_solution(10012832258053840474)
XLA Ops:
  9.7 2.6 collective-permute-start.3
  15.4 2.1 collective-permute-start
  19.3 6.3 %collective-permute-done = bf16[40,1024]{1,0:T(8,128)(2,1)S(1)} collective-permute-done((bf16[40,1024]{1,0:T(8,128)(2,1)S(1)}, bf16[40,1024]{1,0:T(8,128)(2,1)S(1)}, u32[]{:S(2)}, u32[]{:S(2)}) %collective-permute-start) | collective-permute-done | bytes 81952 | tf_op jit(solution)/shard_map/ppermute | solution.py:744
  25.6 12.1 %all-gather = bf16[352,1024]{1,0:T(8,128)(2,1)S(1)} all-gather(bf16[88,1024]{1,0:T(8,128)(2,1)S(1)} %pad_maximum_fusion.6), channel_id=2, replica_groups=mesh['xh'=2,'y'=4,'core'=2,'xl'=2,'z'=4] {'xh','xl'}, dimensions={0}, use_global_device_ids=true | all-gather | bytes 901120 | tf_op jit(solution)/shard_map/all_gather | solution.py:748
  41.1 8.4 %convert_bitcast_fusion = (f32[4096]{0:T(1024)S(1)}, s32[32,128]{1,0:T(8,128)S(1)}) fusion(s32[]{:T(128)} %get-tuple-element.141, s32[]{:T(128)} %get-tuple-element.137, s32[]{:T(128)} %get-tuple-element.95, s32[]{:T(128)} %get-tuple-element.93, s32[]{:T(128)} %get-tuple-element.139, s32[]{:T(128)} %get-tuple-element.143, s32[]{:T(128)} %get-tuple-element.94, ...), kind=kLoop, calls=%fused_computation.115 | loop fusion | flops 126976 | bytes 49204 | tf_op jit(solution)/shard_map/convert_element_type | solution.py:786
  50.2 9.4 %fusion.11 = (f32[4096,64]{1,0:T(8,128)S(1)}, f32[4096,64]{1,0:T(8,128)}, f32[4096,64]{1,0:T(8,128)}) fusion(f32[64]{0:T(128)S(1)} %multiply_power_fusion, f32[4096]{0:T(1024)S(1)} %get-tuple-element.107), kind=kLoop, calls=%fused_computation.41 | loop fusion | flops 524288 | bytes 3162368 | tf_op jit(solution)/shard_map/neg | solution.py:790
  59.6 2.8 collective-permute-start.5
  62.3 4.1 collective-permute-start.6
  66.5 2.1 collective-permute-start.7
  68.6 6.0 %all-to-all-start = ((bf16[16,8,512]{2,1,0:T(8,128)(2,1)}), bf16[16,8,512]{2,1,0:T(8,128)(2,1)S(1)}, u32[]{:S(2)}, u32[]{:S(2)}) async-start(bf16[16,8,512]{2,1,0:T(8,128)(2,1)} %maximum_bitcast_fusion.1), calls=%async_computation | async-start | bytes 262144 | tf_op jit(solution)/shard_map/all_to_all | solution.py:750
  74.6 2.3 constant_dynamic-update-slice_fusion.5
  77.8 17.2 %all-to-all-done = bf16[16,8,512]{2,1,0:T(8,128)(2,1)S(1)} async-done(((bf16[16,8,512]{2,1,0:T(8,128)(2,1)}), bf16[16,8,512]{2,1,0:T(8,128)(2,1)S(1)}, u32[]{:S(2)}, u32[]{:S(2)}) %all-to-all-start) | async-done | bytes 131104 | tf_op jit(solution)/shard_map/all_to_all | solution.py:750
  95.5 8.9 %collective-permute-done.11 = bf16[16,8,512]{2,1,0:T(8,128)(2,1)S(1)} collective-permute-done((bf16[16,8,512]{2,1,0:T(8,128)(2,1)S(1)}, bf16[16,8,512]{2,1,0:T(8,128)(2,1)S(1)}, u32[]{:S(2)}, u32[]{:S(2)}) %collective-permute-start.11) | collective-permute-done | bytes 131104 | tf_op jit(solution)/shard_map/ppermute | solution.py:607
  104.4 9.4 %collective-permute-done.12 = bf16[16,8,512]{2,1,0:T(8,128)(2,1)S(1)} collective-permute-done((bf16[16,8,512]{2,1,0:T(8,128)(2,1)S(1)}, bf16[16,8,512]{2,1,0:T(8,128)(2,1)S(1)}, u32[]{:S(2)}, u32[]{:S(2)}) %collective-permute-start.12) | collective-permute-done | bytes 131104 | tf_op jit(solution)/shard_map/ppermute | solution.py:607
  113.8 7.7 %collective-permute-done.13 = bf16[16,8,512]{2,1,0:T(8,128)(2,1)S(1)} collective-permute-done((bf16[16,8,512]{2,1,0:T(8,128)(2,1)S(1)}, bf16[16,8,512]{2,1,0:T(8,128)(2,1)S(1)}, u32[]{:S(2)}, u32[]{:S(2)}) %collective-permute-start.13) | collective-permute-done | bytes 131104 | tf_op jit(solution)/shard_map/ppermute | solution.py:607
  125.3 2.0 constant_dynamic-update-slice_fusion.x0
  127.4 2.4 collective-permute-start.9
  129.8 2.3 constant_dynamic-update-slice_fusion.4.x1
  133.1 3.2 pad_maximum_fusion
  136.3 9.4 %collective-permute-done.14 = bf16[4,16,8,512]{3,2,0,1:T(8,128)(2,1)S(1)} collective-permute-done((bf16[4,16,8,512]{3,2,0,1:T(8,128)(2,1)S(1)}, bf16[4,16,8,512]{3,2,0,1:T(8,128)(2,1)S(1)}, u32[]{:S(2)}, u32[]{:S(2)}) %collective-permute-start.14) | collective-permute-done | bytes 524320 | tf_op jit(solution)/shard_map/ppermute | solution.py:607
  146.9 18.6 %project.1 = (bf16[4096,128]{1,0:T(8,128)(2,1)S(1)}, bf16[4096,128]{1,0:T(8,128)(2,1)S(1)}, bf16[4096,128]{1,0:T(8,128)(2,1)S(1)}, f32[4096,128]{1,0:T(8,128)S(1...) custom-call(s32[32]{0:T(128)S(1)} %stack.158.place_ref, bf16[8,128,1024]{2,1,0:T(8,128)(2,1)} %constant_dynamic-update-slice_fusion.x0, ...), custom_call_target="tpu_custom_call" | custom-call | tf_op jit(solution)/shard_map/project/pallas_call | solution.py:138
  166.8 26.6 %attend.1 = (bf16[16,256,128]{2,1,0:T(8,128)(2,1)S(1)}, f32[4096,128]{1,0:T(8,128)}, f32[16,256]{1,0:T(8,128)S(1)}) custom-call(s32[16]{0:T(128)S(1)} %and_select_fusion.klo_ref, bf16[4096,128]{1,0:T(8,128)(2,1)S(1)} %get-tuple-element.51.q_ref, bf16[4096,128]{1,0:T(8,128)(2,1)S(1)} %get-tuple-element.52.k_ref, ...), custom_call_target="tpu_custom_call" | custom-call | tf_op jit(solution)/shard_map/attend/pallas_call | solution.py:296
  194.4 7.9 %all-to-all-start.1 = ((bf16[16,256,128]{2,1,0:T(8,128)(2,1)}), bf16[16,256,128]{2,1,0:T(8,128)(2,1)S(1)}, u32[]{:S(2)}, u32[]{:S(2)}) async-start(bf16[16,256,128]{2,1,0:T(8,128)(2,1)} %copy-done.9), calls=%async_computation.1 | async-start | bytes 2097152 | tf_op jit(solution)/shard_map/all_to_all | solution.py:798
  204.3 12.6 %all-to-all-done.1.mixed_ref = bf16[16,256,128]{2,1,0:T(8,128)(2,1)S(1)} async-done(((bf16[16,256,128]{2,1,0:T(8,128)(2,1)}), bf16[16,256,128]{2,1,0:T(8,128)(2,1)S(1)}, u32[]{:S(2)}, u32[]{:S(2)}) %all-to-all-start.1) | async-done | bytes 1048608 | tf_op jit(solution)/shard_map/all_to_all | solution.py:798
  216.9 32.3 %middle.1 = (f32[256,1024]{1,0:T(8,128)}, f32[256,1024]{1,0:T(8,128)S(1)}, bf16[16,256,128]{2,1,0:T(8,128)(2,1)S(1)}, bf16[256,5120]{1,0:T(8,128)(2,1)}, bf16[25...) custom-call(bf16[32,352,1024]{2,1,0:T(8,128)(2,1)} %bitcast.207, ...), custom_call_target="tpu_custom_call" | custom-call | tf_op jit(solution)/shard_map/middle/pallas_call | solution.py:484
  251.9 7.8 %all-to-all-start.2 = ((bf16[16,256,128]{2,1,0:T(8,128)(2,1)}), bf16[16,256,128]{2,1,0:T(8,128)(2,1)}, u32[]{:S(2)}, u32[]{:S(2)}) async-start(bf16[16,256,128]{2,1,0:T(8,128)(2,1)} %copy-done.8), calls=%async_computation.2 | async-start | bytes 2097152 | tf_op jit(solution)/shard_map/all_to_all | solution.py:803
  261.7 7.3 %grad_out.1 = bf16[32,352,1024]{2,1,0:T(8,128)(2,1)} custom-call(bf16[256,5120]{1,0:T(8,128)(2,1)S(1)} %copy-done.5, bf16[256,1024]{1,0:T(8,128)(2,1)S(1)} %copy-done.13, bf16[256,1024]{1,0:T(8,128)(2,1)S(1)} %bitcast.205, bf16[32,352,1024]{2,1,0:T(8,128)(2,1)} %get-tuple-element.60.grads_ref), custom_call_target="tpu_custom_call", output_to_operand_aliasing={{}: (3, {})} | custom-call | tf_op jit(solution)/shard_map/grad_out/pallas_call | solution.py:559
  269.0 5.9 %all-to-all-done.2.do_ref = bf16[16,256,128]{2,1,0:T(8,128)(2,1)} async-done(((bf16[16,256,128]{2,1,0:T(8,128)(2,1)}), bf16[16,256,128]{2,1,0:T(8,128)(2,1)}, u32[]{:S(2)}, u32[]{:S(2)}) %all-to-all-start.2) | async-done | bytes 1048608 | tf_op jit(solution)/shard_map/all_to_all | solution.py:803
  276.2 35.5 %attend_back.1 = (f32[4096,128]{1,0:T(8,128)}, f32[4096,128]{1,0:T(8,128)}, f32[4096,128]{1,0:T(8,128)}) custom-call(s32[16]{0:T(128)S(1)} %and_select_fusion.klo_ref, bf16[4096,128]{1,0:T(8,128)(2,1)S(1)} %get-tuple-element.51.q_ref, bf16[4096,128]{1,0:T(8,128)(2,1)S(1)} %copy-done.2, bf16[4096,128]{1,0:T(8,128)(2,1)S(1)} %copy-done.4, ...), custom_call_target="tpu_custom_call" | custom-call | tf_op jit(solution)/shard_map/attend_back/pallas_call | solution.py:357
  311.7 33.1 %project_back.1 = (bf16[16,128,1024]{2,1,0:T(8,128)(2,1)}, bf16[16,128,1024]{2,1,0:T(8,128)(2,1)}, f32[1024,384]{1,0:T(8,128)}, f32[8,128]{1,0:T(8,128)}) custom-call(s32[32]{0:T(128)} %copy-done.14, bf16[8,128,1024]{2,1,0:T(8,128)(2,1)} %constant_dynamic-update-slice_fusion.x0, bf16[8,128,1024]{2,1,0:T(8,128)(2,1)} %constant_dynamic-update-slice_fusion.4.x1, ...), custom_call_target="tpu_custom_call" | custom-call | tf_op jit(solution)/shard_map/project_back/pallas_call | solution.py:204
  346.0 1.9 fusion.2
  348.9 13.6 %collective-permute-done.15 = bf16[16,4,8,512]{3,2,1,0:T(8,128)(2,1)S(1)} collective-permute-done((bf16[16,4,8,512]{3,2,1,0:T(8,128)(2,1)S(1)}, bf16[16,4,8,512]{3,2,1,0:T(8,128)(2,1)S(1)}, u32[]{:S(2)}, u32[]{:S(2)}) %collective-permute-start.15) | collective-permute-done | bytes 524320 | tf_op jit(solution)/shard_map/ppermute | solution.py:607
  362.6 5.8 %add_convert_fusion = bf16[16,128,1024]{2,1,0:T(8,128)(2,1)S(1)} fusion(bf16[16,128,1024]{2,1,0:T(8,128)(2,1)} %collective-permute-done.16, bf16[16,128,1024]{2,1,0:T(8,128)(2,1)} %get-tuple-element.73), kind=kLoop, calls=%fused_computation | loop fusion | flops 8388608 | bytes 12582912 | tf_op jit(solution)/shard_map/convert_element_type | solution.py:636
  369.6 2.2 collective-permute-start.23
  375.4 4.7 collective-permute-done.17
  380.5 5.3 %collective-permute-done.18 = bf16[16,8,512]{2,1,0:T(8,128)(2,1)} collective-permute-done((bf16[16,8,512]{2,1,0:T(8,128)(2,1)S(1)}, bf16[16,8,512]{2,1,0:T(8,128)(2,1)}, u32[]{:S(2)}, u32[]{:S(2)}) %collective-permute-start.18) | collective-permute-done | bytes 131104 | tf_op jit(solution)/shard_map/ppermute | solution.py:607
  385.8 5.4 %collective-permute-done.19 = bf16[16,8,512]{2,1,0:T(8,128)(2,1)S(1)} collective-permute-done((bf16[16,8,512]{2,1,0:T(8,128)(2,1)S(1)}, bf16[16,8,512]{2,1,0:T(8,128)(2,1)S(1)}, u32[]{:S(2)}, u32[]{:S(2)}) %collective-permute-start.19) | collective-permute-done | bytes 131104 | tf_op jit(solution)/shard_map/ppermute | solution.py:607
  392.9 10.8 %collective-permute-done.22 = bf16[2,128,1024]{2,1,0:T(8,128)(2,1)} collective-permute-done((bf16[2,128,1024]{2,1,0:T(8,128)(2,1)S(1)}, bf16[2,128,1024]{2,1,0:T(8,128)(2,1)}, u32[]{:S(2)}, u32[]{:S(2)}) %collective-permute-start.22) | collective-permute-done | bytes 524320 | tf_op jit(solution)/shard_map/ppermute | solution.py:607
  405.5 2.0 add_convert_fusion.1
  407.5 5.9 %all-to-all-start.3 = ((bf16[16,8,512]{2,1,0:T(8,128)(2,1)}), bf16[16,8,512]{2,1,0:T(8,128)(2,1)S(1)}, u32[]{:S(2)}, u32[]{:S(2)}) async-start(bf16[16,8,512]{2,1,0:T(8,128)(2,1)} %fusion.23), calls=%async_computation.3 | async-start | bytes 262144 | tf_op jit(solution)/shard_map/all_to_all | solution.py:826
  414.5 2.6 collective-permute-start.25
  420.1 2.6 collective-permute-done.24
  425.8 6.9 %collective-permute-done.27 = bf16[128,1024]{1,0:T(8,128)(2,1)} collective-permute-done((bf16[128,1024]{1,0:T(8,128)(2,1)S(1)}, bf16[128,1024]{1,0:T(8,128)(2,1)}, u32[]{:S(2)}, u32[]{:S(2)}) %collective-permute-start.27) | collective-permute-done | bytes 262176 | tf_op jit(solution)/shard_map/ppermute | solution.py:607
  436.5 2.8 collective-permute-start.28
  441.4 5.0 %collective-permute-done.28 = bf16[88,1024]{1,0:T(8,128)(2,1)S(1)} collective-permute-done((bf16[88,1024]{1,0:T(8,128)(2,1)S(1)}, bf16[88,1024]{1,0:T(8,128)(2,1)S(1)}, u32[]{:S(2)}, u32[]{:S(2)}) %collective-permute-start.28) | collective-permute-done | bytes 180256 | tf_op jit(solution)/shard_map/ppermute | solution.py:601
  446.4 4.3 collective-permute-done.30
  450.8 1.9 collective-permute-start.31
  454.0 13.6 %collective-permute-done.31 = f32[40,1024]{1,0:T(8,128)S(1)} collective-permute-done((f32[40,1024]{1,0:T(8,128)S(1)}, f32[40,1024]{1,0:T(8,128)S(1)}, u32[]{:S(2)}, u32[]{:S(2)}) %collective-permute-start.31) | collective-permute-done | bytes 163872 | tf_op jit(solution)/shard_map/ppermute | solution.py:843
  (209 shorter events, 54.7 us)
Async XLA Ops:
  7.2 209.7 %all-gather.4.cloned.1.call-start = ((), (), s32[]{:S(2)}) async-start(), calls=%async_computation.6 | async-start | bytes 23789568 | tf_op jit(solution)/shard_map/all_gather | solution.py:588
  8.3 29.4 %collective-permute-start.2 = (bf16[1,128,1024]{2,1,0:T(8,128)(2,1)S(1)}, bf16[1,128,1024]{2,1,0:T(8,128)(2,1)S(1)}, u32[]{:S(2)}, u32[]{:S(2)}) collective-permute-start(bf16[1,128,1024]{2,1,0:T(8,128)(2,1)S(1)} %get-tuple-element.127), channel_id=1, source_target_pairs={{0,16},{16,32},{32,48},{48,0},{1,17},{17,33},{33,49},{49,1},{2,18}... | collective-permute-start | bytes 786440 | tf_op jit(solution)/shard_map/ppermute | solution.py:607
  9.7 28.0 %collective-permute-start.3 = (bf16[1,128,1024]{2,1,0:T(8,128)(2,1)S(1)}, bf16[1,128,1024]{2,1,0:T(8,128)(2,1)S(1)}, u32[]{:S(2)}, u32[]{:S(2)}) collective-permute-start(bf16[1,128,1024]{2,1,0:T(8,128)(2,1)S(1)} %get-tuple-element.127), channel_id=1, source_target_pairs={{0,32},{16,48},{32,0},{48,16},{1,33},{17,49},{33,1},{49,17},{2,34}... | collective-permute-start | bytes 786440 | tf_op jit(solution)/shard_map/ppermute | solution.py:607
  12.3 25.4 %collective-permute-start.4 = (bf16[1,128,1024]{2,1,0:T(8,128)(2,1)S(1)}, bf16[1,128,1024]{2,1,0:T(8,128)(2,1)S(1)}, u32[]{:S(2)}, u32[]{:S(2)}) collective-permute-start(bf16[1,128,1024]{2,1,0:T(8,128)(2,1)S(1)} %get-tuple-element.127), channel_id=1, source_target_pairs={{0,48},{16,0},{32,16},{48,32},{1,49},{17,1},{33,17},{49,33},{2,50}... | collective-permute-start | bytes 786440 | tf_op jit(solution)/shard_map/ppermute | solution.py:607
  13.4 24.3 %collective-permute-start.1 = (bf16[1,128,1024]{2,1,0:T(8,128)(2,1)S(1)}, bf16[1,128,1024]{2,1,0:T(8,128)(2,1)S(1)}, u32[]{:S(2)}, u32[]{:S(2)}) collective-permute-start(bf16[1,128,1024]{2,1,0:T(8,128)(2,1)S(1)} %get-tuple-element.128), channel_id=1, source_target_pairs={{0,64},{64,0},{1,65},{65,1},{2,66},{66,2},{3,67},{67,3},{4,68},{68... | collective-permute-start | bytes 786440 | tf_op jit(solution)/shard_map/ppermute | solution.py:607
  15.4 10.2 %collective-permute-start = (bf16[40,1024]{1,0:T(8,128)(2,1)S(1)}, bf16[40,1024]{1,0:T(8,128)(2,1)S(1)}, u32[]{:S(2)}, u32[]{:S(2)}) collective-permute-start(bf16[40,1024]{1,0:T(8,128)(2,1)S(1)} %convert_element_type.188), channel_id=1, source_target_pairs={{0,0},{8,1},{16,2},{24,3},{1,4},{9,5},{17,6},{25,7},{4,8},{12,9},{... | collective-permute-start | bytes 245768 | tf_op jit(solution)/shard_map/ppermute | solution.py:744
  50.1 96.8 %copy-start.14 = (s32[32]{0:T(128)}, s32[32]{0:T(128)S(1)}, u32[]{:S(2)}) copy-start(s32[32]{0:T(128)S(1)} %stack.158.place_ref) | copy-start | bytes 388
  59.6 62.0 %collective-permute-start.5 = (bf16[2,128,1024]{2,1,0:T(8,128)(2,1)S(1)}, bf16[2,128,1024]{2,1,0:T(8,128)(2,1)}, u32[]{:S(2)}, u32[]{:S(2)}) collective-permute-start(bf16[2,128,1024]{2,1,0:T(8,128)(2,1)S(1)} %pad_maximum_fusion.4), channel_id=1, source_target_pairs={{0,16},{16,32},{32,48},{48,0},{1,17},{17,33},{33,49},{49,1},{2,18}... | collective-permute-start | bytes 1572872 | tf_op jit(solution)/shard_map/ppermute | solution.py:607
  62.3 61.1 %collective-permute-start.6 = (bf16[2,128,1024]{2,1,0:T(8,128)(2,1)S(1)}, bf16[2,128,1024]{2,1,0:T(8,128)(2,1)}, u32[]{:S(2)}, u32[]{:S(2)}) collective-permute-start(bf16[2,128,1024]{2,1,0:T(8,128)(2,1)S(1)} %pad_maximum_fusion.4), channel_id=1, source_target_pairs={{0,32},{16,48},{32,0},{48,16},{1,33},{17,49},{33,1},{49,17},{2,34}... | collective-permute-start | bytes 1572872 | tf_op jit(solution)/shard_map/ppermute | solution.py:607
  66.5 58.9 %collective-permute-start.7 = (bf16[2,128,1024]{2,1,0:T(8,128)(2,1)S(1)}, bf16[2,128,1024]{2,1,0:T(8,128)(2,1)}, u32[]{:S(2)}, u32[]{:S(2)}) collective-permute-start(bf16[2,128,1024]{2,1,0:T(8,128)(2,1)S(1)} %pad_maximum_fusion.4), channel_id=1, source_target_pairs={{0,48},{16,0},{32,16},{48,32},{1,49},{17,1},{33,17},{49,33},{2,50}... | collective-permute-start | bytes 1572872 | tf_op jit(solution)/shard_map/ppermute | solution.py:607
  68.6 26.4 %all-to-all-start = ((bf16[16,8,512]{2,1,0:T(8,128)(2,1)}), bf16[16,8,512]{2,1,0:T(8,128)(2,1)S(1)}, u32[]{:S(2)}, u32[]{:S(2)}) async-start(bf16[16,8,512]{2,1,0:T(8,128)(2,1)} %maximum_bitcast_fusion.1), calls=%async_computation | async-start | bytes 262144 | tf_op jit(solution)/shard_map/all_to_all | solution.py:750
  74.6 55.3 %collective-permute-start.8 = (bf16[4,128,1024]{2,1,0:T(8,128)(2,1)}, bf16[4,128,1024]{2,1,0:T(8,128)(2,1)}, u32[]{:S(2)}, u32[]{:S(2)}) collective-permute-start(bf16[4,128,1024]{2,1,0:T(8,128)(2,1)} %pad_maximum_fusion.2), channel_id=1, source_target_pairs={{0,64},{64,0},{1,65},{65,1},{2,66},{66,2},{3,67},{67,3},{4,68},{68... | collective-permute-start | bytes 3145736 | tf_op jit(solution)/shard_map/ppermute | solution.py:607
  95.0 9.4 %collective-permute-start.11 = (bf16[16,8,512]{2,1,0:T(8,128)(2,1)S(1)}, bf16[16,8,512]{2,1,0:T(8,128)(2,1)S(1)}, u32[]{:S(2)}, u32[]{:S(2)}) collective-permute-start(bf16[16,8,512]{2,1,0:T(8,128)(2,1)S(1)} %all-to-all-done), channel_id=1, source_target_pairs={{0,3},{1,0},{2,1},{3,2},{4,7},{5,4},{6,5},{7,6},{8,11},{9,8},{10,9... | collective-permute-start | bytes 393224 | tf_op jit(solution)/shard_map/ppermute | solution.py:607
  104.4 9.4 %collective-permute-start.12 = (bf16[16,8,512]{2,1,0:T(8,128)(2,1)S(1)}, bf16[16,8,512]{2,1,0:T(8,128)(2,1)S(1)}, u32[]{:S(2)}, u32[]{:S(2)}) collective-permute-start(bf16[16,8,512]{2,1,0:T(8,128)(2,1)S(1)} %all-to-all-done), channel_id=1, source_target_pairs={{0,2},{1,3},{2,0},{3,1},{4,6},{5,7},{6,4},{7,5},{8,10},{9,11},{10,... | collective-permute-start | bytes 393224 | tf_op jit(solution)/shard_map/ppermute | solution.py:607
  113.8 7.7 %collective-permute-start.13 = (bf16[16,8,512]{2,1,0:T(8,128)(2,1)S(1)}, bf16[16,8,512]{2,1,0:T(8,128)(2,1)S(1)}, u32[]{:S(2)}, u32[]{:S(2)}) collective-permute-start(bf16[16,8,512]{2,1,0:T(8,128)(2,1)S(1)} %all-to-all-done), channel_id=1, source_target_pairs={{0,1},{1,2},{2,3},{3,0},{4,5},{5,6},{6,7},{7,4},{8,9},{9,10},{10,1... | collective-permute-start | bytes 393224 | tf_op jit(solution)/shard_map/ppermute | solution.py:607
  127.4 19.2 %collective-permute-start.9 = (bf16[8,128,1024]{2,1,0:T(8,128)(2,1)}, bf16[8,128,1024]{2,1,0:T(8,128)(2,1)}, u32[]{:S(2)}, u32[]{:S(2)}) collective-permute-start(bf16[8,128,1024]{2,1,0:T(8,128)(2,1)} %constant_dynamic-update-slice_fusion.x0), channel_id=1, source_target_pairs={{0,8},{8,0},{1,9},{9,1},{2,10},{10,2},{3,11},{11,3},{4,12},{12,4},... | collective-permute-start | bytes 6291464 | tf_op jit(solution)/shard_map/ppermute | solution.py:607
  132.1 14.5 %collective-permute-start.10 = (bf16[8,128,1024]{2,1,0:T(8,128)(2,1)}, bf16[8,128,1024]{2,1,0:T(8,128)(2,1)}, u32[]{:S(2)}, u32[]{:S(2)}) collective-permute-start(bf16[8,128,1024]{2,1,0:T(8,128)(2,1)} %constant_dynamic-update-slice_fusion.4.x1), channel_id=1, source_target_pairs={{0,8},{8,0},{1,9},{9,1},{2,10},{10,2},{3,11},{11,3},{4,12},{12,4},... | collective-permute-start | bytes 6291464 | tf_op jit(solution)/shard_map/ppermute | solution.py:607
  132.2 13.5 %collective-permute-start.14 = (bf16[4,16,8,512]{3,2,0,1:T(8,128)(2,1)S(1)}, bf16[4,16,8,512]{3,2,0,1:T(8,128)(2,1)S(1)}, u32[]{:S(2)}, u32[]{:S(2)}) collective-permute-start(bf16[4,16,8,512]{3,2,0,1:T(8,128)(2,1)S(1)} %constant_dynamic-slice_fusion), channel_id=1, source_target_pairs={{0,4},{4,0},{1,5},{5,1},{2,6},{6,2},{3,7},{7,3},{8,12},{12,8},{9,1... | collective-permute-start | bytes 1572872 | tf_op jit(solution)/shard_map/ppermute | solution.py:607
  146.4 19.1 %copy-start.15 = (f32[1,128]{1,0:T(1,128)}, f32[1,128]{1,0:T(1,128)S(1)}, u32[]{:S(2)}) copy-start(f32[1,128]{1,0:T(1,128)S(1)} %get-tuple-element.149.gk_ref) | copy-start | bytes 1540
  166.8 26.6 %copy-start.1 = (bf16[4096,128]{1,0:T(8,128)(2,1)}, bf16[4096,128]{1,0:T(8,128)(2,1)S(1)}, u32[]{:S(2)}) copy-start(bf16[4096,128]{1,0:T(8,128)(2,1)S(1)} %get-tuple-element.52.k_ref) | copy-start | bytes 3145732
  166.8 26.6 %copy-start.3 = (bf16[4096,128]{1,0:T(8,128)(2,1)}, bf16[4096,128]{1,0:T(8,128)(2,1)S(1)}, u32[]{:S(2)}) copy-start(bf16[4096,128]{1,0:T(8,128)(2,1)S(1)} %get-tuple-element.53.v_ref) | copy-start | bytes 3145732
  194.4 22.4 %copy-start = (bf16[1,256,1024]{2,1,0:T(8,128)(2,1)S(1)}, bf16[1,256,1024]{2,1,0:T(8,128)(2,1)}, u32[]{:S(2)}) copy-start(bf16[1,256,1024]{2,1,0:T(8,128)(2,1)} %param.14) | copy-start | bytes 1572868
  194.4 22.4 %copy-start.6 = (bf16[1,256,1024]{2,1,0:T(8,128)(2,1)S(1)}, bf16[1,256,1024]{2,1,0:T(8,128)(2,1)}, u32[]{:S(2)}) copy-start(bf16[1,256,1024]{2,1,0:T(8,128)(2,1)} %param.15) | copy-start | bytes 1572868
  194.4 22.4 %all-to-all-start.1 = ((bf16[16,256,128]{2,1,0:T(8,128)(2,1)}), bf16[16,256,128]{2,1,0:T(8,128)(2,1)S(1)}, u32[]{:S(2)}, u32[]{:S(2)}) async-start(bf16[16,256,128]{2,1,0:T(8,128)(2,1)} %copy-done.9), calls=%async_computation.1 | async-start | bytes 2097152 | tf_op jit(solution)/shard_map/all_to_all | solution.py:798
  251.9 23.0 %all-to-all-start.2 = ((bf16[16,256,128]{2,1,0:T(8,128)(2,1)}), bf16[16,256,128]{2,1,0:T(8,128)(2,1)}, u32[]{:S(2)}, u32[]{:S(2)}) async-start(bf16[16,256,128]{2,1,0:T(8,128)(2,1)} %copy-done.8), calls=%async_computation.2 | async-start | bytes 2097152 | tf_op jit(solution)/shard_map/all_to_all | solution.py:803
  259.7 174.5 %reduce-scatter.2.cloned.1.call-start = ((), (), s32[]{:S(2)}) async-start(), calls=%async_computation.5 | async-start | bytes 23789568 | tf_op jit(solution)/shard_map/reduce_scatter | solution.py:806
  311.7 34.3 %copy-start.19 = (bf16[16,2,4,8,384]{4,3,2,1,0:T(8,128)(2,1)S(1)}, bf16[16,2,4,8,384]{4,3,2,1,0:T(8,128)(2,1)}, u32[]{:S(2)}) copy-start(bf16[16,2,4,8,384]{4,3,2,1,0:T(8,128)(2,1)} %copy-done.18) | copy-start | bytes 2359300
  344.8 17.9 %collective-permute-start.16 = (bf16[16,128,1024]{2,1,0:T(8,128)(2,1)}, bf16[16,128,1024]{2,1,0:T(8,128)(2,1)}, u32[]{:S(2)}, u32[]{:S(2)}) collective-permute-start(bf16[16,128,1024]{2,1,0:T(8,128)(2,1)} %get-tuple-element.74), channel_id=1, source_target_pairs={{0,8},{8,0},{1,9},{9,1},{2,10},{10,2},{3,11},{11,3},{4,12},{12,4},... | collective-permute-start | bytes 12582920 | tf_op jit(solution)/shard_map/ppermute | solution.py:607
  348.5 13.9 %collective-permute-start.15 = (bf16[16,4,8,512]{3,2,1,0:T(8,128)(2,1)S(1)}, bf16[16,4,8,512]{3,2,1,0:T(8,128)(2,1)S(1)}, u32[]{:S(2)}, u32[]{:S(2)}) collective-permute-start(bf16[16,4,8,512]{3,2,1,0:T(8,128)(2,1)S(1)} %fusion.13), channel_id=1, source_target_pairs={{0,4},{4,0},{1,5},{5,1},{2,6},{6,2},{3,7},{7,3},{8,12},{12,8},{9,1... | collective-permute-start | bytes 1572872 | tf_op jit(solution)/shard_map/ppermute | solution.py:607
  369.6 36.0 %collective-permute-start.23 = (bf16[4,128,1024]{2,1,0:T(8,128)(2,1)}, bf16[4,128,1024]{2,1,0:T(8,128)(2,1)}, u32[]{:S(2)}, u32[]{:S(2)}) collective-permute-start(bf16[4,128,1024]{2,1,0:T(8,128)(2,1)} %slice.165), channel_id=1, source_target_pairs={{0,64},{64,0},{1,65},{65,1},{2,66},{66,2},{3,67},{67,3},{4,68},{68... | collective-permute-start | bytes 3145736 | tf_op jit(solution)/shard_map/ppermute | solution.py:607
  371.9 8.2 %collective-permute-start.17 = (bf16[16,8,512]{2,1,0:T(8,128)(2,1)S(1)}, bf16[16,8,512]{2,1,0:T(8,128)(2,1)S(1)}, u32[]{:S(2)}, u32[]{:S(2)}) collective-permute-start(bf16[16,8,512]{2,1,0:T(8,128)(2,1)S(1)} %get-tuple-element.124), channel_id=1, source_target_pairs={{0,1},{1,2},{2,3},{3,0},{4,5},{5,6},{6,7},{7,4},{8,9},{9,10},{10,1... | collective-permute-start | bytes 393224 | tf_op jit(solution)/shard_map/ppermute | solution.py:607
  373.3 19.5 %collective-permute-start.20 = (bf16[2,128,1024]{2,1,0:T(8,128)(2,1)}, bf16[2,128,1024]{2,1,0:T(8,128)(2,1)S(1)}, u32[]{:S(2)}, u32[]{:S(2)}) collective-permute-start(bf16[2,128,1024]{2,1,0:T(8,128)(2,1)} %get-tuple-element.111), channel_id=1, source_target_pairs={{0,48},{16,0},{32,16},{48,32},{1,49},{17,1},{33,17},{49,33},{2,50}... | collective-permute-start | bytes 1572872 | tf_op jit(solution)/shard_map/ppermute | solution.py:607
  374.9 18.0 %collective-permute-start.21 = (bf16[2,128,1024]{2,1,0:T(8,128)(2,1)}, bf16[2,128,1024]{2,1,0:T(8,128)(2,1)S(1)}, u32[]{:S(2)}, u32[]{:S(2)}) collective-permute-start(bf16[2,128,1024]{2,1,0:T(8,128)(2,1)} %get-tuple-element.113), channel_id=1, source_target_pairs={{0,32},{16,48},{32,0},{48,16},{1,33},{17,49},{33,1},{49,17},{2,34}... | collective-permute-start | bytes 1572872 | tf_op jit(solution)/shard_map/ppermute | solution.py:607
  374.9 28.8 %collective-permute-start.22 = (bf16[2,128,1024]{2,1,0:T(8,128)(2,1)S(1)}, bf16[2,128,1024]{2,1,0:T(8,128)(2,1)}, u32[]{:S(2)}, u32[]{:S(2)}) collective-permute-start(bf16[2,128,1024]{2,1,0:T(8,128)(2,1)S(1)} %get-tuple-element.112), channel_id=1, source_target_pairs={{0,16},{16,32},{32,48},{48,0},{1,17},{17,33},{33,49},{49,1},{2,18}... | collective-permute-start | bytes 1572872 | tf_op jit(solution)/shard_map/ppermute | solution.py:607
  380.1 5.7 %collective-permute-start.18 = (bf16[16,8,512]{2,1,0:T(8,128)(2,1)S(1)}, bf16[16,8,512]{2,1,0:T(8,128)(2,1)}, u32[]{:S(2)}, u32[]{:S(2)}) collective-permute-start(bf16[16,8,512]{2,1,0:T(8,128)(2,1)S(1)} %get-tuple-element.126), channel_id=1, source_target_pairs={{0,2},{1,3},{2,0},{3,1},{4,6},{5,7},{6,4},{7,5},{8,10},{9,11},{10,... | collective-permute-start | bytes 393224 | tf_op jit(solution)/shard_map/ppermute | solution.py:607
  385.8 5.4 %collective-permute-start.19 = (bf16[16,8,512]{2,1,0:T(8,128)(2,1)S(1)}, bf16[16,8,512]{2,1,0:T(8,128)(2,1)S(1)}, u32[]{:S(2)}, u32[]{:S(2)}) collective-permute-start(bf16[16,8,512]{2,1,0:T(8,128)(2,1)S(1)} %get-tuple-element.125), channel_id=1, source_target_pairs={{0,3},{1,0},{2,1},{3,2},{4,7},{5,4},{6,5},{7,6},{8,11},{9,8},{10,9... | collective-permute-start | bytes 393224 | tf_op jit(solution)/shard_map/ppermute | solution.py:607
  407.5 11.9 %all-to-all-start.3 = ((bf16[16,8,512]{2,1,0:T(8,128)(2,1)}), bf16[16,8,512]{2,1,0:T(8,128)(2,1)S(1)}, u32[]{:S(2)}, u32[]{:S(2)}) async-start(bf16[16,8,512]{2,1,0:T(8,128)(2,1)} %fusion.23), calls=%async_computation.3 | async-start | bytes 262144 | tf_op jit(solution)/shard_map/all_to_all | solution.py:826
  413.5 9.2 %collective-permute-start.24 = (bf16[128,1024]{1,0:T(8,128)(2,1)S(1)}, bf16[128,1024]{1,0:T(8,128)(2,1)}, u32[]{:S(2)}, u32[]{:S(2)}) collective-permute-start(bf16[128,1024]{1,0:T(8,128)(2,1)S(1)} %slice_bitcast_fusion.4), channel_id=1, source_target_pairs={{0,64},{64,0},{1,65},{65,1},{2,66},{66,2},{3,67},{67,3},{4,68},{68... | collective-permute-start | bytes 786440 | tf_op jit(solution)/shard_map/ppermute | solution.py:607
  414.5 10.6 %collective-permute-start.25 = (bf16[128,1024]{1,0:T(8,128)(2,1)}, bf16[128,1024]{1,0:T(8,128)(2,1)S(1)}, u32[]{:S(2)}, u32[]{:S(2)}) collective-permute-start(bf16[128,1024]{1,0:T(8,128)(2,1)} %get-tuple-element.116), channel_id=1, source_target_pairs={{0,48},{16,0},{32,16},{48,32},{1,49},{17,1},{33,17},{49,33},{2,50}... | collective-permute-start | bytes 786440 | tf_op jit(solution)/shard_map/ppermute | solution.py:607
  417.1 8.8 %collective-permute-start.26 = (bf16[128,1024]{1,0:T(8,128)(2,1)}, bf16[128,1024]{1,0:T(8,128)(2,1)}, u32[]{:S(2)}, u32[]{:S(2)}) collective-permute-start(bf16[128,1024]{1,0:T(8,128)(2,1)} %get-tuple-element.118), channel_id=1, source_target_pairs={{0,32},{16,48},{32,0},{48,16},{1,33},{17,49},{33,1},{49,17},{2,34}... | collective-permute-start | bytes 786440 | tf_op jit(solution)/shard_map/ppermute | solution.py:607
  417.6 15.1 %collective-permute-start.27 = (bf16[128,1024]{1,0:T(8,128)(2,1)S(1)}, bf16[128,1024]{1,0:T(8,128)(2,1)}, u32[]{:S(2)}, u32[]{:S(2)}) collective-permute-start(bf16[128,1024]{1,0:T(8,128)(2,1)S(1)} %get-tuple-element.117), channel_id=1, source_target_pairs={{0,16},{16,32},{32,48},{48,0},{1,17},{17,33},{33,49},{49,1},{2,18}... | collective-permute-start | bytes 786440 | tf_op jit(solution)/shard_map/ppermute | solution.py:607
  436.5 9.9 %collective-permute-start.28 = (bf16[88,1024]{1,0:T(8,128)(2,1)S(1)}, bf16[88,1024]{1,0:T(8,128)(2,1)S(1)}, u32[]{:S(2)}, u32[]{:S(2)}) collective-permute-start(bf16[88,1024]{1,0:T(8,128)(2,1)S(1)} %get-tuple-element.121), channel_id=1, source_target_pairs={{0,4},{4,64},{64,68},{68,0},{1,5},{5,65},{65,69},{69,1},{2,6},{6,6... | collective-permute-start | bytes 540680 | tf_op jit(solution)/shard_map/ppermute | solution.py:601
  439.2 7.1 %collective-permute-start.29 = (bf16[88,1024]{1,0:T(8,128)(2,1)S(1)}, bf16[88,1024]{1,0:T(8,128)(2,1)S(1)}, u32[]{:S(2)}, u32[]{:S(2)}) collective-permute-start(bf16[88,1024]{1,0:T(8,128)(2,1)S(1)} %get-tuple-element.122), channel_id=1, source_target_pairs={{0,64},{4,68},{64,0},{68,4},{1,65},{5,69},{65,1},{69,5},{2,66},{6,... | collective-permute-start | bytes 540680 | tf_op jit(solution)/shard_map/ppermute | solution.py:601
  439.3 11.3 %collective-permute-start.30 = (bf16[88,1024]{1,0:T(8,128)(2,1)S(1)}, bf16[88,1024]{1,0:T(8,128)(2,1)S(1)}, u32[]{:S(2)}, u32[]{:S(2)}) collective-permute-start(bf16[88,1024]{1,0:T(8,128)(2,1)S(1)} %get-tuple-element.123), channel_id=1, source_target_pairs={{0,68},{4,0},{64,4},{68,64},{1,69},{5,1},{65,5},{69,65},{2,70},{6,... | collective-permute-start | bytes 540680 | tf_op jit(solution)/shard_map/ppermute | solution.py:601
  441.4 26.1 %copy-start.23 = (f32[40,1024]{1,0:T(8,128)S(1)}, f32[40,1024]{1,0:T(8,128)}, u32[]{:S(2)}) copy-start(f32[40,1024]{1,0:T(8,128)} %param.19) | copy-start | bytes 491524
  441.4 26.1 %copy-start.26 = (f32[40,1024]{1,0:T(8,128)S(1)}, f32[40,1024]{1,0:T(8,128)}, u32[]{:S(2)}) copy-start(f32[40,1024]{1,0:T(8,128)} %param.25) | copy-start | bytes 491524
  441.4 26.1 %copy-start.27 = (f32[40,1024]{1,0:T(8,128)S(1)}, f32[40,1024]{1,0:T(8,128)}, u32[]{:S(2)}) copy-start(f32[40,1024]{1,0:T(8,128)} %param.22) | copy-start | bytes 491524
  450.8 16.7 %collective-permute-start.31 = (f32[40,1024]{1,0:T(8,128)S(1)}, f32[40,1024]{1,0:T(8,128)S(1)}, u32[]{:S(2)}, u32[]{:S(2)}) collective-permute-start(f32[40,1024]{1,0:T(8,128)S(1)} %slice.200), channel_id=1, source_target_pairs={{0,0},{1,8},{2,16},{3,24},{4,1},{5,9},{6,17},{7,25},{8,4},{9,12},{... | collective-permute-start | bytes 491528 | tf_op jit(solution)/shard_map/ppermute | solution.py:843
  (23 other events, 142.8 us)
Sparse Core Ops, SparseCore 0:
  40.0 110.3 all-gather.3
  275.0 145.8 reduce-scatter.1

commit v3 on v2

--- a/solution.py
+++ b/solution.py
@@ -28,7 +28,8 @@
 SHARD = ("xl", "z")
 EVERY = CTX + SHARD
 AXIS_X = ("xh", "xl")
-AXIS_YZ = ("y", "z", "core")
+AXIS_YZ = ("y", "z")
+AXIS_CYZ = ("core", "y", "z")
 SIZES = {"xh": 2, "y": 4, "core": 2, "xl": 2, "z": 4}
 
 LOG2_E = 1.4426950408889634
@@ -369,33 +370,18 @@
 CHUNK_ROWS = 32
 N_CHUNKS = 3
 CHUNK = FF // N_CHUNKS
+Q_WIDTH = H_Q * HD
+HALF_OUT = (Q_WIDTH + FF) // 2
+HALF_MID = 512
+LEFT = HALF_OUT + HALF_MID
 
 
 def middle_kernel(
-    full_ref,
-    mixed_ref,
-    tok_ref,
-    cot_ref,
-    gain_ref,
-    shuffle_ref,
-    gate_ref,
-    up_ref,
-    out_ref,
-    dres_ref,
-    dob_ref,
-    feat_ref,
-    drb_ref,
-    grad_ref,
-    dgain_ref,
-    w_out,
-    resid,
-    mid_low,
-    grad_mid,
-    grad_up,
-    sems,
+    full_ref, mixed_ref, tok_ref, cot_ref, gain_ref, shuffle_ref, gate_ref, up_ref,
+    out_ref, dres_ref, dob_ref, left_ref, wide_ref, dgain_ref,
+    w_out, resid, mid_low, grad_mid, sems,
 ):
     step = pl.program_id(0)
-    q_width = H_Q * HD
     width = tok_ref.shape[1]
 
     def fetch(i):
@@ -406,51 +392,59 @@
         )
 
     n_fetch = full_ref.shape[0]
-    n_first = -(-q_width // OUT_ROWS)
+    n_first = -(-Q_WIDTH // OUT_ROWS)
 
     @pl.when(step == 0)
     def _():
         for i in range(n_fetch):
             fetch(i).start()
         for h in range(H_Q):
-            feat_ref[:, h * HD : (h + 1) * HD] = mixed_ref[h]
+            left_ref[0, :, h * HD : (h + 1) * HD] = mixed_ref[h]
         for i in range(n_first):
             fetch(i).wait()
-        residual = tok_ref[...].astype(f32) + dot_nn(feat_ref[:, :q_width], w_out[:q_width, :])
+        residual = tok_ref[...].astype(f32) + dot_nn(
+            left_ref[0, :, :Q_WIDTH], w_out[:Q_WIDTH, :]
+        )
         resid[...] = residual
         out_ref[...] = residual
         normed = rms_norm(residual, gain_ref[...]).astype(bf16)
-        mid_low[...] = dot_nn(normed, shuffle_ref[...]).astype(bf16)
+        low = dot_nn(normed, shuffle_ref[...]).astype(bf16)
+        mid_low[...] = low
+        for side in range(2):
+            left_ref[side, :, HALF_OUT:] = low[:, side * HALF_MID : (side + 1) * HALF_MID]
         grad_mid[...] = jnp.zeros_like(grad_mid)
         for i in range(n_first, n_fetch):
             fetch(i).wait()
 
-    @pl.when((step > 0) & (step < 2 * N_CHUNKS + 1) & (step % 2 == 1))
-    def _():
-        at = pl.multiple_of(q_width + ((step - 1) // 2) * CHUNK, CHUNK)
-        gate_w = gate_ref[...].reshape(width, CHUNK)
-        gate = dot_nn(mid_low[...], gate_w)
-        up = dot_nn(mid_low[...], up_ref[...].reshape(width, CHUNK))
-        sigmoid_gate = 1.0 / (1.0 + jnp.exp(-gate))
-        activated = gate * sigmoid_gate
-        hidden = (activated * up).astype(bf16)
-        feat_ref[:, pl.ds(at, CHUNK)] = hidden
-        down_w = w_out[pl.ds(at, CHUNK), :]
-        out_ref[...] += dot_nn(hidden, down_w)
-        grad_hidden = dot_nt(cot_ref[...], down_w)
-        grad_up[...] = (grad_hidden * activated).astype(bf16)
-        grad_gate = (
-            grad_hidden * up * sigmoid_gate * (1.0 + gate * (1.0 - sigmoid_gate))
-        ).astype(bf16)
-        grad_mid[...] += dot_nt(grad_gate, gate_w)
-        grad_ref[...] = dot_tn(mid_low[...], grad_gate).astype(bf16).reshape(grad_ref.shape)
-
-    @pl.when((step > 0) & (step < 2 * N_CHUNKS + 1) & (step % 2 == 0))
-    def _():
-        grad_mid[...] += dot_nt(grad_up[...], up_ref[...].reshape(width, CHUNK))
-        grad_ref[...] = dot_tn(mid_low[...], grad_up[...]).astype(bf16).reshape(grad_ref.shape)
-
-    @pl.when(step == 2 * N_CHUNKS + 1)
+    for f in range(N_CHUNKS):
+
+        @pl.when(step == f + 1)
+        def _(f=f):
+            at = Q_WIDTH + f * CHUNK
+            gate_w = gate_ref[...].reshape(width, CHUNK)
+            up_w = up_ref[...].reshape(width, CHUNK)
+            gate = dot_nn(mid_low[...], gate_w)
+            up = dot_nn(mid_low[...], up_w)
+            sigmoid_gate = 1.0 / (1.0 + jnp.exp(-gate))
+            activated = gate * sigmoid_gate
+            hidden = (activated * up).astype(bf16)
+            cut = min(max(HALF_OUT - at, 0), CHUNK)
+            if cut > 0:
+                left_ref[0, :, at : at + cut] = hidden[:, :cut]
+            if cut < CHUNK:
+                left_ref[1, :, at + cut - HALF_OUT : at + CHUNK - HALF_OUT] = hidden[:, cut:]
+            down_w = w_out[at : at + CHUNK, :]
+            out_ref[...] += dot_nn(hidden, down_w)
+            grad_hidden = dot_nt(cot_ref[...], down_w)
+            grad_up = (grad_hidden * activated).astype(bf16)
+            grad_gate = (
+                grad_hidden * up * sigmoid_gate * (1.0 + gate * (1.0 - sigmoid_gate))
+            ).astype(bf16)
+            wide_ref[:, f * CHUNK : (f + 1) * CHUNK] = grad_gate
+            wide_ref[:, FF + f * CHUNK : FF + (f + 1) * CHUNK] = grad_up
+            grad_mid[...] += dot_nt(grad_gate, gate_w) + dot_nt(grad_up, up_w)
+
+    @pl.when(step == N_CHUNKS + 1)
     def _():
         grad = dot_nt(grad_mid[...].astype(bf16), shuffle_ref[...])
         part, terms = rms_back(resid[...], gain_ref[...], grad)
@@ -458,7 +452,7 @@
         dres = cot_ref[...].astype(f32) + part
         dres_ref[...] = dres
         low = dres.astype(bf16)
-        drb_ref[...] = low
+        wide_ref[:, 2 * FF :] = low
         for c in range(4):
             piece = dot_nt(low, w_out[c * 4 * HD : (c + 1) * 4 * HD, :]).astype(bf16)
             for h in range(4):
@@ -469,21 +463,17 @@
     rows, width = tok.shape
     n_blocks = full.shape[0]
     first = OUT_ROWS // CHUNK_ROWS
-    q_width = H_Q * HD
 
     def chunk_of(i):
-        return jnp.clip((i - 1) // 2, 0, N_CHUNKS - 1)
-
-    def grad_at(i):
-        i = jnp.clip(i, 1, 2 * N_CHUNKS)
-        return (0, first + N_CHUNKS * ((i - 1) % 2) + (i - 1) // 2, 0)
+        return jnp.clip(i - 1, 0, N_CHUNKS - 1)
 
     def whole(shape):
         return pl.BlockSpec(shape, lambda i: (0,) * len(shape))
 
+    chunk = (n_blocks, CHUNK_ROWS, CHUNK)
     return pl.pallas_call(
         middle_kernel,
-        grid=(2 * N_CHUNKS + 2,),
+        grid=(N_CHUNKS + 2,),
         in_specs=[
             pl.BlockSpec(memory_space=pl.ANY),
             whole((H_Q, rows, HD)),
@@ -491,86 +481,103 @@
             whole((rows, width)),
             whole((1, width)),
             whole((width, width)),
-            pl.BlockSpec((n_blocks, CHUNK_ROWS, CHUNK), lambda i: (0, first + chunk_of(i), 0)),
-            pl.BlockSpec(
-                (n_blocks, CHUNK_ROWS, CHUNK), lambda i: (0, first + N_CHUNKS + chunk_of(i), 0)
-            ),
+            pl.BlockSpec(chunk, lambda i: (0, first + chunk_of(i), 0)),
+            pl.BlockSpec(chunk, lambda i: (0, first + N_CHUNKS + chunk_of(i), 0)),
         ],
         out_specs=[
             whole((rows, width)),
             whole((rows, width)),
             whole((H_Q, rows, HD)),
-            whole((rows, q_width + FF)),
-            whole((rows, width)),
-            pl.BlockSpec((n_blocks, CHUNK_ROWS, CHUNK), grad_at),
+            whole((2, rows, LEFT)),
+            whole((rows, 2 * FF + width)),
             whole((1, width)),
         ],
         out_shape=[
             jax.ShapeDtypeStruct((rows, width), f32),
             jax.ShapeDtypeStruct((rows, width), f32),
             jax.ShapeDtypeStruct((H_Q, rows, HD), bf16),
-            jax.ShapeDtypeStruct((rows, q_width + FF), bf16),
-            jax.ShapeDtypeStruct((rows, width), bf16),
-            jax.ShapeDtypeStruct(full.shape, bf16),
+            jax.ShapeDtypeStruct((2, rows, LEFT), bf16),
+            jax.ShapeDtypeStruct((rows, 2 * FF + width), bf16),
             jax.ShapeDtypeStruct((1, width), f32),
         ],
         scratch_shapes=[
-            pltpu.VMEM((q_width + FF, width), bf16),
+            pltpu.VMEM((Q_WIDTH + FF, width), bf16),
             pltpu.VMEM((rows, width), f32),
             pltpu.VMEM((rows, width), bf16),
             pltpu.VMEM((rows, width), f32),
-            pltpu.VMEM((rows, CHUNK), bf16),
             pltpu.SemaphoreType.DMA((n_blocks,)),
         ],
-        compiler_params=pltpu.CompilerParams(vmem_limit_bytes=VMEM_BYTES),
+        compiler_params=pltpu.CompilerParams(vmem_limit_bytes=BIG_VMEM_BYTES),
         name="middle",
     )(full, mixed, tok, cot, gain, shuffle, full, full)
 
 
-def grad_out_kernel(feat_ref, drb_ref, cot_ref, grads_ref, out_ref):
+def grad_ffn_kernel(left_a, left_b, right_a, right_b, out_ref):
+    total = dot_tn(left_a[...], right_a[...]) + dot_tn(left_b[...], right_b[...])
+    out_ref[...] = total.astype(bf16).reshape(out_ref.shape)
+
+
+def grad_ffn(lefts, wides, n_blocks):
+    rows = lefts[0].shape[0]
+    left = pl.BlockSpec((rows, HALF_MID), lambda i: (0, HALF_OUT // HALF_MID))
+    right = pl.BlockSpec((rows, CHUNK), lambda i: (0, i))
+    first = OUT_ROWS // CHUNK_ROWS
+    height = OUT_ROWS + 2 * N_CHUNKS * CHUNK_ROWS
+    return pl.pallas_call(
+        grad_ffn_kernel,
+        grid=(2 * N_CHUNKS,),
+        in_specs=[left, left, right, right],
+        out_specs=pl.BlockSpec((n_blocks, CHUNK_ROWS, CHUNK), lambda i: (0, first + i, 0)),
+        out_shape=jax.ShapeDtypeStruct((n_blocks, height, CHUNK), bf16),
+        compiler_params=pltpu.CompilerParams(vmem_limit_bytes=VMEM_BYTES),
+        name="grad_ffn",
+    )(*lefts, *wides)
+
+
+def grad_out_kernel(core_ref, left_a, left_b, drb_a, drb_b, cot_a, cot_b, grads_ref, out_ref):
     step = pl.program_id(0)
-    q_width = H_Q * HD
-    block = feat_ref.shape[1]
-    both = q_width // block
-    cut = q_width % block
+    block = left_a.shape[1]
+    both = Q_WIDTH // block
+    cut = Q_WIDTH % block
+    lower = core_ref[0] == 0
 
     def store(value):
         out_ref[...] = value.astype(bf16).reshape(out_ref.shape)
 
-    @pl.when(step < both)
+    @pl.when(lower & (step < both))
     def _():
-        store(dot_tn(feat_ref[...], drb_ref[...]))
-
-    @pl.when(step == both)
+        store(dot_tn(left_a[...], drb_a[...]) + dot_tn(left_b[...], drb_b[...]))
+
+    @pl.when(lower & (step == both))
     def _():
-        upper = dot_tn(feat_ref[:, :cut], drb_ref[...])
-        lower = dot_tn(feat_ref[:, cut:], cot_ref[...])
-        store(jnp.concatenate([upper, lower], axis=0))
-
-    @pl.when(step > both)
+        top = dot_tn(left_a[:, :cut], drb_a[...]) + dot_tn(left_b[:, :cut], drb_b[...])
+        rest = dot_tn(left_a[:, cut:], cot_a[...]) + dot_tn(left_b[:, cut:], cot_b[...])
+        store(jnp.concatenate([top, rest], axis=0))
+
+    @pl.when(core_ref[0] == 1)
     def _():
-        store(dot_tn(feat_ref[...], cot_ref[...]))
-
-
-def grad_out(feat, drb, cot, grads):
-    rows, n_features = feat.shape
-    width = drb.shape[1]
+        store(dot_tn(left_a[...], cot_a[...]) + dot_tn(left_b[...], cot_b[...]))
+
+
+def grad_out(core, lefts, wides, cots, grads):
+    rows, width = cots[0].shape
     blocks = 4
+    left = pl.BlockSpec((rows, blocks * OUT_ROWS), lambda i, core: (0, i))
+    drb = pl.BlockSpec((rows, width), lambda i, core: (0, 2 * N_CHUNKS))
+    cot = pl.BlockSpec((rows, width), lambda i, core: (0, 0))
     return pl.pallas_call(
         grad_out_kernel,
-        grid=(grads.shape[0] // blocks,),
-        in_specs=[
-            pl.BlockSpec((rows, blocks * OUT_ROWS), lambda i: (0, i)),
-            pl.BlockSpec((rows, width), lambda i: (0, 0)),
-            pl.BlockSpec((rows, width), lambda i: (0, 0)),
-            pl.BlockSpec(memory_space=pl.ANY),
-        ],
-        out_specs=pl.BlockSpec((blocks, OUT_ROWS, width), lambda i: (i, 0, 0)),
+        grid_spec=pltpu.PrefetchScalarGridSpec(
+            num_scalar_prefetch=1,
+            grid=(grads.shape[0] // blocks,),
+            in_specs=[left, left, drb, drb, cot, cot, pl.BlockSpec(memory_space=pl.ANY)],
+            out_specs=pl.BlockSpec((blocks, OUT_ROWS, width), lambda i, core: (i, 0, 0)),
+        ),
         out_shape=jax.ShapeDtypeStruct(grads.shape, bf16),
-        input_output_aliases={3: 0},
+        input_output_aliases={7: 0},
         compiler_params=pltpu.CompilerParams(vmem_limit_bytes=VMEM_BYTES),
         name="grad_out",
-    )(feat, drb, cot, grads)
+    )(core, *lefts, *wides, *cots, grads)
 
 
 def adam_step(master, first_old, second_old, gradient, rate):
@@ -585,7 +592,7 @@
 
 
 def gathered(x):
-    return lax.all_gather(x, AXIS_YZ, axis=0, tiled=True)
+    return lax.all_gather(x, AXIS_CYZ, axis=0, tiled=True)
 
 
 def sum_over_x(blocks):
@@ -669,18 +676,16 @@
 
 
 def gather_shard(x):
-    z = lax.axis_index("z")
     xl = lax.axis_index("xl")
-    ring = [x] + [shift(x, "z", -step) for step in (1, 2, 3)]
-    ring = lax.dynamic_slice_in_dim(jnp.stack(ring + ring[:3]), lax.rem(4 - z, 4), 4, 0)
+    ring = lax.all_gather(x, "z", axis=0, tiled=False)
     other = shift(ring, "xl", 1)
     return jnp.stack([jnp.where(xl == 0, ring, other), jnp.where(xl == 0, other, ring)])
 
 
 def natural_of_permuted(x):
     tail = x.shape[1:]
-    x = x.reshape((4, 4, 2, 2, 2) + tail)
-    x = x.transpose((3, 0, 2, 4, 1) + tuple(range(5, 5 + len(tail))))
+    x = x.reshape((2, 4, 4, 2, 2) + tail)
+    x = x.transpose((3, 1, 0, 4, 2) + tuple(range(5, 5 + len(tail))))
     return x.reshape((128,) + tail)
 
 
@@ -692,7 +697,7 @@
         core = (n // 8) % 2
         y = (n // 16) % 4
         xh = n // 64
-        pairs.append((n, (((y * 4 + z) * 2 + core) * 2 + xh) * 2 + xl))
+        pairs.append((n, (((core * 4 + y) * 4 + z) * 2 + xh) * 2 + xl))
     return pairs
 
 
@@ -747,7 +752,9 @@
     own_rest = jnp.concatenate([own_out, own_ffn], axis=0)
     own_rest = lax.all_gather(own_rest, AXIS_X, axis=0, tiled=False)
     own_head, own_rest, pair, ring = lax.optimization_barrier((own_head, own_rest, pair, ring))
-    head = gather_shard(lax.all_to_all(own_head, CTX, 0, 0, tiled=True))
+    head = lax.all_to_all(own_head, CTX, 0, 0, tiled=True)
+    head, segments, pad_mask = lax.optimization_barrier((head, segments, pad_mask))
+    head = gather_shard(head)
     head = head.transpose(2, 0, 1, 3, 4)
     gain_vals = head[:, :, :, 0, HEAD_COLS : HEAD_COLS + owned_gains].reshape(-1).astype(f32)
     w_head = head[..., :HEAD_COLS].reshape(width, HEAD_COLS)
@@ -797,13 +804,19 @@
     o_send, o_nat, l_inv = attend(klo, q, k, v, lens, rows)
     mixed = lax.all_to_all(o_send, CTX, 0, 0, tiled=True)
 
-    output, grad_residual, do_send, features, resid_low, grads, gain_two_terms = middle(
+    output, grad_residual, do_send, left, wide, gain_two_terms = middle(
         full, mixed, tokens[0], cotangent[0], gain_two.reshape(1, width), shuffle
     )
+    core = lax.axis_index("core")
+    lefts = (pick(left, core, 2, 0), shift(pick(left, core + 1, 2, 0), "core", 1))
+    wides = (wide, shift(wide, "core", 1))
+    cots = (cotangent[0], shift(cotangent[0], "core", 1))
+    grads = grad_ffn(lefts, wides, full.shape[0] // 2)
+    grads = grad_out(core.astype(jnp.int32).reshape(1), lefts, wides, cots, grads)
     do = lax.all_to_all(do_send, CTX, 0, 0, tiled=True)
-    grads = grad_out(features, resid_low, cotangent[0], grads)
     do, grads = lax.optimization_barrier((do, grads))
-    grads = lax.psum_scatter(grads, AXIS_YZ, scatter_dimension=0, tiled=True)[0]
+    grads = grads.reshape(-1, width)
+    grads = lax.psum_scatter(grads, AXIS_YZ, scatter_dimension=0, tiled=True)
 
     head_grads = attend_back(klo, q, k, v, do, o_nat, l_inv, lens)
     da_near, da_far, dw_head, gain_qk = project_back(

time: 482 us -> 454 us (0.942)
  the two profiles are of different devices: /device:TPU:103 before, /device:TPU:7 now
where the time goes in v3:
time: 454 us; the launch traced here: 447 us
  Pallas kernels  149 us (33%)
  waiting for transfers between devices  98.8 us (22%)
  starting transfers between devices  80.4 us (18%)
  other arithmetic  53.8 us (12%)
  local copies, waits for them, and re-layouts  27.4 us (6%)
  blocking collectives  22.2 us (5%)
  between operations  15.2 us (3%)
    ppermute x27, waiting for transfers between devices, shift(): return lax.ppermute(x, axis, [(i, (i + step) % n) for i in range(n)])  44.6 us
    ppermute x27, starting transfers between devices, shift(): return lax.ppermute(x, axis, [(i, (i + step) % n) for i in range(n)])  34.3 us
    pallas_call x1, Pallas kernels, attend_back(): pl.pallas_call(attend_back_kernel, in_specs=[pl.BlockSpec(memory_space=pl...  33.1 us
    pallas_call x1, Pallas kernels, project_back(): pl.pallas_call(project_back_kernel, grid_spec=pltpu.PrefetchScalarGridSpe...  31.7 us
    pallas_call x1, Pallas kernels, middle(): pl.pallas_call(middle_kernel, grid=(N_CHUNKS + 2,), in_specs=[pl.BlockSpe...  26 us
    pallas_call x1, Pallas kernels, attend(): pl.pallas_call(attend_kernel, in_specs=[pl.BlockSpec(memory_space=pltpu.S...  25.1 us
    all_to_all x1, waiting for transfers between devices, body(): head = lax.all_to_all(own_head, CTX, 0, 0, tiled=True)  21.6 us
    pallas_call x1, Pallas kernels, project(): pl.pallas_call(project_kernel, grid_spec=pltpu.PrefetchScalarGridSpec(num...  18.4 us
  transfers between devices with their start and end apart: 38, of which 15 were waited for; matrix products, arithmetic and copies ran while one was open for 16% of the time, Pallas kernels for 28%

profile of v3, /device:TPU:7, one launch (start us, length us, event | category | flops | bytes accessed | tf_op | source)
XLA Modules:
  0.0 447.0 jit_solution(1706663161031946772)
XLA Ops:
  9.7 2.6 collective-permute-start.3
  15.4 7.2 %collective-permute-start = (bf16[40,1024]{1,0:T(8,128)(2,1)S(1)}, bf16[40,1024]{1,0:T(8,128)(2,1)S(1)}, u32[]{:S(2)}, u32[]{:S(2)}) collective-permute-start(bf16[40,1024]{1,0:T(8,128)(2,1)S(1)} %convert_element_type.188), channel_id=1, source_target_pairs={{0,0},{4,1},{8,2},{12,3},{1,4},{5,5},{9,6},{13,7},{64,8},{68,9},{7... | collective-permute-start | bytes 245768 | tf_op jit(solution)/shard_map/ppermute | solution.py:749
  24.4 1.8 collective-permute-done
  26.2 11.7 %all-gather = bf16[352,1024]{1,0:T(8,128)(2,1)S(1)} all-gather(bf16[88,1024]{1,0:T(8,128)(2,1)S(1)} %pad_maximum_fusion.6), channel_id=2, replica_groups=mesh['xh'=2,'y'=4,'core'=2,'xl'=2,'z'=4] {'xh','xl'}, dimensions={0}, use_global_device_ids=true | all-gather | bytes 901120 | tf_op jit(solution)/shard_map/all_gather | solution.py:753
  41.8 1.7 collective-permute-start.7
  43.5 13.4 %all-to-all-start = ((bf16[16,8,512]{2,1,0:T(8,128)(2,1)}), bf16[16,8,512]{2,1,0:T(8,128)(2,1)S(1)}, u32[]{:S(2)}, u32[]{:S(2)}) async-start(bf16[16,8,512]{2,1,0:T(8,128)(2,1)} %maximum_bitcast_fusion.1), calls=%async_computation | async-start | bytes 262144 | tf_op jit(solution)/shard_map/all_to_all | solution.py:755
  59.1 21.6 %all-to-all-done = bf16[16,8,512]{2,1,0:T(8,128)(2,1)S(1)} async-done(((bf16[16,8,512]{2,1,0:T(8,128)(2,1)}), bf16[16,8,512]{2,1,0:T(8,128)(2,1)S(1)}, u32[]{:S(2)}, u32[]{:S(2)}) %all-to-all-start) | async-done | bytes 131104 | tf_op jit(solution)/shard_map/all_to_all | solution.py:755
  80.8 10.5 %all-gather.2 = bf16[64,8,512]{2,1,0:T(8,128)(2,1)S(1)} all-gather(bf16[16,8,512]{2,1,0:T(8,128)(2,1)S(1)} %all-to-all-done), channel_id=4, replica_groups=mesh['xh'=2,'y'=4,'core'=2,'xl'=2,'z'=4] {'z'}, dimensions={0}, use_global_device_ids=true | all-gather | bytes 655360 | tf_op jit(solution)/shard_map/all_gather | solution.py:680
  93.1 8.5 %convert_bitcast_fusion = (f32[4096]{0:T(1024)S(1)}, s32[32,128]{1,0:T(8,128)S(1)}) fusion(s32[]{:T(128)} %get-tuple-element.147, s32[]{:T(128)} %get-tuple-element.143, s32[]{:T(128)} %get-tuple-element.99, s32[]{:T(128)} %get-tuple-element.97, s32[]{:T(128)} %get-tuple-element.145, s32[]{:T(128)} %get-tuple-element.149, s32[]{:T(128)} %get-tuple-element.98, ...), kind=kLoop, calls=%fused_computation.103 | loop fusion | flops 126976 | bytes 49204 | tf_op jit(solution)/shard_map/convert_element_type | solution.py:793
  101.6 9.8 %fusion.11 = (f32[4096,64]{1,0:T(8,128)}, f32[4096,64]{1,0:T(8,128)}, f32[4096,64]{1,0:T(8,128)}) fusion(f32[64]{0:T(128)S(1)} %multiply_power_fusion, f32[4096]{0:T(1024)S(1)} %get-tuple-element.111), kind=kLoop, calls=%fused_computation.43 | loop fusion | flops 524288 | bytes 3162368 | tf_op jit(solution)/shard_map/neg | solution.py:797
  112.0 1.9 constant_dynamic-update-slice_fusion.2
  113.8 2.1 constant_dynamic-update-slice_fusion.1
  115.9 1.9 constant_dynamic-update-slice_fusion.x0
  117.8 3.7 collective-permute-start.9
  123.4 5.9 %pad_maximum_fusion = (f32[4096,128]{1,0:T(8,128)}, f32[4096,128]{1,0:T(8,128)}) fusion(f32[4096,64]{1,0:T(8,128)} %get-tuple-element.139, f32[4096,64]{1,0:T(8,128)S(1)} %copy-done.17, f32[4096,64]{1,0:T(8,128)S(1)} %copy-done.16), kind=kLoop, calls=%fused_computation.5 | loop fusion | flops 1048576 | bytes 7340032 | tf_op jit(solution)/shard_map/concatenate | solution.py:796
  132.1 18.4 %project.1 = (bf16[4096,128]{1,0:T(8,128)(2,1)S(1)}, bf16[4096,128]{1,0:T(8,128)(2,1)S(1)}, bf16[4096,128]{1,0:T(8,128)(2,1)S(1)}, f32[4096,128]{1,0:T(8,128)S(1...) custom-call(s32[32]{0:T(128)S(1)} %stack.140.place_ref, bf16[8,128,1024]{2,1,0:T(8,128)(2,1)} %constant_dynamic-update-slice_fusion.x0, ...), custom_call_target="tpu_custom_call" | custom-call | tf_op jit(solution)/shard_map/project/pallas_call | solution.py:139
  151.9 25.1 %attend.1 = (bf16[16,256,128]{2,1,0:T(8,128)(2,1)}, f32[4096,128]{1,0:T(8,128)}, f32[16,256]{1,0:T(8,128)S(1)}) custom-call(s32[16]{0:T(128)S(1)} %and_select_fusion.klo_ref, bf16[4096,128]{1,0:T(8,128)(2,1)S(1)} %get-tuple-element.56.q_ref, bf16[4096,128]{1,0:T(8,128)(2,1)S(1)} %get-tuple-element.57.k_ref, bf16[4096,128]{1,0:T(8,128)(2,1)S(1)} %get-tuple-element.58.v_ref, ...), custom_call_target="tpu_custom_call" | custom-call | tf_op jit(solution)/shard_map/attend/pallas_call | solution.py:297
  178.0 6.9 %all-to-all-start.1 = ((bf16[16,256,128]{2,1,0:T(8,128)(2,1)}), bf16[16,256,128]{2,1,0:T(8,128)(2,1)S(1)}, u32[]{:S(2)}, u32[]{:S(2)}) async-start(bf16[16,256,128]{2,1,0:T(8,128)(2,1)} %get-tuple-element.59), calls=%async_computation.1 | async-start | bytes 2097152 | tf_op jit(solution)/shard_map/all_to_all | solution.py:805
  185.0 1.7 fusion.shuffle_ref
  186.7 12.7 %all-to-all-done.1.mixed_ref = bf16[16,256,128]{2,1,0:T(8,128)(2,1)S(1)} async-done(((bf16[16,256,128]{2,1,0:T(8,128)(2,1)}), bf16[16,256,128]{2,1,0:T(8,128)(2,1)S(1)}, u32[]{:S(2)}, u32[]{:S(2)}) %all-to-all-start.1) | async-done | bytes 1048608 | tf_op jit(solution)/shard_map/all_to_all | solution.py:805
  200.4 26.0 %middle.1 = (f32[256,1024]{1,0:T(8,128)}, f32[256,1024]{1,0:T(8,128)}, bf16[16,256,128]{2,1,0:T(8,128)(2,1)}, bf16[2,256,3072]{2,1,0:T(8,128)(2,1)}, bf16[256,7168]{1,0:T(8,128)(2,1)}, /*index=5*/f32[1,1024]{1,0:T(1,128)}) custom-call(bf16[32,352,1024]{2,1,0:T(8,128)(2,1)} %bitcast.196, bf16[16,256,128]{2,1,0:T(8,128)(2,1)} %copy-done.18, ...), custom_call_target="tpu_custom_call" | custom-call | tf_op jit(solution)/shard_map/middle/pallas_call | solution.py:474
  227.4 3.2 dynamic-slice_bitcast_fusion
  230.7 7.3 %all-to-all-start.2 = ((bf16[16,256,128]{2,1,0:T(8,128)(2,1)}), bf16[16,256,128]{2,1,0:T(8,128)(2,1)}, u32[]{:S(2)}, u32[]{:S(2)}) async-start(bf16[16,256,128]{2,1,0:T(8,128)(2,1)} %get-tuple-element.62), calls=%async_computation.2 | async-start | bytes 2097152 | tf_op jit(solution)/shard_map/all_to_all | solution.py:816
  238.4 8.6 %grad_ffn.1.grads_ref = bf16[16,352,1024]{2,1,0:T(8,128)(2,1)} custom-call(bf16[256,3072]{1,0:T(8,128)(2,1)S(1)} %get-tuple-element.119.left_a, bf16[256,3072]{1,0:T(8,128)(2,1)S(1)} %collective-permute-done.12.left_b, bf16[256,7168]{1,0:T(8,128)(2,1)} %get-tuple-element.64.right_a.drb_a, bf16[256,7168]{1,0:T(8,128)(2,1)} %collective-permute-done.13.right_b.drb_b), custom_call_target="tpu_custom_call" | custom-call | tf_op jit(solution)/shard_map/grad_ffn/pallas_call | solution.py:526
  247.0 6.3 %grad_out.1 = bf16[16,352,1024]{2,1,0:T(8,128)(2,1)} custom-call(s32[1]{0:T(128)} %bitcast.67.core_ref, bf16[256,3072]{1,0:T(8,128)(2,1)S(1)} %get-tuple-element.119.left_a, bf16[256,3072]{1,0:T(8,128)(2,1)S(1)} %collective-permute-done.12.left_b, bf16[256,7168]{1,0:T(8,128)(2,1)} %get-tuple-element.64.right_a.drb_a, ...), custom_call_target="tpu_custom_call", output_to_operand_aliasing={{}: (7, {})} | custom-call | tf_op jit(solution)/shard_map/grad_out/pallas_call | solution.py:568
  255.2 33.1 %attend_back.1 = (f32[4096,128]{1,0:T(8,128)}, f32[4096,128]{1,0:T(8,128)}, f32[4096,128]{1,0:T(8,128)}) custom-call(s32[16]{0:T(128)S(1)} %and_select_fusion.klo_ref, bf16[4096,128]{1,0:T(8,128)(2,1)S(1)} %copy-done.1, bf16[4096,128]{1,0:T(8,128)(2,1)S(1)} %copy-done.3, bf16[4096,128]{1,0:T(8,128)(2,1)S(1)} %copy-done.5, ...), custom_call_target="tpu_custom_call" | custom-call | tf_op jit(solution)/shard_map/attend_back/pallas_call | solution.py:358
  288.3 31.7 %project_back.1 = (bf16[16,128,1024]{2,1,0:T(8,128)(2,1)}, bf16[16,128,1024]{2,1,0:T(8,128)(2,1)}, f32[1024,384]{1,0:T(8,128)}, f32[8,128]{1,0:T(8,128)}) custom-call(s32[32]{0:T(128)} %copy-done.8, bf16[8,128,1024]{2,1,0:T(8,128)(2,1)} %constant_dynamic-update-slice_fusion.x0, bf16[8,128,1024]{2,1,0:T(8,128)(2,1)} %copy-done.13, ...), custom_call_target="tpu_custom_call" | custom-call | tf_op jit(solution)/shard_map/project_back/pallas_call | solution.py:205
  321.0 1.9 fusion.2
  323.5 2.9 collective-permute-start.15
  326.4 12.2 %collective-permute-done.15 = bf16[16,4,8,512]{3,2,1,0:T(8,128)(2,1)S(1)} collective-permute-done((bf16[16,4,8,512]{3,2,1,0:T(8,128)(2,1)S(1)}, bf16[16,4,8,512]{3,2,1,0:T(8,128)(2,1)S(1)}, u32[]{:S(2)}, u32[]{:S(2)}) %collective-permute-start.15) | collective-permute-done | bytes 524320 | tf_op jit(solution)/shard_map/ppermute | solution.py:614
  338.8 5.7 %add_convert_fusion = bf16[16,128,1024]{2,1,0:T(8,128)(2,1)S(1)} fusion(bf16[16,128,1024]{2,1,0:T(8,128)(2,1)} %collective-permute-done.16, bf16[16,128,1024]{2,1,0:T(8,128)(2,1)} %get-tuple-element.77), kind=kLoop, calls=%fused_computation | loop fusion | flops 8388608 | bytes 12582912 | tf_op jit(solution)/shard_map/convert_element_type | solution.py:643
  345.6 3.4 collective-permute-start.23
  349.2 3.6 collective-permute-start.17
  355.4 2.3 collective-permute-start.18
  358.0 3.2 collective-permute-done.18
  362.6 3.0 collective-permute-done.19
  368.5 12.8 %collective-permute-done.22 = bf16[2,128,1024]{2,1,0:T(8,128)(2,1)} collective-permute-done((bf16[2,128,1024]{2,1,0:T(8,128)(2,1)S(1)}, bf16[2,128,1024]{2,1,0:T(8,128)(2,1)}, u32[]{:S(2)}, u32[]{:S(2)}) %collective-permute-start.22) | collective-permute-done | bytes 524320 | tf_op jit(solution)/shard_map/ppermute | solution.py:614
  382.8 2.0 add_convert_fusion.1
  384.8 5.5 %all-to-all-start.3 = ((bf16[16,8,512]{2,1,0:T(8,128)(2,1)}), bf16[16,8,512]{2,1,0:T(8,128)(2,1)S(1)}, u32[]{:S(2)}, u32[]{:S(2)}) async-start(bf16[16,8,512]{2,1,0:T(8,128)(2,1)} %fusion.23), calls=%async_computation.3 | async-start | bytes 262144 | tf_op jit(solution)/shard_map/all_to_all | solution.py:839
  391.4 2.6 collective-permute-start.25
  396.4 3.1 collective-permute-done.24
  400.6 2.1 collective-permute-done.26
  402.7 6.9 %collective-permute-done.27 = bf16[128,1024]{1,0:T(8,128)(2,1)} collective-permute-done((bf16[128,1024]{1,0:T(8,128)(2,1)S(1)}, bf16[128,1024]{1,0:T(8,128)(2,1)}, u32[]{:S(2)}, u32[]{:S(2)}) %collective-permute-start.27) | collective-permute-done | bytes 262176 | tf_op jit(solution)/shard_map/ppermute | solution.py:614
  413.4 3.2 collective-permute-start.28
  418.6 5.2 %collective-permute-done.28 = bf16[88,1024]{1,0:T(8,128)(2,1)S(1)} collective-permute-done((bf16[88,1024]{1,0:T(8,128)(2,1)S(1)}, bf16[88,1024]{1,0:T(8,128)(2,1)S(1)}, u32[]{:S(2)}, u32[]{:S(2)}) %collective-permute-start.28) | collective-permute-done | bytes 180256 | tf_op jit(solution)/shard_map/ppermute | solution.py:608
  423.8 4.1 collective-permute-done.30
  428.0 1.9 collective-permute-start.31
  431.1 8.0 %collective-permute-done.31 = f32[40,1024]{1,0:T(8,128)S(1)} collective-permute-done((f32[40,1024]{1,0:T(8,128)S(1)}, f32[40,1024]{1,0:T(8,128)S(1)}, u32[]{:S(2)}, u32[]{:S(2)}) %collective-permute-start.31) | collective-permute-done | bytes 163872 | tf_op jit(solution)/shard_map/ppermute | solution.py:856
  (205 shorter events, 50.9 us)
Async XLA Ops:
  7.2 192.3 %all-gather.5.cloned.1.call-start = ((), (), s32[]{:S(2)}) async-start(), calls=%async_computation.6 | async-start | bytes 23789568 | tf_op jit(solution)/shard_map/all_gather | solution.py:595
  8.3 29.7 %collective-permute-start.2 = (bf16[1,128,1024]{2,1,0:T(8,128)(2,1)S(1)}, bf16[1,128,1024]{2,1,0:T(8,128)(2,1)S(1)}, u32[]{:S(2)}, u32[]{:S(2)}) collective-permute-start(bf16[1,128,1024]{2,1,0:T(8,128)(2,1)S(1)} %get-tuple-element.133), channel_id=1, source_target_pairs={{0,16},{16,32},{32,48},{48,0},{1,17},{17,33},{33,49},{49,1},{2,18}... | collective-permute-start | bytes 786440 | tf_op jit(solution)/shard_map/ppermute | solution.py:614
  9.7 28.4 %collective-permute-start.3 = (bf16[1,128,1024]{2,1,0:T(8,128)(2,1)S(1)}, bf16[1,128,1024]{2,1,0:T(8,128)(2,1)S(1)}, u32[]{:S(2)}, u32[]{:S(2)}) collective-permute-start(bf16[1,128,1024]{2,1,0:T(8,128)(2,1)S(1)} %get-tuple-element.133), channel_id=1, source_target_pairs={{0,32},{16,48},{32,0},{48,16},{1,33},{17,49},{33,1},{49,17},{2,34}... | collective-permute-start | bytes 786440 | tf_op jit(solution)/shard_map/ppermute | solution.py:614
  12.3 25.8 %collective-permute-start.4 = (bf16[1,128,1024]{2,1,0:T(8,128)(2,1)S(1)}, bf16[1,128,1024]{2,1,0:T(8,128)(2,1)S(1)}, u32[]{:S(2)}, u32[]{:S(2)}) collective-permute-start(bf16[1,128,1024]{2,1,0:T(8,128)(2,1)S(1)} %get-tuple-element.133), channel_id=1, source_target_pairs={{0,48},{16,0},{32,16},{48,32},{1,49},{17,1},{33,17},{49,33},{2,50}... | collective-permute-start | bytes 786440 | tf_op jit(solution)/shard_map/ppermute | solution.py:614
  13.4 24.6 %collective-permute-start.1 = (bf16[1,128,1024]{2,1,0:T(8,128)(2,1)S(1)}, bf16[1,128,1024]{2,1,0:T(8,128)(2,1)S(1)}, u32[]{:S(2)}, u32[]{:S(2)}) collective-permute-start(bf16[1,128,1024]{2,1,0:T(8,128)(2,1)S(1)} %get-tuple-element.134), channel_id=1, source_target_pairs={{0,64},{64,0},{1,65},{65,1},{2,66},{66,2},{3,67},{67,3},{4,68},{68... | collective-permute-start | bytes 786440 | tf_op jit(solution)/shard_map/ppermute | solution.py:614
  15.4 10.8 %collective-permute-start = (bf16[40,1024]{1,0:T(8,128)(2,1)S(1)}, bf16[40,1024]{1,0:T(8,128)(2,1)S(1)}, u32[]{:S(2)}, u32[]{:S(2)}) collective-permute-start(bf16[40,1024]{1,0:T(8,128)(2,1)S(1)} %convert_element_type.188), channel_id=1, source_target_pairs={{0,0},{4,1},{8,2},{12,3},{1,4},{5,5},{9,6},{13,7},{64,8},{68,9},{7... | collective-permute-start | bytes 245768 | tf_op jit(solution)/shard_map/ppermute | solution.py:749
  40.2 40.6 %copy-start.26 = (s32[1,4096]{1,0:T(1,128)S(1)}, s32[1,4096]{1,0:T(1,128)}, u32[]{:S(2)}) copy-start(s32[1,4096]{1,0:T(1,128)} %param.16) | copy-start | bytes 49156
  40.5 91.6 %copy-start.8 = (s32[32]{0:T(128)}, s32[32]{0:T(128)S(1)}, u32[]{:S(2)}) copy-start(s32[32]{0:T(128)S(1)} %stack.140.place_ref) | copy-start | bytes 388
  40.6 71.4 %collective-permute-start.5 = (bf16[2,128,1024]{2,1,0:T(8,128)(2,1)S(1)}, bf16[2,128,1024]{2,1,0:T(8,128)(2,1)}, u32[]{:S(2)}, u32[]{:S(2)}) collective-permute-start(bf16[2,128,1024]{2,1,0:T(8,128)(2,1)S(1)} %pad_maximum_fusion.4), channel_id=1, source_target_pairs={{0,16},{16,32},{32,48},{48,0},{1,17},{17,33},{33,49},{49,1},{2,18}... | collective-permute-start | bytes 1572872 | tf_op jit(solution)/shard_map/ppermute | solution.py:614
  41.0 72.8 %collective-permute-start.6 = (bf16[2,128,1024]{2,1,0:T(8,128)(2,1)S(1)}, bf16[2,128,1024]{2,1,0:T(8,128)(2,1)}, u32[]{:S(2)}, u32[]{:S(2)}) collective-permute-start(bf16[2,128,1024]{2,1,0:T(8,128)(2,1)S(1)} %pad_maximum_fusion.4), channel_id=1, source_target_pairs={{0,32},{16,48},{32,0},{48,16},{1,33},{17,49},{33,1},{49,17},{2,34}... | collective-permute-start | bytes 1572872 | tf_op jit(solution)/shard_map/ppermute | solution.py:614
  41.8 74.1 %collective-permute-start.7 = (bf16[2,128,1024]{2,1,0:T(8,128)(2,1)S(1)}, bf16[2,128,1024]{2,1,0:T(8,128)(2,1)}, u32[]{:S(2)}, u32[]{:S(2)}) collective-permute-start(bf16[2,128,1024]{2,1,0:T(8,128)(2,1)S(1)} %pad_maximum_fusion.4), channel_id=1, source_target_pairs={{0,48},{16,0},{32,16},{48,32},{1,49},{17,1},{33,17},{49,33},{2,50}... | collective-permute-start | bytes 1572872 | tf_op jit(solution)/shard_map/ppermute | solution.py:614
  43.5 37.2 %all-to-all-start = ((bf16[16,8,512]{2,1,0:T(8,128)(2,1)}), bf16[16,8,512]{2,1,0:T(8,128)(2,1)S(1)}, u32[]{:S(2)}, u32[]{:S(2)}) async-start(bf16[16,8,512]{2,1,0:T(8,128)(2,1)} %maximum_bitcast_fusion.1), calls=%async_computation | async-start | bytes 262144 | tf_op jit(solution)/shard_map/all_to_all | solution.py:755
  56.9 64.6 %collective-permute-start.8 = (bf16[4,128,1024]{2,1,0:T(8,128)(2,1)}, bf16[4,128,1024]{2,1,0:T(8,128)(2,1)}, u32[]{:S(2)}, u32[]{:S(2)}) collective-permute-start(bf16[4,128,1024]{2,1,0:T(8,128)(2,1)} %pad_maximum_fusion.2), channel_id=1, source_target_pairs={{0,64},{64,0},{1,65},{65,1},{2,66},{66,2},{3,67},{67,3},{4,68},{68... | collective-permute-start | bytes 3145736 | tf_op jit(solution)/shard_map/ppermute | solution.py:614
  92.2 37.1 %collective-permute-start.11 = (bf16[4,16,8,512]{3,1,2,0:T(8,128)(2,1)}, bf16[4,16,8,512]{3,1,2,0:T(8,128)(2,1)}, u32[]{:S(2)}, u32[]{:S(2)}) collective-permute-start(bf16[4,16,8,512]{3,1,2,0:T(8,128)(2,1)} %copy.64), channel_id=1, source_target_pairs={{0,4},{4,0},{1,5},{5,1},{2,6},{6,2},{3,7},{7,3},{8,12},{12,8},{9,1... | collective-permute-start | bytes 1572872 | tf_op jit(solution)/shard_map/ppermute | solution.py:614
  117.8 14.3 %collective-permute-start.9 = (bf16[8,128,1024]{2,1,0:T(8,128)(2,1)}, bf16[8,128,1024]{2,1,0:T(8,128)(2,1)}, u32[]{:S(2)}, u32[]{:S(2)}) collective-permute-start(bf16[8,128,1024]{2,1,0:T(8,128)(2,1)} %constant_dynamic-update-slice_fusion.x0), channel_id=1, source_target_pairs={{0,8},{8,0},{1,9},{9,1},{2,10},{10,2},{3,11},{11,3},{4,12},{12,4},... | collective-permute-start | bytes 6291464 | tf_op jit(solution)/shard_map/ppermute | solution.py:614
  122.8 9.3 %collective-permute-start.10 = (bf16[8,128,1024]{2,1,0:T(8,128)(2,1)S(1)}, bf16[8,128,1024]{2,1,0:T(8,128)(2,1)}, u32[]{:S(2)}, u32[]{:S(2)}) collective-permute-start(bf16[8,128,1024]{2,1,0:T(8,128)(2,1)S(1)} %constant_dynamic-update-slice_fusion.4.x1), channel_id=1, source_target_pairs={{0,8},{8,0},{1,9},{9,1},{2,10},{10,2},{3,11},{11,3},{4,12},{12,4},... | collective-permute-start | bytes 6291464 | tf_op jit(solution)/shard_map/ppermute | solution.py:614
  131.1 19.4 %copy-start.9 = (f32[1,128]{1,0:T(1,128)}, f32[1,128]{1,0:T(1,128)S(1)}, u32[]{:S(2)}) copy-start(f32[1,128]{1,0:T(1,128)S(1)} %get-tuple-element.155.gk_ref) | copy-start | bytes 1540
  151.9 25.1 %copy-start.2 = (bf16[4096,128]{1,0:T(8,128)(2,1)}, bf16[4096,128]{1,0:T(8,128)(2,1)S(1)}, u32[]{:S(2)}) copy-start(bf16[4096,128]{1,0:T(8,128)(2,1)S(1)} %get-tuple-element.57.k_ref) | copy-start | bytes 3145732
  151.9 25.1 %copy-start.4 = (bf16[4096,128]{1,0:T(8,128)(2,1)}, bf16[4096,128]{1,0:T(8,128)(2,1)S(1)}, u32[]{:S(2)}) copy-start(bf16[4096,128]{1,0:T(8,128)(2,1)S(1)} %get-tuple-element.58.v_ref) | copy-start | bytes 3145732
  178.0 21.5 %all-to-all-start.1 = ((bf16[16,256,128]{2,1,0:T(8,128)(2,1)}), bf16[16,256,128]{2,1,0:T(8,128)(2,1)S(1)}, u32[]{:S(2)}, u32[]{:S(2)}) async-start(bf16[16,256,128]{2,1,0:T(8,128)(2,1)} %get-tuple-element.59), calls=%async_computation.1 | async-start | bytes 2097152 | tf_op jit(solution)/shard_map/all_to_all | solution.py:805
  226.4 12.0 %collective-permute-start.13 = (bf16[256,7168]{1,0:T(8,128)(2,1)}, bf16[256,7168]{1,0:T(8,128)(2,1)}, u32[]{:S(2)}, u32[]{:S(2)}) collective-permute-start(bf16[256,7168]{1,0:T(8,128)(2,1)} %get-tuple-element.64.right_a.drb_a), channel_id=1, source_target_pairs={{0,8},{8,0},{1,9},{9,1},{2,10},{10,2},{3,11},{11,3},{4,12},{12,4},... | collective-permute-start | bytes 11010056 | tf_op jit(solution)/shard_map/ppermute | solution.py:614
  230.6 7.8 %collective-permute-start.12 = (bf16[256,3072]{1,0:T(8,128)(2,1)}, bf16[256,3072]{1,0:T(8,128)(2,1)S(1)}, u32[]{:S(2)}, u32[]{:S(2)}) collective-permute-start(bf16[256,3072]{1,0:T(8,128)(2,1)} %get-tuple-element.118), channel_id=1, source_target_pairs={{0,8},{8,0},{1,9},{9,1},{2,10},{10,2},{3,11},{11,3},{4,12},{12,4},... | collective-permute-start | bytes 4718600 | tf_op jit(solution)/shard_map/ppermute | solution.py:614
  230.7 22.7 %all-to-all-start.2 = ((bf16[16,256,128]{2,1,0:T(8,128)(2,1)}), bf16[16,256,128]{2,1,0:T(8,128)(2,1)}, u32[]{:S(2)}, u32[]{:S(2)}) async-start(bf16[16,256,128]{2,1,0:T(8,128)(2,1)} %get-tuple-element.62), calls=%async_computation.2 | async-start | bytes 2097152 | tf_op jit(solution)/shard_map/all_to_all | solution.py:816
  237.9 173.2 %reduce-scatter.2.cloned.1.call-start = ((), (), s32[]{:S(2)}) async-start(), calls=%async_computation.5 | async-start | bytes 12255232 | tf_op jit(solution)/shard_map/reduce_scatter | solution.py:819
  238.0 9.0 %collective-permute-start.14 = (bf16[256,1024]{1,0:T(8,128)(2,1)}, bf16[256,1024]{1,0:T(8,128)(2,1)S(1)}, u32[]{:S(2)}, u32[]{:S(2)}) collective-permute-start(bf16[256,1024]{1,0:T(8,128)(2,1)} %bitcast.194), channel_id=1, source_target_pairs={{0,8},{8,0},{1,9},{9,1},{2,10},{10,2},{3,11},{11,3},{4,12},{12,4},... | collective-permute-start | bytes 1572872 | tf_op jit(solution)/shard_map/ppermute | solution.py:614
  288.3 32.0 %copy-start.28 = (f32[1,1024]{1,0:T(1,128)S(1)}, f32[1,1024]{1,0:T(1,128)}, u32[]{:S(2)}) copy-start(f32[1,1024]{1,0:T(1,128)} %get-tuple-element.75) | copy-start | bytes 12292
  288.3 32.7 %copy-start.15 = (bf16[16,2,4,8,384]{4,3,2,1,0:T(8,128)(2,1)S(1)}, bf16[16,2,4,8,384]{4,3,2,1,0:T(8,128)(2,1)}, u32[]{:S(2)}) copy-start(bf16[16,2,4,8,384]{4,3,2,1,0:T(8,128)(2,1)} %copy-done.14) | copy-start | bytes 2359300
  320.0 18.8 %collective-permute-start.16 = (bf16[16,128,1024]{2,1,0:T(8,128)(2,1)}, bf16[16,128,1024]{2,1,0:T(8,128)(2,1)}, u32[]{:S(2)}, u32[]{:S(2)}) collective-permute-start(bf16[16,128,1024]{2,1,0:T(8,128)(2,1)} %get-tuple-element.78), channel_id=1, source_target_pairs={{0,8},{8,0},{1,9},{9,1},{2,10},{10,2},{3,11},{11,3},{4,12},{12,4},... | collective-permute-start | bytes 12582920 | tf_op jit(solution)/shard_map/ppermute | solution.py:614
  323.5 15.1 %collective-permute-start.15 = (bf16[16,4,8,512]{3,2,1,0:T(8,128)(2,1)S(1)}, bf16[16,4,8,512]{3,2,1,0:T(8,128)(2,1)S(1)}, u32[]{:S(2)}, u32[]{:S(2)}) collective-permute-start(bf16[16,4,8,512]{3,2,1,0:T(8,128)(2,1)S(1)} %fusion.13), channel_id=1, source_target_pairs={{0,4},{4,0},{1,5},{5,1},{2,6},{6,2},{3,7},{7,3},{8,12},{12,8},{9,1... | collective-permute-start | bytes 1572872 | tf_op jit(solution)/shard_map/ppermute | solution.py:614
  345.6 37.2 %collective-permute-start.23 = (bf16[4,128,1024]{2,1,0:T(8,128)(2,1)}, bf16[4,128,1024]{2,1,0:T(8,128)(2,1)}, u32[]{:S(2)}, u32[]{:S(2)}) collective-permute-start(bf16[4,128,1024]{2,1,0:T(8,128)(2,1)} %slice.163), channel_id=1, source_target_pairs={{0,64},{64,0},{1,65},{65,1},{2,66},{66,2},{3,67},{67,3},{4,68},{68... | collective-permute-start | bytes 3145736 | tf_op jit(solution)/shard_map/ppermute | solution.py:614
  349.2 6.2 %collective-permute-start.17 = (bf16[16,8,512]{2,1,0:T(8,128)(2,1)S(1)}, bf16[16,8,512]{2,1,0:T(8,128)(2,1)S(1)}, u32[]{:S(2)}, u32[]{:S(2)}) collective-permute-start(bf16[16,8,512]{2,1,0:T(8,128)(2,1)S(1)} %get-tuple-element.130), channel_id=1, source_target_pairs={{0,1},{1,2},{2,3},{3,0},{4,5},{5,6},{6,7},{7,4},{8,9},{9,10},{10,1... | collective-permute-start | bytes 393224 | tf_op jit(solution)/shard_map/ppermute | solution.py:614
  353.9 13.3 %collective-permute-start.20 = (bf16[2,128,1024]{2,1,0:T(8,128)(2,1)}, bf16[2,128,1024]{2,1,0:T(8,128)(2,1)S(1)}, u32[]{:S(2)}, u32[]{:S(2)}) collective-permute-start(bf16[2,128,1024]{2,1,0:T(8,128)(2,1)} %get-tuple-element.115), channel_id=1, source_target_pairs={{0,48},{16,0},{32,16},{48,32},{1,49},{17,1},{33,17},{49,33},{2,50}... | collective-permute-start | bytes 1572872 | tf_op jit(solution)/shard_map/ppermute | solution.py:614
  354.9 13.6 %collective-permute-start.21 = (bf16[2,128,1024]{2,1,0:T(8,128)(2,1)}, bf16[2,128,1024]{2,1,0:T(8,128)(2,1)S(1)}, u32[]{:S(2)}, u32[]{:S(2)}) collective-permute-start(bf16[2,128,1024]{2,1,0:T(8,128)(2,1)} %get-tuple-element.117), channel_id=1, source_target_pairs={{0,32},{16,48},{32,0},{48,16},{1,33},{17,49},{33,1},{49,17},{2,34}... | collective-permute-start | bytes 1572872 | tf_op jit(solution)/shard_map/ppermute | solution.py:614
  354.9 26.4 %collective-permute-start.22 = (bf16[2,128,1024]{2,1,0:T(8,128)(2,1)S(1)}, bf16[2,128,1024]{2,1,0:T(8,128)(2,1)}, u32[]{:S(2)}, u32[]{:S(2)}) collective-permute-start(bf16[2,128,1024]{2,1,0:T(8,128)(2,1)S(1)} %get-tuple-element.116), channel_id=1, source_target_pairs={{0,16},{16,32},{32,48},{48,0},{1,17},{17,33},{33,49},{49,1},{2,18}... | collective-permute-start | bytes 1572872 | tf_op jit(solution)/shard_map/ppermute | solution.py:614
  355.4 5.7 %collective-permute-start.18 = (bf16[16,8,512]{2,1,0:T(8,128)(2,1)S(1)}, bf16[16,8,512]{2,1,0:T(8,128)(2,1)}, u32[]{:S(2)}, u32[]{:S(2)}) collective-permute-start(bf16[16,8,512]{2,1,0:T(8,128)(2,1)S(1)} %get-tuple-element.132), channel_id=1, source_target_pairs={{0,2},{1,3},{2,0},{3,1},{4,6},{5,7},{6,4},{7,5},{8,10},{9,11},{10,... | collective-permute-start | bytes 393224 | tf_op jit(solution)/shard_map/ppermute | solution.py:614
  361.2 4.5 %collective-permute-start.19 = (bf16[16,8,512]{2,1,0:T(8,128)(2,1)S(1)}, bf16[16,8,512]{2,1,0:T(8,128)(2,1)S(1)}, u32[]{:S(2)}, u32[]{:S(2)}) collective-permute-start(bf16[16,8,512]{2,1,0:T(8,128)(2,1)S(1)} %get-tuple-element.131), channel_id=1, source_target_pairs={{0,3},{1,0},{2,1},{3,2},{4,7},{5,4},{6,5},{7,6},{8,11},{9,8},{10,9... | collective-permute-start | bytes 393224 | tf_op jit(solution)/shard_map/ppermute | solution.py:614
  384.8 11.0 %all-to-all-start.3 = ((bf16[16,8,512]{2,1,0:T(8,128)(2,1)}), bf16[16,8,512]{2,1,0:T(8,128)(2,1)S(1)}, u32[]{:S(2)}, u32[]{:S(2)}) async-start(bf16[16,8,512]{2,1,0:T(8,128)(2,1)} %fusion.23), calls=%async_computation.3 | async-start | bytes 262144 | tf_op jit(solution)/shard_map/all_to_all | solution.py:839
  390.4 9.2 %collective-permute-start.24 = (bf16[128,1024]{1,0:T(8,128)(2,1)S(1)}, bf16[128,1024]{1,0:T(8,128)(2,1)}, u32[]{:S(2)}, u32[]{:S(2)}) collective-permute-start(bf16[128,1024]{1,0:T(8,128)(2,1)S(1)} %slice_bitcast_fusion.4), channel_id=1, source_target_pairs={{0,64},{64,0},{1,65},{65,1},{2,66},{66,2},{3,67},{67,3},{4,68},{68... | collective-permute-start | bytes 786440 | tf_op jit(solution)/shard_map/ppermute | solution.py:614
  391.4 9.2 %collective-permute-start.25 = (bf16[128,1024]{1,0:T(8,128)(2,1)}, bf16[128,1024]{1,0:T(8,128)(2,1)S(1)}, u32[]{:S(2)}, u32[]{:S(2)}) collective-permute-start(bf16[128,1024]{1,0:T(8,128)(2,1)} %get-tuple-element.122), channel_id=1, source_target_pairs={{0,48},{16,0},{32,16},{48,32},{1,49},{17,1},{33,17},{49,33},{2,50}... | collective-permute-start | bytes 786440 | tf_op jit(solution)/shard_map/ppermute | solution.py:614
  394.0 8.8 %collective-permute-start.26 = (bf16[128,1024]{1,0:T(8,128)(2,1)}, bf16[128,1024]{1,0:T(8,128)(2,1)}, u32[]{:S(2)}, u32[]{:S(2)}) collective-permute-start(bf16[128,1024]{1,0:T(8,128)(2,1)} %get-tuple-element.124), channel_id=1, source_target_pairs={{0,32},{16,48},{32,0},{48,16},{1,33},{17,49},{33,1},{49,17},{2,34}... | collective-permute-start | bytes 786440 | tf_op jit(solution)/shard_map/ppermute | solution.py:614
  394.5 15.1 %collective-permute-start.27 = (bf16[128,1024]{1,0:T(8,128)(2,1)S(1)}, bf16[128,1024]{1,0:T(8,128)(2,1)}, u32[]{:S(2)}, u32[]{:S(2)}) collective-permute-start(bf16[128,1024]{1,0:T(8,128)(2,1)S(1)} %get-tuple-element.123), channel_id=1, source_target_pairs={{0,16},{16,32},{32,48},{48,0},{1,17},{17,33},{33,49},{49,1},{2,18}... | collective-permute-start | bytes 786440 | tf_op jit(solution)/shard_map/ppermute | solution.py:614
  413.4 10.4 %collective-permute-start.28 = (bf16[88,1024]{1,0:T(8,128)(2,1)S(1)}, bf16[88,1024]{1,0:T(8,128)(2,1)S(1)}, u32[]{:S(2)}, u32[]{:S(2)}) collective-permute-start(bf16[88,1024]{1,0:T(8,128)(2,1)S(1)} %get-tuple-element.127), channel_id=1, source_target_pairs={{0,4},{4,64},{64,68},{68,0},{1,5},{5,65},{65,69},{69,1},{2,6},{6,6... | collective-permute-start | bytes 540680 | tf_op jit(solution)/shard_map/ppermute | solution.py:608
  416.6 7.2 %collective-permute-start.29 = (bf16[88,1024]{1,0:T(8,128)(2,1)S(1)}, bf16[88,1024]{1,0:T(8,128)(2,1)S(1)}, u32[]{:S(2)}, u32[]{:S(2)}) collective-permute-start(bf16[88,1024]{1,0:T(8,128)(2,1)S(1)} %get-tuple-element.128), channel_id=1, source_target_pairs={{0,64},{4,68},{64,0},{68,4},{1,65},{5,69},{65,1},{69,5},{2,66},{6,... | collective-permute-start | bytes 540680 | tf_op jit(solution)/shard_map/ppermute | solution.py:608
  416.6 11.2 %collective-permute-start.30 = (bf16[88,1024]{1,0:T(8,128)(2,1)S(1)}, bf16[88,1024]{1,0:T(8,128)(2,1)S(1)}, u32[]{:S(2)}, u32[]{:S(2)}) collective-permute-start(bf16[88,1024]{1,0:T(8,128)(2,1)S(1)} %get-tuple-element.129), channel_id=1, source_target_pairs={{0,68},{4,0},{64,4},{68,64},{1,69},{5,1},{65,5},{69,65},{2,70},{6,... | collective-permute-start | bytes 540680 | tf_op jit(solution)/shard_map/ppermute | solution.py:608
  418.6 20.6 %copy-start.21 = (f32[40,1024]{1,0:T(8,128)S(1)}, f32[40,1024]{1,0:T(8,128)}, u32[]{:S(2)}) copy-start(f32[40,1024]{1,0:T(8,128)} %param.19) | copy-start | bytes 491524
  418.6 20.6 %copy-start.24 = (f32[40,1024]{1,0:T(8,128)S(1)}, f32[40,1024]{1,0:T(8,128)}, u32[]{:S(2)}) copy-start(f32[40,1024]{1,0:T(8,128)} %param.25) | copy-start | bytes 491524
  418.6 20.6 %copy-start.25 = (f32[40,1024]{1,0:T(8,128)S(1)}, f32[40,1024]{1,0:T(8,128)}, u32[]{:S(2)}) copy-start(f32[40,1024]{1,0:T(8,128)} %param.22) | copy-start | bytes 491524
  428.0 11.1 %collective-permute-start.31 = (f32[40,1024]{1,0:T(8,128)S(1)}, f32[40,1024]{1,0:T(8,128)S(1)}, u32[]{:S(2)}, u32[]{:S(2)}) collective-permute-start(f32[40,1024]{1,0:T(8,128)S(1)} %slice.198), channel_id=1, source_target_pairs={{0,0},{1,4},{2,8},{3,12},{4,1},{5,5},{6,9},{7,13},{8,64},{9,68},{1... | collective-permute-start | bytes 491528 | tf_op jit(solution)/shard_map/ppermute | solution.py:856
  (22 other events, 171.9 us)
Sparse Core Ops, SparseCore 0:
  40.3 101.5 all-gather.4
  253.5 93.9 reduce-scatter.1

commit v4 on v3

--- a/solution.py
+++ b/solution.py
@@ -34,8 +34,9 @@
 
 LOG2_E = 1.4426950408889634
 SCORE_SCALE = 1.0 / math.sqrt(HD)
-BQ = 256
+BQ = 512
 BK = 512
+SUB = 256
 VMEM_BYTES = 48 * 1024 * 1024
 BIG_VMEM_BYTES = 60 * 1024 * 1024
 
@@ -92,6 +93,15 @@
 
 def rows_of(place_ref, step, i):
     return pl.ds(pl.multiple_of(place_ref[step * STEP_BLOCKS + i] * HALF, HALF), HALF)
+
+
+def head_mean(x):
+    return lax.dot_general(
+        x.astype(bf16),
+        jnp.full((HD, HD), 1.0 / HD, bf16),
+        (((1,), (0,)), ((), ())),
+        preferred_element_type=f32,
+    )
 
 
 def project_kernel(
@@ -111,14 +121,14 @@
             sin = sin_ref[at, :]
 
             def roped(raw, gain, cos=cos, sin=sin):
-                normed = rms_norm(raw, gain)
+                normed = raw * lax.rsqrt(head_mean(raw * raw) + NORM_EPS) * gain
                 return normed * cos + pltpu.roll(normed, HD // 2, 1) * sin
 
             query = prod[part, :HD]
             key = prod[part, HD : 2 * HD]
-            inv_ref[at, :] = jnp.broadcast_to(inverse[part], (HALF, HD))
-            qraw_ref[at, :] = query
-            kraw_ref[at, :] = key
+            inv_ref[at, :] = jnp.broadcast_to(inverse[part], (HALF, HD)).astype(bf16)
+            qraw_ref[at, :] = query.astype(bf16)
+            kraw_ref[at, :] = key.astype(bf16)
             q_ref[at, :] = (roped(query, gq_ref[...]) * (SCORE_SCALE * LOG2_E)).astype(bf16)
             k_ref[at, :] = roped(key, gk_ref[...]).astype(bf16)
             v_ref[at, :] = prod[part, 2 * HD :].astype(bf16)
@@ -134,7 +144,6 @@
     width = w.shape[0]
     span = cos.shape[0]
     low = jax.ShapeDtypeStruct((span, HD), bf16)
-    wide = jax.ShapeDtypeStruct((span, HD), f32)
     whole = fixed((span, HD))
     return pl.pallas_call(
         project_kernel,
@@ -145,7 +154,7 @@
             + [fixed((width, HEAD_COLS)), whole, whole, fixed((1, HD)), fixed((1, HD))],
             out_specs=[whole] * 6,
         ),
-        out_shape=[low, low, low, wide, wide, wide],
+        out_shape=[low] * 6,
         compiler_params=pltpu.CompilerParams(vmem_limit_bytes=VMEM_BYTES),
         name="project",
     )(place, *groups, w, cos, sin, gq, gk)
@@ -173,11 +182,15 @@
 
             def back(raw, gain, grad, cos=cos, sin=sin):
                 unrot = grad * cos + pltpu.roll(grad * sin, HD // 2, 1)
-                return rms_back(raw, gain, unrot)
-
-            grad_q, q_terms = back(qraw_ref[at, :], gq_ref[...], dq_ref[at, :])
-            grad_k, k_terms = back(kraw_ref[at, :], gk_ref[...], dk_ref[at, :])
-            inverse = inv_ref[at, :]
+                inv_rms = lax.rsqrt(head_mean(raw * raw) + NORM_EPS)
+                normed = raw * inv_rms
+                scaled_up = unrot * gain
+                grad = inv_rms * (scaled_up - normed * head_mean(scaled_up * normed))
+                return grad, unrot * normed
+
+            grad_q, q_terms = back(qraw_ref[at, :].astype(f32), gq_ref[...], dq_ref[at, :])
+            grad_k, k_terms = back(kraw_ref[at, :].astype(f32), gk_ref[...], dk_ref[at, :])
+            inverse = inv_ref[at, :].astype(f32)
             for c, grad in enumerate((grad_q, grad_k, dv_ref[at, :])):
                 grads[part, c * HD : (c + 1) * HD] = grad.astype(bf16)
                 scaled[part, c * HD : (c + 1) * HD] = (grad * inverse).astype(bf16)
@@ -240,44 +253,63 @@
 
 def key_mask(len_row, offset):
     ahead = (
-        lax.broadcasted_iota(jnp.int32, (BK, BQ), 1)
-        - lax.broadcasted_iota(jnp.int32, (BK, BQ), 0)
+        lax.broadcasted_iota(jnp.int32, (SUB, BQ), 1)
+        - lax.broadcasted_iota(jnp.int32, (SUB, BQ), 0)
         + offset
     )
     return (ahead >= 0) & (ahead <= len_row)
 
 
-def attend_kernel(klo_ref, q_ref, k_ref, v_ref, len_ref, osend_ref, onat_ref, linv_ref, vt):
+def key_loops(bounds_ref, qb, q_at, tile):
+    low = bounds_ref[0, qb]
+    high = (q_at + BQ - 1) // BK + 1
+    first = jnp.minimum(bounds_ref[1, qb], high)
+    last = jnp.maximum((q_at + 1) // BK, first)
+
+    def run(masked):
+        def step(kb, _):
+            tile(kb, masked)
+            return 0
+
+        return step
+
+    lax.fori_loop(low, first, run(True), 0)
+    lax.fori_loop(first, last, run(False), 0)
+    lax.fori_loop(last, high, run(True), 0)
+
+
+def attend_kernel(
+    bounds_ref, q_ref, k_ref, v_ref, len_ref, osend_ref, onat_ref, linv_ref, acc, total
+):
     n_dev, rows, _ = osend_ref.shape
     half = rows // 2
     span = q_ref.shape[0]
-    for c in range(span // BQ):
-        to = slice(c * BQ, (c + 1) * BQ)
-        vt[:, to] = v_ref[to, :].astype(f32).T.astype(bf16)
-
     def q_step(qb, _):
         q_at = pl.multiple_of(qb * BQ, BQ)
         q_blk = q_ref[pl.ds(q_at, BQ), :]
         len_row = len_ref[pl.ds(qb, 1), :]
-
-        def k_step(kb, carry):
-            acc, total = carry
-            k_at = pl.multiple_of(kb * BK, BK)
-            s = dot_nt(k_ref[pl.ds(k_at, BK), :], q_blk)
-            p = jnp.where(key_mask(len_row, q_at - k_at), jnp.exp2(s), 0.0)
-            total = total + jnp.sum(p.reshape(BK // 8, 8, BQ), axis=0)
-            acc = acc + dot_nn(vt[:, pl.ds(k_at, BK)], p.astype(bf16))
-            return acc, total
-
-        acc, total = lax.fori_loop(
-            klo_ref[qb],
-            (q_at + BQ - 1) // BK + 1,
-            k_step,
-            (jnp.zeros((HD, BQ), f32), jnp.zeros((8, BQ), f32)),
-        )
-        inverse = 1.0 / jnp.sum(total, axis=0, keepdims=True)
+        acc[...] = jnp.zeros_like(acc)
+        total[...] = jnp.zeros_like(total)
+
+        def tile(kb, masked):
+            mixed = None
+            summed = None
+            for c in range(BK // SUB):
+                k_at = pl.multiple_of(kb * BK + c * SUB, SUB)
+                p = jnp.exp2(dot_nt(k_ref[pl.ds(k_at, SUB), :], q_blk))
+                if masked:
+                    p = jnp.where(key_mask(len_row, q_at - k_at), p, 0.0)
+                part = jnp.sum(p.reshape(SUB // 8, 8, BQ), axis=0)
+                more = dot_tn(v_ref[pl.ds(k_at, SUB), :], p.astype(bf16))
+                summed = part if summed is None else summed + part
+                mixed = more if mixed is None else mixed + more
+            acc[...] += mixed
+            total[...] += summed
+
+        key_loops(bounds_ref, qb, q_at, tile)
+        inverse = 1.0 / jnp.sum(total[...], axis=0, keepdims=True)
         linv_ref[pl.ds(qb, 1), :] = inverse
-        onat_ref[pl.ds(q_at, BQ), :] = (acc * inverse).T
+        onat_ref[pl.ds(q_at, BQ), :] = (acc[...] * inverse).T
         return 0
 
     lax.fori_loop(0, span // BQ, q_step, 0)
@@ -303,14 +335,17 @@
             jax.ShapeDtypeStruct((span, HD), f32),
             jax.ShapeDtypeStruct((span // BQ, BQ), f32),
         ],
-        scratch_shapes=[pltpu.VMEM((HD, span), bf16)],
+        scratch_shapes=[
+            pltpu.VMEM((HD, BQ), f32),
+            pltpu.VMEM((8, BQ), f32),
+        ],
         compiler_params=pltpu.CompilerParams(vmem_limit_bytes=VMEM_BYTES),
         name="attend",
     )(klo, q, k, v, lens)
 
 
 def attend_back_kernel(
-    klo_ref, q_ref, k_ref, v_ref, do_ref, onat_ref, linv_ref, len_ref, dq, dk, dv, kt, don
+    bounds_ref, q_ref, k_ref, v_ref, do_ref, onat_ref, linv_ref, len_ref, dq, dk, dv, don, acc
 ):
     n_dev, rows, _ = do_ref.shape
     half = rows // 2
@@ -319,7 +354,6 @@
         dev, side = dealt_slot(place, n_dev)
         to = slice(place * half, (place + 1) * half)
         don[to, :] = do_ref[dev, side * half : (side + 1) * half, :]
-        kt[:, to] = k_ref[to, :].astype(f32).T.astype(bf16)
     dk[...] = jnp.zeros_like(dk)
     dv[...] = jnp.zeros_like(dv)
 
@@ -331,22 +365,26 @@
         inverse = linv_ref[pl.ds(qb, 1), :]
         mixed = (do_blk.astype(f32) * onat_ref[pl.ds(q_at, BQ), :]).T
         delta = jnp.sum(mixed, axis=0, keepdims=True)
-
-        def k_step(kb, acc):
-            k_at = pl.multiple_of(kb * BK, BK)
-            here = pl.ds(k_at, BK)
-            s = dot_nt(k_ref[here, :], q_blk)
-            p = jnp.where(key_mask(len_row, q_at - k_at), jnp.exp2(s) * inverse, 0.0)
-            dp = dot_nt(v_ref[here, :], do_blk)
-            ds = (p * (dp - delta)).astype(bf16)
-            dv[here, :] += dot_nn(p.astype(bf16), do_blk)
-            dk[here, :] += dot_nn(ds, q_blk)
-            return acc + dot_nn(kt[:, here], ds)
-
-        acc = lax.fori_loop(
-            klo_ref[qb], (q_at + BQ - 1) // BK + 1, k_step, jnp.zeros((HD, BQ), f32)
-        )
-        dq[pl.ds(q_at, BQ), :] = (acc * SCORE_SCALE).T
+        acc[...] = jnp.zeros_like(acc)
+
+        def tile(kb, masked):
+            total = None
+            for c in range(BK // SUB):
+                k_at = pl.multiple_of(kb * BK + c * SUB, SUB)
+                here = pl.ds(k_at, SUB)
+                p = jnp.exp2(dot_nt(k_ref[here, :], q_blk)) * inverse
+                if masked:
+                    p = jnp.where(key_mask(len_row, q_at - k_at), p, 0.0)
+                dp = dot_nt(v_ref[here, :], do_blk)
+                ds = (p * (dp - delta)).astype(bf16)
+                dv[here, :] += dot_nn(p.astype(bf16), do_blk)
+                dk[here, :] += dot_nn(ds, q_blk)
+                more = dot_tn(k_ref[here, :], ds)
+                total = more if total is None else total + more
+            acc[...] += total
+
+        key_loops(bounds_ref, qb, q_at, tile)
+        dq[pl.ds(q_at, BQ), :] = (acc[...] * SCORE_SCALE).T
         return 0
 
     lax.fori_loop(0, span // BQ, q_step, 0)
@@ -360,7 +398,10 @@
         in_specs=[pl.BlockSpec(memory_space=pltpu.SMEM)] + [vmem()] * 7,
         out_specs=[vmem()] * 3,
         out_shape=[jax.ShapeDtypeStruct((span, HD), f32)] * 3,
-        scratch_shapes=[pltpu.VMEM((HD, span), bf16), pltpu.VMEM((span, HD), bf16)],
+        scratch_shapes=[
+            pltpu.VMEM((span, HD), bf16),
+            pltpu.VMEM((HD, BQ), f32),
+        ],
         compiler_params=pltpu.CompilerParams(vmem_limit_bytes=VMEM_BYTES),
         name="attend_back",
     )(klo, q, k, v, do, onat, linv, lens)
@@ -595,20 +636,6 @@
     return lax.all_gather(x, AXIS_CYZ, axis=0, tiled=True)
 
 
-def sum_over_x(blocks):
-    me = lax.axis_index(AXIS_X)
-    n = blocks.shape[0]
-
-    def block(i):
-        return lax.dynamic_index_in_dim(blocks, lax.rem(i, n), 0, keepdims=False)
-
-    total = block(me).astype(f32)
-    for shift in range(1, n):
-        pairs = [(i, (i + shift) % n) for i in range(n)]
-        total = total + lax.ppermute(block(me + shift), AXIS_X, pairs).astype(f32)
-    return total
-
-
 def shift(x, axis, step):
     n = SIZES[axis]
     return lax.ppermute(x, axis, [(i, (i + step) % n) for i in range(n)])
@@ -659,27 +686,6 @@
 
 def pick(v, i, n, axis):
     return lax.dynamic_index_in_dim(v, lax.rem(i, n), axis, keepdims=False)
-
-
-def sum_over_xl(x):
-    xl = lax.axis_index("xl")
-    return pick(x, xl, 2, 1).astype(f32) + shift(pick(x, xl + 1, 2, 1), "xl", 1).astype(f32)
-
-
-def sum_over_z(x):
-    z = lax.axis_index("z")
-    low = x.astype(bf16)
-    total = pick(x, z, 4, 1)
-    for step in (1, 2, 3):
-        total = total + shift(pick(low, z + step, 4, 1), "z", step).astype(f32)
-    return total
-
-
-def gather_shard(x):
-    xl = lax.axis_index("xl")
-    ring = lax.all_gather(x, "z", axis=0, tiled=False)
-    other = shift(ring, "xl", 1)
-    return jnp.stack([jnp.where(xl == 0, ring, other), jnp.where(xl == 0, other, ring)])
 
 
 def natural_of_permuted(x):
@@ -745,17 +751,18 @@
         axis=2,
     ).transpose(1, 0, 2)
     pair, ring = first_moves(tokens[0])
+    head = lax.all_to_all(own_head, CTX, 0, 0, tiled=True)
+    head = lax.all_gather(head, SHARD, axis=0, tiled=False)
     pairs = owner_pairs()
     own_out = lax.ppermute(w_out.astype(bf16), EVERY, [(p, n) for n, p in pairs])
     own_ffn = low_in[:, attn_cols:].reshape(owned, 2 * N_CHUNKS, CHUNK)
     own_ffn = own_ffn.transpose(1, 0, 2).reshape(2 * N_CHUNKS * owned, CHUNK)
     own_rest = jnp.concatenate([own_out, own_ffn], axis=0)
     own_rest = lax.all_gather(own_rest, AXIS_X, axis=0, tiled=False)
-    own_head, own_rest, pair, ring = lax.optimization_barrier((own_head, own_rest, pair, ring))
-    head = lax.all_to_all(own_head, CTX, 0, 0, tiled=True)
-    head, segments, pad_mask = lax.optimization_barrier((head, segments, pad_mask))
-    head = gather_shard(head)
-    head = head.transpose(2, 0, 1, 3, 4)
+    segments, pad_mask, own_rest, pair, ring = lax.optimization_barrier(
+        (segments, pad_mask, own_rest, pair, ring)
+    )
+    head = head.reshape((2, 4) + own_head.shape).transpose(2, 0, 1, 3, 4)
     gain_vals = head[:, :, :, 0, HEAD_COLS : HEAD_COLS + owned_gains].reshape(-1).astype(f32)
     w_head = head[..., :HEAD_COLS].reshape(width, HEAD_COLS)
     gain_one = gain_vals[:width]
@@ -786,7 +793,10 @@
         start = jnp.where(docs == number, before, start)
     place_in = at - start
     lens = jnp.where(live == 1, place_in, 0)
-    klo = jnp.min((at - lens).reshape(span // BQ, BQ), axis=1) // BK
+    first_key = (at - lens).reshape(span // BQ, BQ)
+    klo = jnp.stack(
+        [jnp.min(first_key, axis=1) // BK, (jnp.max(first_key, axis=1) + BK - 1) // BK]
+    )
     lens = lens.reshape(span // BQ, BQ)
     halves = jnp.arange(HD // 2, dtype=f32)
     inverse = ROPE_BASE ** (-2.0 * halves / HD)
@@ -830,18 +840,21 @@
     )
     dw_head = (dw_head * gain_one[:, None]).reshape(n_dev, owned, HEAD_COLS)
     dw_head = jnp.concatenate([dw_head, grad_gains], axis=2).astype(bf16)
-    dw_head = sum_over_xl(dw_head.reshape(n_ctx, 2, 4, owned, PAD_COLS))
+    dw_head = dw_head.reshape(n_ctx, n_dev // n_ctx, owned, PAD_COLS).transpose(1, 0, 2, 3)
     plane = sum_over_core(da_near, da_far)
-    dw_head, plane = lax.optimization_barrier((dw_head, plane))
-    dw_head = sum_over_z(dw_head).astype(bf16)
-    one, two = first_sums(plane)
-    dw_head, one, two = lax.optimization_barrier((dw_head, one, two))
-    dw_head = lax.all_to_all(dw_head, CTX, 0, 0, tiled=True).astype(f32)
-
-    grad_a = second_sums(one, two)
+    dw_head, _, _ = lax.optimization_barrier((dw_head, grads, plane))
+    dw_head = lax.psum_scatter(
+        dw_head.reshape(-1, PAD_COLS), SHARD, scatter_dimension=0, tiled=True
+    )
+    grads, dw_head = lax.optimization_barrier((grads, dw_head))
+    dw_head = lax.all_to_all(
+        dw_head.reshape(n_ctx, owned, PAD_COLS), CTX, 0, 0, tiled=True
+    ).astype(f32)
+    owned_gain_grad = jnp.sum(dw_head[:, 0, HEAD_COLS : HEAD_COLS + owned_gains], axis=0)
+
+    grad_a = second_sums(*first_sums(plane))
     inputs = tokens[0].astype(f32)
     input_grad = grad_residual + rms_back(inputs, gain_one, grad_a)[0]
-    owned_gain_grad = jnp.sum(dw_head[:, 0, HEAD_COLS : HEAD_COLS + owned_gains], axis=0)
 
     def columns(x):
         return x.transpose(1, 0, 2).reshape(owned, -1)
@@ -852,7 +865,8 @@
     out_part = grads[:OUT_ROWS].reshape(n_x, OUT_ROWS // n_x, width)
     ffn_part = grads[OUT_ROWS:].reshape(2 * N_CHUNKS, n_x, owned, CHUNK)
     ffn_part = ffn_part.transpose(1, 0, 2, 3).reshape(n_x, 2 * N_CHUNKS * owned, CHUNK)
-    grads = sum_over_x(jnp.concatenate([out_part, ffn_part], axis=1))
+    grads = jnp.concatenate([out_part, ffn_part], axis=1).reshape(-1, width)
+    grads = lax.psum_scatter(grads, AXIS_X, scatter_dimension=0, tiled=True).astype(f32)
     owned_out = lax.ppermute(grads[: OUT_ROWS // n_x], EVERY, pairs)
     owned_ffn = grads[OUT_ROWS // n_x :].reshape(2 * N_CHUNKS, owned, CHUNK)
     owned_in = jnp.concatenate(

time: 454 us -> 422 us (0.930)
  the two profiles are of different devices: /device:TPU:7 before, /device:TPU:96 now
where the time goes in v4:
time: 422 us; the launch traced here: 415 us
  Pallas kernels  124 us (29%)
  waiting for transfers between devices  121 us (29%)
  other arithmetic  52.5 us (12%)
  starting transfers between devices  42.4 us (10%)
  blocking collectives  34.4 us (8%)
  local copies, waits for them, and re-layouts  25.5 us (6%)
  between operations  14.8 us (4%)
    reduce_scatter x1, waiting for transfers between devices, body(): grads = lax.psum_scatter(grads, AXIS_YZ, scatter_dimension=0, tiled=True)  35.6 us
    pallas_call x1, Pallas kernels, attend_back(): pl.pallas_call(attend_back_kernel, in_specs=[pl.BlockSpec(memory_space=pl...  28.1 us
    pallas_call x1, Pallas kernels, middle(): pl.pallas_call(middle_kernel, grid=(N_CHUNKS + 2,), in_specs=[pl.BlockSpe...  26 us
    pallas_call x1, Pallas kernels, project_back(): pl.pallas_call(project_back_kernel, grid_spec=pltpu.PrefetchScalarGridSpe...  23.7 us
    ppermute x22, waiting for transfers between devices, shift(): return lax.ppermute(x, axis, [(i, (i + step) % n) for i in range(n)])  21.8 us
    ppermute x22, starting transfers between devices, shift(): return lax.ppermute(x, axis, [(i, (i + step) % n) for i in range(n)])  21 us
    all_gather x1, blocking collectives, body(): own_rest = lax.all_gather(own_rest, AXIS_X, axis=0, tiled=False)  19.3 us
    reduce_scatter x1, waiting for transfers between devices, body(): lax.psum_scatter(dw_head.reshape(-1, PAD_COLS), SHARD, scatter_dimension=...  19.1 us
  transfers between devices with their start and end apart: 32, of which 14 were waited for; matrix products, arithmetic and copies ran while one was open for 17% of the time, Pallas kernels for 24%

profile of v4, /device:TPU:96, one launch (start us, length us, event | category | flops | bytes accessed | tf_op | source)
XLA Modules:
  0.0 414.9 jit_solution(9269813316437392496)
XLA Ops:
  9.0 15.1 %all_to_all.20 = bf16[16,8,512]{2,1,0:T(8,128)(2,1)} all-to-all(bf16[16,8,512]{2,1,0:T(8,128)(2,1)S(1)} %maximum_bitcast_fusion.1), channel_id=1, replica_groups=mesh['xh'=2,'y'=4,'core'=2,'xl'=2,'z'=4] {'xh','y','core'}, dimensions={0} | all-to-all | bytes 262144 | tf_op jit(solution)/shard_map/all_to_all | solution.py:754
  25.1 1.9 collective-permute-start
  31.2 3.1 collective-permute-done
  34.3 19.3 %all-gather = bf16[352,1024]{1,0:T(8,128)(2,1)S(1)} all-gather(bf16[88,1024]{1,0:T(8,128)(2,1)S(1)} %pad_maximum_fusion.7), channel_id=2, replica_groups=mesh['xh'=2,'y'=4,'core'=2,'xl'=2,'z'=4] {'xh','xl'}, dimensions={0}, use_global_device_ids=true | all-gather | bytes 901120 | tf_op jit(solution)/shard_map/all_gather | solution.py:761
  56.1 3.4 collective-permute-start.7
  61.0 1.7 collective-permute-start.8
  63.6 8.4 %convert_bitcast_fusion = (f32[4096]{0:T(1024)S(1)}, s32[32,128]{1,0:T(8,128)S(1)}) fusion(s32[]{:T(128)} %get-tuple-element.132, s32[]{:T(128)} %get-tuple-element.128, s32[]{:T(128)} %get-tuple-element.93, s32[]{:T(128)} %get-tuple-element.91, s32[]{:T(128)} %get-tuple-element.130, s32[]{:T(128)} %get-tuple-element.134, s32[]{:T(128)} %get-tuple-element.92, ...), kind=kLoop, calls=%fused_computation.71 | loop fusion | flops 126976 | bytes 49204 | tf_op jit(solution)/shard_map/convert_element_type | solution.py:803
  72.0 9.8 %fusion.11 = (f32[4096,64]{1,0:T(8,128)}, f32[4096,64]{1,0:T(8,128)}, f32[4096,64]{1,0:T(8,128)}) fusion(f32[64]{0:T(128)S(1)} %multiply_power_fusion, f32[4096]{0:T(1024)S(1)} %get-tuple-element.105), kind=kLoop, calls=%fused_computation.32 | loop fusion | flops 524288 | bytes 3162368 | tf_op jit(solution)/shard_map/neg | solution.py:807
  81.9 1.9 constant_dynamic-update-slice_fusion.3
  83.8 4.2 %collective-permute-done.5 = bf16[2,128,1024]{2,1,0:T(8,128)(2,1)} collective-permute-done((bf16[2,128,1024]{2,1,0:T(8,128)(2,1)}, bf16[2,128,1024]{2,1,0:T(8,128)(2,1)}, u32[]{:S(2)}, u32[]{:S(2)}) %collective-permute-start.5) | collective-permute-done | bytes 524320 | tf_op jit(solution)/shard_map/ppermute | solution.py:641
  88.0 1.9 constant_dynamic-update-slice_fusion.2
  89.9 1.9 constant_dynamic-update-slice_fusion.1
  91.8 1.9 constant_dynamic-update-slice_fusion.x0
  96.7 6.6 %pad_maximum_fusion = (f32[4096,128]{1,0:T(8,128)}, f32[4096,128]{1,0:T(8,128)}) fusion(f32[4096,64]{1,0:T(8,128)} %get-tuple-element.124, f32[4096,64]{1,0:T(8,128)} %get-tuple-element.123, f32[4096,64]{1,0:T(8,128)} %get-tuple-element.122), kind=kLoop, calls=%fused_computation.5 | loop fusion | flops 1048576 | bytes 7340032 | tf_op jit(solution)/shard_map/concatenate | solution.py:806
  103.4 1.9 copy.86
  106.7 13.9 %project.1 = (bf16[4096,128]{1,0:T(8,128)(2,1)S(1)}, bf16[4096,128]{1,0:T(8,128)(2,1)S(1)}, bf16[4096,128]{1,0:T(8,128)(2,1)S(1)}, bf16[4096,128]{1,0:T(8,128)(2...) custom-call(s32[32]{0:T(128)S(1)} %stack.137.place_ref, ...), custom_call_target="tpu_custom_call" | custom-call | tf_op jit(solution)/shard_map/project/pallas_call | solution.py:148
  121.6 17.8 %attend.1 = (bf16[16,256,128]{2,1,0:T(8,128)(2,1)}, f32[4096,128]{1,0:T(8,128)}, f32[8,512]{1,0:T(8,128)S(1)}) custom-call(s32[2,8]{1,0:T(2,128)S(1)} %pad_add_fusion.1.bounds_ref, bf16[4096,128]{1,0:T(8,128)(2,1)S(1)} %get-tuple-element.50.q_ref, bf16[4096,128]{1,0:T(8,128)(2,1)S(1)} %get-tuple-element.51.k_ref, ...), custom_call_target="tpu_custom_call" | custom-call | tf_op jit(solution)/shard_map/attend/pallas_call | solution.py:329
  140.3 6.6 %all-to-all-start.1 = ((bf16[16,256,128]{2,1,0:T(8,128)(2,1)}), bf16[16,256,128]{2,1,0:T(8,128)(2,1)S(1)}, u32[]{:S(2)}, u32[]{:S(2)}) async-start(bf16[16,256,128]{2,1,0:T(8,128)(2,1)} %get-tuple-element.53), calls=%async_computation.1 | async-start | bytes 2097152 | tf_op jit(solution)/shard_map/all_to_all | solution.py:815
  147.1 1.8 fusion.shuffle_ref
  148.8 16.1 %all-to-all-done.1.mixed_ref = bf16[16,256,128]{2,1,0:T(8,128)(2,1)S(1)} async-done(((bf16[16,256,128]{2,1,0:T(8,128)(2,1)}), bf16[16,256,128]{2,1,0:T(8,128)(2,1)S(1)}, u32[]{:S(2)}, u32[]{:S(2)}) %all-to-all-start.1) | async-done | bytes 1048608 | tf_op jit(solution)/shard_map/all_to_all | solution.py:815
  165.9 26.0 %middle.1 = (f32[256,1024]{1,0:T(8,128)}, f32[256,1024]{1,0:T(8,128)}, bf16[16,256,128]{2,1,0:T(8,128)(2,1)}, bf16[2,256,3072]{2,1,0:T(8,128)(2,1)}, bf16[256,7168]{1,0:T(8,128)(2,1)}, /*index=5*/f32[1,1024]{1,0:T(1,128)}) custom-call(bf16[32,352,1024]{2,1,0:T(8,128)(2,1)} %bitcast.186, bf16[16,256,128]{2,1,0:T(8,128)(2,1)} %copy-done.17, ...), custom_call_target="tpu_custom_call" | custom-call | tf_op jit(solution)/shard_map/middle/pallas_call | solution.py:515
  192.1 3.3 dynamic-slice_bitcast_fusion
  195.8 4.3 %all-to-all-start.2 = ((bf16[16,256,128]{2,1,0:T(8,128)(2,1)}), bf16[16,256,128]{2,1,0:T(8,128)(2,1)}, u32[]{:S(2)}, u32[]{:S(2)}) async-start(bf16[16,256,128]{2,1,0:T(8,128)(2,1)} %get-tuple-element.56), calls=%async_computation.2 | async-start | bytes 2097152 | tf_op jit(solution)/shard_map/all_to_all | solution.py:826
  200.9 8.5 %grad_ffn.1.grads_ref = bf16[16,352,1024]{2,1,0:T(8,128)(2,1)} custom-call(bf16[256,3072]{1,0:T(8,128)(2,1)S(1)} %get-tuple-element.112.left_a, bf16[256,3072]{1,0:T(8,128)(2,1)S(1)} %collective-permute-done.11.left_b, bf16[256,7168]{1,0:T(8,128)(2,1)} %get-tuple-element.58.right_a.drb_a, bf16[256,7168]{1,0:T(8,128)(2,1)} %collective-permute-done.12.right_b.drb_b), custom_call_target="tpu_custom_call" | custom-call | tf_op jit(solution)/shard_map/grad_ffn/pallas_call | solution.py:567
  209.5 6.4 %grad_out.1 = bf16[16,352,1024]{2,1,0:T(8,128)(2,1)} custom-call(s32[1]{0:T(128)} %bitcast.68.core_ref, bf16[256,3072]{1,0:T(8,128)(2,1)S(1)} %get-tuple-element.112.left_a, bf16[256,3072]{1,0:T(8,128)(2,1)S(1)} %collective-permute-done.11.left_b, bf16[256,7168]{1,0:T(8,128)(2,1)} %get-tuple-element.58.right_a.drb_a, ...), custom_call_target="tpu_custom_call", output_to_operand_aliasing={{}: (7, {})} | custom-call | tf_op jit(solution)/shard_map/grad_out/pallas_call | solution.py:609
  215.8 2.4 all-to-all-done.2.do_ref
  220.1 28.1 %attend_back.1 = (f32[4096,128]{1,0:T(8,128)}, f32[4096,128]{1,0:T(8,128)}, f32[4096,128]{1,0:T(8,128)}) custom-call(s32[2,8]{1,0:T(2,128)S(1)} %pad_add_fusion.1.bounds_ref, bf16[4096,128]{1,0:T(8,128)(2,1)S(1)} %copy-done.1, bf16[4096,128]{1,0:T(8,128)(2,1)S(1)} %copy-done.3, bf16[4096,128]{1,0:T(8,128)(2,1)S(1)} %copy-done.5, ...), custom_call_target="tpu_custom_call" | custom-call | tf_op jit(solution)/shard_map/attend_back/pallas_call | solution.py:396
  248.2 23.7 %project_back.1 = (bf16[16,128,1024]{2,1,0:T(8,128)(2,1)}, bf16[16,128,1024]{2,1,0:T(8,128)(2,1)}, f32[1024,384]{1,0:T(8,128)}, f32[8,128]{1,0:T(8,128)}) custom-call(s32[32]{0:T(128)} %copy-done.9, bf16[8,128,1024]{2,1,0:T(8,128)(2,1)} %constant_dynamic-update-slice_fusion.x0, bf16[8,128,1024]{2,1,0:T(8,128)(2,1)} %copy-done.14, ...), custom_call_target="tpu_custom_call" | custom-call | tf_op jit(solution)/shard_map/project_back/pallas_call | solution.py:218
  273.0 2.0 multiply_convert_fusion
  275.4 4.4 %collective-permute-done.14 = bf16[16,128,1024]{2,1,0:T(8,128)(2,1)} collective-permute-done((bf16[16,128,1024]{2,1,0:T(8,128)(2,1)}, bf16[16,128,1024]{2,1,0:T(8,128)(2,1)}, u32[]{:S(2)}, u32[]{:S(2)}) %collective-permute-start.14) | collective-permute-done | bytes 4194336 | tf_op jit(solution)/shard_map/ppermute | solution.py:641
  279.7 5.8 %add_convert_fusion = bf16[16,128,1024]{2,1,0:T(8,128)(2,1)S(1)} fusion(bf16[16,128,1024]{2,1,0:T(8,128)(2,1)} %collective-permute-done.14, bf16[16,128,1024]{2,1,0:T(8,128)(2,1)} %get-tuple-element.68), kind=kLoop, calls=%fused_computation | loop fusion | flops 8388608 | bytes 12582912 | tf_op jit(solution)/shard_map/convert_element_type | solution.py:670
  288.0 2.1 collective-permute-start.15
  290.1 2.3 collective-permute-start.16
  293.5 35.6 %reduce-scatter.4.cloned.1.call-done = bf16[352,1024]{1,0:T(8,128)(2,1)} async-done(((bf16[5632,1024]{1,0:T(8,128)(2,1)}), bf16[352,1024]{1,0:T(8,128)(2,1)}) %reduce-scatter.4.cloned.1.call-update) | async-done | bytes 720912 | tf_op jit(solution)/shard_map/reduce_scatter | solution.py:829
  329.3 1.9 add_convert_fusion.2
  331.2 1.7 collective-permute-start.18
  333.0 1.6 add_convert_fusion.1
  334.7 2.0 collective-permute-start.22
  336.8 4.4 %collective-permute-done.18 = bf16[128,1024]{1,0:T(8,128)(2,1)S(1)} collective-permute-done((bf16[128,1024]{1,0:T(8,128)(2,1)S(1)}, bf16[128,1024]{1,0:T(8,128)(2,1)S(1)}, u32[]{:S(2)}, u32[]{:S(2)}) %collective-permute-start.18) | collective-permute-done | bytes 262176 | tf_op jit(solution)/shard_map/ppermute | solution.py:641
  341.2 2.7 collective-permute-done.20
  343.9 5.7 %collective-permute-done.22 = bf16[128,1024]{1,0:T(8,128)(2,1)S(1)} collective-permute-done((bf16[128,1024]{1,0:T(8,128)(2,1)S(1)}, bf16[128,1024]{1,0:T(8,128)(2,1)S(1)}, u32[]{:S(2)}, u32[]{:S(2)}) %collective-permute-start.22) | collective-permute-done | bytes 262176 | tf_op jit(solution)/shard_map/ppermute | solution.py:641
  349.8 19.1 %reduce-scatter.6.cloned.1.call-done = bf16[128,512]{1,0:T(8,128)(2,1)} async-done(((bf16[1024,512]{1,0:T(8,128)(2,1)}), bf16[128,512]{1,0:T(8,128)(2,1)}) %reduce-scatter.6.cloned.1.call-update) | async-done | bytes 131088 | tf_op jit(solution)/shard_map/reduce_scatter | solution.py:846
  370.2 6.5 %all-to-all-start.3 = ((bf16[16,8,512]{2,1,0:T(8,128)(2,1)}), bf16[16,8,512]{2,1,0:T(8,128)(2,1)S(1)}, u32[]{:S(2)}, u32[]{:S(2)}) async-start(bf16[16,8,512]{2,1,0:T(8,128)(2,1)} %bitcast.85), calls=%async_computation.5 | async-start | bytes 262144 | tf_op jit(solution)/shard_map/all_to_all | solution.py:850
  378.0 6.9 %all-to-all-done.3 = bf16[16,8,512]{2,1,0:T(8,128)(2,1)S(1)} async-done(((bf16[16,8,512]{2,1,0:T(8,128)(2,1)}), bf16[16,8,512]{2,1,0:T(8,128)(2,1)S(1)}, u32[]{:S(2)}, u32[]{:S(2)}) %all-to-all-start.3) | async-done | bytes 131104 | tf_op jit(solution)/shard_map/all_to_all | solution.py:850
  385.6 8.5 %reduce-scatter.8.cloned.1.call-done = bf16[88,1024]{1,0:T(8,128)(2,1)} async-done(((bf16[352,1024]{1,0:T(8,128)(2,1)}), bf16[88,1024]{1,0:T(8,128)(2,1)}) %reduce-scatter.8.cloned.1.call-update) | async-done | bytes 180240 | tf_op jit(solution)/shard_map/reduce_scatter | solution.py:869
  395.0 1.9 collective-permute-start.23
  397.9 2.2 fusion.23
  400.1 7.2 %collective-permute-done.23 = f32[40,1024]{1,0:T(8,128)S(1)} collective-permute-done((f32[40,1024]{1,0:T(8,128)S(1)}, f32[40,1024]{1,0:T(8,128)S(1)}, u32[]{:S(2)}, u32[]{:S(2)}) %collective-permute-start.23) | collective-permute-done | bytes 163872 | tf_op jit(solution)/shard_map/ppermute | solution.py:870
  (188 shorter events, 33.7 us)
Async XLA Ops:
  7.2 96.2 %all-gather.8.cloned.1.call-start = ((), (), s32[]{:S(2)}) async-start(), calls=%async_computation.11 | async-start | bytes 1179648 | tf_op jit(solution)/shard_map/all_gather | solution.py:755
  24.1 140.8 %all-gather.6.cloned.1.call-start = ((), (), s32[]{:S(2)}) async-start(), calls=%async_computation.10 | async-start | bytes 23789568 | tf_op jit(solution)/shard_map/all_gather | solution.py:636
  25.1 9.2 %collective-permute-start = (bf16[40,1024]{1,0:T(8,128)(2,1)S(1)}, bf16[40,1024]{1,0:T(8,128)(2,1)S(1)}, u32[]{:S(2)}, u32[]{:S(2)}) collective-permute-start(bf16[40,1024]{1,0:T(8,128)(2,1)S(1)} %convert_element_type.150), channel_id=1, source_target_pairs={{0,0},{4,1},{8,2},{12,3},{1,4},{5,5},{9,6},{13,7},{64,8},{68,9},{7... | collective-permute-start | bytes 245768 | tf_op jit(solution)/shard_map/ppermute | solution.py:757
  28.1 26.3 %collective-permute-start.4 = (bf16[1,128,1024]{2,1,0:T(8,128)(2,1)S(1)}, bf16[1,128,1024]{2,1,0:T(8,128)(2,1)S(1)}, u32[]{:S(2)}, u32[]{:S(2)}) collective-permute-start(bf16[1,128,1024]{2,1,0:T(8,128)(2,1)S(1)} %get-tuple-element.118), channel_id=1, source_target_pairs={{0,48},{16,0},{32,16},{48,32},{1,49},{17,1},{33,17},{49,33},{2,50}... | collective-permute-start | bytes 786440 | tf_op jit(solution)/shard_map/ppermute | solution.py:641
  29.2 25.2 %collective-permute-start.3 = (bf16[1,128,1024]{2,1,0:T(8,128)(2,1)S(1)}, bf16[1,128,1024]{2,1,0:T(8,128)(2,1)S(1)}, u32[]{:S(2)}, u32[]{:S(2)}) collective-permute-start(bf16[1,128,1024]{2,1,0:T(8,128)(2,1)S(1)} %get-tuple-element.118), channel_id=1, source_target_pairs={{0,32},{16,48},{32,0},{48,16},{1,33},{17,49},{33,1},{49,17},{2,34}... | collective-permute-start | bytes 786440 | tf_op jit(solution)/shard_map/ppermute | solution.py:641
  30.4 24.1 %collective-permute-start.2 = (bf16[1,128,1024]{2,1,0:T(8,128)(2,1)S(1)}, bf16[1,128,1024]{2,1,0:T(8,128)(2,1)S(1)}, u32[]{:S(2)}, u32[]{:S(2)}) collective-permute-start(bf16[1,128,1024]{2,1,0:T(8,128)(2,1)S(1)} %get-tuple-element.118), channel_id=1, source_target_pairs={{0,16},{16,32},{32,48},{48,0},{1,17},{17,33},{33,49},{49,1},{2,18}... | collective-permute-start | bytes 786440 | tf_op jit(solution)/shard_map/ppermute | solution.py:641
  30.4 23.2 %collective-permute-start.1 = (bf16[1,128,1024]{2,1,0:T(8,128)(2,1)S(1)}, bf16[1,128,1024]{2,1,0:T(8,128)(2,1)S(1)}, u32[]{:S(2)}, u32[]{:S(2)}) collective-permute-start(bf16[1,128,1024]{2,1,0:T(8,128)(2,1)S(1)} %get-tuple-element.119), channel_id=1, source_target_pairs={{0,64},{64,0},{1,65},{65,1},{2,66},{66,2},{3,67},{67,3},{4,68},{68... | collective-permute-start | bytes 786440 | tf_op jit(solution)/shard_map/ppermute | solution.py:641
  56.1 50.6 %copy-start.9 = (s32[32]{0:T(128)}, s32[32]{0:T(128)S(1)}, u32[]{:S(2)}) copy-start(s32[32]{0:T(128)S(1)} %stack.137.place_ref) | copy-start | bytes 388
  56.1 35.6 %collective-permute-start.7 = (bf16[2,128,1024]{2,1,0:T(8,128)(2,1)}, bf16[2,128,1024]{2,1,0:T(8,128)(2,1)}, u32[]{:S(2)}, u32[]{:S(2)}) collective-permute-start(bf16[2,128,1024]{2,1,0:T(8,128)(2,1)} %pad_maximum_fusion.5), channel_id=1, source_target_pairs={{0,48},{16,0},{32,16},{48,32},{1,49},{17,1},{33,17},{49,33},{2,50}... | collective-permute-start | bytes 1572872 | tf_op jit(solution)/shard_map/ppermute | solution.py:641
  59.5 30.3 %collective-permute-start.6 = (bf16[2,128,1024]{2,1,0:T(8,128)(2,1)}, bf16[2,128,1024]{2,1,0:T(8,128)(2,1)}, u32[]{:S(2)}, u32[]{:S(2)}) collective-permute-start(bf16[2,128,1024]{2,1,0:T(8,128)(2,1)} %pad_maximum_fusion.5), channel_id=1, source_target_pairs={{0,32},{16,48},{32,0},{48,16},{1,33},{17,49},{33,1},{49,17},{2,34}... | collective-permute-start | bytes 1572872 | tf_op jit(solution)/shard_map/ppermute | solution.py:641
  60.4 27.6 %collective-permute-start.5 = (bf16[2,128,1024]{2,1,0:T(8,128)(2,1)}, bf16[2,128,1024]{2,1,0:T(8,128)(2,1)}, u32[]{:S(2)}, u32[]{:S(2)}) collective-permute-start(bf16[2,128,1024]{2,1,0:T(8,128)(2,1)} %pad_maximum_fusion.5), channel_id=1, source_target_pairs={{0,16},{16,32},{32,48},{48,0},{1,17},{17,33},{33,49},{49,1},{2,18}... | collective-permute-start | bytes 1572872 | tf_op jit(solution)/shard_map/ppermute | solution.py:641
  61.0 32.6 %collective-permute-start.8 = (bf16[4,128,1024]{2,1,0:T(8,128)(2,1)S(1)}, bf16[4,128,1024]{2,1,0:T(8,128)(2,1)}, u32[]{:S(2)}, u32[]{:S(2)}) collective-permute-start(bf16[4,128,1024]{2,1,0:T(8,128)(2,1)S(1)} %pad_maximum_fusion.2), channel_id=1, source_target_pairs={{0,64},{64,0},{1,65},{65,1},{2,66},{66,2},{3,67},{67,3},{4,68},{68... | collective-permute-start | bytes 3145736 | tf_op jit(solution)/shard_map/ppermute | solution.py:641
  93.6 13.0 %collective-permute-start.9 = (bf16[8,128,1024]{2,1,0:T(8,128)(2,1)}, bf16[8,128,1024]{2,1,0:T(8,128)(2,1)}, u32[]{:S(2)}, u32[]{:S(2)}) collective-permute-start(bf16[8,128,1024]{2,1,0:T(8,128)(2,1)} %constant_dynamic-update-slice_fusion.x0), channel_id=1, source_target_pairs={{0,8},{8,0},{1,9},{9,1},{2,10},{10,2},{3,11},{11,3},{4,12},{12,4},... | collective-permute-start | bytes 6291464 | tf_op jit(solution)/shard_map/ppermute | solution.py:641
  95.0 11.7 %collective-permute-start.10 = (bf16[8,128,1024]{2,1,0:T(8,128)(2,1)S(1)}, bf16[8,128,1024]{2,1,0:T(8,128)(2,1)}, u32[]{:S(2)}, u32[]{:S(2)}) collective-permute-start(bf16[8,128,1024]{2,1,0:T(8,128)(2,1)S(1)} %constant_dynamic-update-slice_fusion.4.x1), channel_id=1, source_target_pairs={{0,8},{8,0},{1,9},{9,1},{2,10},{10,2},{3,11},{11,3},{4,12},{12,4},... | collective-permute-start | bytes 6291464 | tf_op jit(solution)/shard_map/ppermute | solution.py:641
  105.5 15.0 %copy-start.15 = (bf16[16,2,4,8,384]{4,3,2,1,0:T(8,128)(2,1)}, bf16[16,2,4,8,384]{4,3,2,1,0:T(8,128)(2,1)S(1)}, u32[]{:S(2)}) copy-start(bf16[16,2,4,8,384]{4,3,2,1,0:T(8,128)(2,1)S(1)} %copy.70) | copy-start | bytes 2359300
  105.8 14.8 %copy-start.10 = (f32[1,128]{1,0:T(1,128)}, f32[1,128]{1,0:T(1,128)S(1)}, u32[]{:S(2)}) copy-start(f32[1,128]{1,0:T(1,128)S(1)} %get-tuple-element.140.gk_ref) | copy-start | bytes 1540
  105.8 14.8 %copy-start.11 = (f32[1,128]{1,0:T(1,128)}, f32[1,128]{1,0:T(1,128)S(1)}, u32[]{:S(2)}) copy-start(f32[1,128]{1,0:T(1,128)S(1)} %get-tuple-element.141.gq_ref) | copy-start | bytes 1540
  121.6 17.8 %copy-start.2 = (bf16[4096,128]{1,0:T(8,128)(2,1)}, bf16[4096,128]{1,0:T(8,128)(2,1)S(1)}, u32[]{:S(2)}) copy-start(bf16[4096,128]{1,0:T(8,128)(2,1)S(1)} %get-tuple-element.51.k_ref) | copy-start | bytes 3145732
  121.6 17.8 %copy-start.4 = (bf16[4096,128]{1,0:T(8,128)(2,1)}, bf16[4096,128]{1,0:T(8,128)(2,1)S(1)}, u32[]{:S(2)}) copy-start(bf16[4096,128]{1,0:T(8,128)(2,1)S(1)} %get-tuple-element.52.v_ref) | copy-start | bytes 3145732
  121.6 17.8 %copy-start.8 = (bf16[4096,128]{1,0:T(8,128)(2,1)}, bf16[4096,128]{1,0:T(8,128)(2,1)S(1)}, u32[]{:S(2)}) copy-start(bf16[4096,128]{1,0:T(8,128)(2,1)S(1)} %get-tuple-element.66.kraw_ref) | copy-start | bytes 3145732
  140.3 24.6 %all-to-all-start.1 = ((bf16[16,256,128]{2,1,0:T(8,128)(2,1)}), bf16[16,256,128]{2,1,0:T(8,128)(2,1)S(1)}, u32[]{:S(2)}, u32[]{:S(2)}) async-start(bf16[16,256,128]{2,1,0:T(8,128)(2,1)} %get-tuple-element.53), calls=%async_computation.1 | async-start | bytes 2097152 | tf_op jit(solution)/shard_map/all_to_all | solution.py:815
  192.0 9.0 %collective-permute-start.12 = (bf16[256,7168]{1,0:T(8,128)(2,1)}, bf16[256,7168]{1,0:T(8,128)(2,1)}, u32[]{:S(2)}, u32[]{:S(2)}) collective-permute-start(bf16[256,7168]{1,0:T(8,128)(2,1)} %get-tuple-element.58.right_a.drb_a), channel_id=1, source_target_pairs={{0,8},{8,0},{1,9},{9,1},{2,10},{10,2},{3,11},{11,3},{4,12},{12,4},... | collective-permute-start | bytes 11010056 | tf_op jit(solution)/shard_map/ppermute | solution.py:641
  195.4 5.6 %collective-permute-start.11 = (bf16[256,3072]{1,0:T(8,128)(2,1)}, bf16[256,3072]{1,0:T(8,128)(2,1)S(1)}, u32[]{:S(2)}, u32[]{:S(2)}) collective-permute-start(bf16[256,3072]{1,0:T(8,128)(2,1)} %get-tuple-element.111), channel_id=1, source_target_pairs={{0,8},{8,0},{1,9},{9,1},{2,10},{10,2},{3,11},{11,3},{4,12},{12,4},... | collective-permute-start | bytes 4718600 | tf_op jit(solution)/shard_map/ppermute | solution.py:641
  195.8 22.4 %all-to-all-start.2 = ((bf16[16,256,128]{2,1,0:T(8,128)(2,1)}), bf16[16,256,128]{2,1,0:T(8,128)(2,1)}, u32[]{:S(2)}, u32[]{:S(2)}) async-start(bf16[16,256,128]{2,1,0:T(8,128)(2,1)} %get-tuple-element.56), calls=%async_computation.2 | async-start | bytes 2097152 | tf_op jit(solution)/shard_map/all_to_all | solution.py:826
  200.2 128.8 %reduce-scatter.4.cloned.1.call-start = ((), (), s32[]{:S(2)}) async-start(), calls=%async_computation.7 | async-start | bytes 12255232 | tf_op jit(solution)/shard_map/reduce_scatter | solution.py:829
  200.2 9.2 %collective-permute-start.13 = (bf16[256,1024]{1,0:T(8,128)(2,1)}, bf16[256,1024]{1,0:T(8,128)(2,1)S(1)}, u32[]{:S(2)}, u32[]{:S(2)}) collective-permute-start(bf16[256,1024]{1,0:T(8,128)(2,1)} %bitcast.184), channel_id=1, source_target_pairs={{0,8},{8,0},{1,9},{9,1},{2,10},{10,2},{3,11},{11,3},{4,12},{12,4},... | collective-permute-start | bytes 1572872 | tf_op jit(solution)/shard_map/ppermute | solution.py:641
  218.2 150.7 %reduce-scatter.6.cloned.1.call-start = ((), (), s32[]{:S(2)}) async-start(), calls=%async_computation.8 | async-start | bytes 1179648 | tf_op jit(solution)/shard_map/reduce_scatter | solution.py:846
  248.2 24.0 %copy-start.25 = (f32[1,1024]{1,0:T(1,128)S(1)}, f32[1,1024]{1,0:T(1,128)}, u32[]{:S(2)}) copy-start(f32[1,1024]{1,0:T(1,128)} %get-tuple-element.72) | copy-start | bytes 12292
  248.2 24.8 %copy-start.16 = (bf16[16,2,4,8,384]{4,3,2,1,0:T(8,128)(2,1)S(1)}, bf16[16,2,4,8,384]{4,3,2,1,0:T(8,128)(2,1)}, u32[]{:S(2)}) copy-start(bf16[16,2,4,8,384]{4,3,2,1,0:T(8,128)(2,1)} %copy-done.15) | copy-start | bytes 2359300
  272.0 7.8 %collective-permute-start.14 = (bf16[16,128,1024]{2,1,0:T(8,128)(2,1)}, bf16[16,128,1024]{2,1,0:T(8,128)(2,1)}, u32[]{:S(2)}, u32[]{:S(2)}) collective-permute-start(bf16[16,128,1024]{2,1,0:T(8,128)(2,1)} %get-tuple-element.69), channel_id=1, source_target_pairs={{0,8},{8,0},{1,9},{9,1},{2,10},{10,2},{3,11},{11,3},{4,12},{12,4},... | collective-permute-start | bytes 12582920 | tf_op jit(solution)/shard_map/ppermute | solution.py:641
  285.6 47.4 %collective-permute-start.19 = (bf16[4,128,1024]{2,1,0:T(8,128)(2,1)S(1)}, bf16[4,128,1024]{2,1,0:T(8,128)(2,1)S(1)}, u32[]{:S(2)}, u32[]{:S(2)}) collective-permute-start(bf16[4,128,1024]{2,1,0:T(8,128)(2,1)S(1)} %slice.199), channel_id=1, source_target_pairs={{0,64},{64,0},{1,65},{65,1},{2,66},{66,2},{3,67},{67,3},{4,68},{68... | collective-permute-start | bytes 3145736 | tf_op jit(solution)/shard_map/ppermute | solution.py:641
  288.0 41.1 %copy-start.13 = (bf16[1,256,1024]{2,1,0:T(8,128)(2,1)S(1)}, bf16[1,256,1024]{2,1,0:T(8,128)(2,1)}, u32[]{:S(2)}) copy-start(bf16[1,256,1024]{2,1,0:T(8,128)(2,1)} %param.14) | copy-start | bytes 1572868
  288.0 41.3 %collective-permute-start.15 = (bf16[2,128,1024]{2,1,0:T(8,128)(2,1)}, bf16[2,128,1024]{2,1,0:T(8,128)(2,1)}, u32[]{:S(2)}, u32[]{:S(2)}) collective-permute-start(bf16[2,128,1024]{2,1,0:T(8,128)(2,1)} %get-tuple-element.108), channel_id=1, source_target_pairs={{0,48},{16,0},{32,16},{48,32},{1,49},{17,1},{33,17},{49,33},{2,50}... | collective-permute-start | bytes 1572872 | tf_op jit(solution)/shard_map/ppermute | solution.py:641
  290.1 39.2 %collective-permute-start.17 = (bf16[2,128,1024]{2,1,0:T(8,128)(2,1)}, bf16[2,128,1024]{2,1,0:T(8,128)(2,1)}, u32[]{:S(2)}, u32[]{:S(2)}) collective-permute-start(bf16[2,128,1024]{2,1,0:T(8,128)(2,1)} %get-tuple-element.109), channel_id=1, source_target_pairs={{0,16},{16,32},{32,48},{48,0},{1,17},{17,33},{33,49},{49,1},{2,18}... | collective-permute-start | bytes 1572872 | tf_op jit(solution)/shard_map/ppermute | solution.py:641
  290.1 39.2 %collective-permute-start.16 = (bf16[2,128,1024]{2,1,0:T(8,128)(2,1)}, bf16[2,128,1024]{2,1,0:T(8,128)(2,1)}, u32[]{:S(2)}, u32[]{:S(2)}) collective-permute-start(bf16[2,128,1024]{2,1,0:T(8,128)(2,1)} %get-tuple-element.110), channel_id=1, source_target_pairs={{0,32},{16,48},{32,0},{48,16},{1,33},{17,49},{33,1},{49,17},{2,34}... | collective-permute-start | bytes 1572872 | tf_op jit(solution)/shard_map/ppermute | solution.py:641
  329.1 65.1 %reduce-scatter.8.cloned.1.call-start = ((), (), s32[]{:S(2)}) async-start(), calls=%async_computation.9 | async-start | bytes 901120 | tf_op jit(solution)/shard_map/reduce_scatter | solution.py:869
  331.2 9.9 %collective-permute-start.18 = (bf16[128,1024]{1,0:T(8,128)(2,1)S(1)}, bf16[128,1024]{1,0:T(8,128)(2,1)S(1)}, u32[]{:S(2)}, u32[]{:S(2)}) collective-permute-start(bf16[128,1024]{1,0:T(8,128)(2,1)S(1)} %slice_bitcast_fusion.5), channel_id=1, source_target_pairs={{0,64},{64,0},{1,65},{65,1},{2,66},{66,2},{3,67},{67,3},{4,68},{68... | collective-permute-start | bytes 786440 | tf_op jit(solution)/shard_map/ppermute | solution.py:641
  334.6 34.3 %slice-start.1 = ((bf16[352,1024]{1,0:T(8,128)(2,1)}), bf16[192,1024]{1,0:T(8,128)(2,1)S(1)}, s32[]{:S(2)}) async-start(bf16[352,1024]{1,0:T(8,128)(2,1)} %reduce-scatter.4.cloned.1.call-done), calls=%async_computation.13 | async-start | bytes 786432 | tf_op jit(solution)/shard_map/slice | solution.py:866
  334.7 9.3 %collective-permute-start.20 = (bf16[128,1024]{1,0:T(8,128)(2,1)S(1)}, bf16[128,1024]{1,0:T(8,128)(2,1)S(1)}, u32[]{:S(2)}, u32[]{:S(2)}) collective-permute-start(bf16[128,1024]{1,0:T(8,128)(2,1)S(1)} %get-tuple-element.115), channel_id=1, source_target_pairs={{0,48},{16,0},{32,16},{48,32},{1,49},{17,1},{33,17},{49,33},{2,50}... | collective-permute-start | bytes 786440 | tf_op jit(solution)/shard_map/ppermute | solution.py:641
  334.7 14.9 %collective-permute-start.22 = (bf16[128,1024]{1,0:T(8,128)(2,1)S(1)}, bf16[128,1024]{1,0:T(8,128)(2,1)S(1)}, u32[]{:S(2)}, u32[]{:S(2)}) collective-permute-start(bf16[128,1024]{1,0:T(8,128)(2,1)S(1)} %get-tuple-element.116), channel_id=1, source_target_pairs={{0,16},{16,32},{32,48},{48,0},{1,17},{17,33},{33,49},{49,1},{2,18}... | collective-permute-start | bytes 786440 | tf_op jit(solution)/shard_map/ppermute | solution.py:641
  336.7 12.9 %collective-permute-start.21 = (bf16[128,1024]{1,0:T(8,128)(2,1)S(1)}, bf16[128,1024]{1,0:T(8,128)(2,1)S(1)}, u32[]{:S(2)}, u32[]{:S(2)}) collective-permute-start(bf16[128,1024]{1,0:T(8,128)(2,1)S(1)} %get-tuple-element.117), channel_id=1, source_target_pairs={{0,32},{16,48},{32,0},{48,16},{1,33},{17,49},{33,1},{49,17},{2,34}... | collective-permute-start | bytes 786440 | tf_op jit(solution)/shard_map/ppermute | solution.py:641
  341.2 27.8 %slice-start = ((bf16[352,1024]{1,0:T(8,128)(2,1)}), bf16[160,1024]{1,0:T(8,128)(2,1)S(1)}, s32[]{:S(2)}) async-start(bf16[352,1024]{1,0:T(8,128)(2,1)} %reduce-scatter.4.cloned.1.call-done), calls=%async_computation.12 | async-start | bytes 655360 | tf_op jit(solution)/shard_map/slice | solution.py:865
  370.2 14.7 %all-to-all-start.3 = ((bf16[16,8,512]{2,1,0:T(8,128)(2,1)}), bf16[16,8,512]{2,1,0:T(8,128)(2,1)S(1)}, u32[]{:S(2)}, u32[]{:S(2)}) async-start(bf16[16,8,512]{2,1,0:T(8,128)(2,1)} %bitcast.85), calls=%async_computation.5 | async-start | bytes 262144 | tf_op jit(solution)/shard_map/all_to_all | solution.py:850
  376.8 21.1 %copy-start.18 = (f32[8,10240]{1,0:T(8,128)S(1)}, f32[8,10240]{1,0:T(8,128)}, u32[]{:S(2)}) copy-start(f32[8,10240]{1,0:T(8,128)} %param.18) | copy-start | bytes 983044
  378.0 29.3 %copy-start.20 = (f32[40,1024]{1,0:T(8,128)S(1)}, f32[40,1024]{1,0:T(8,128)}, u32[]{:S(2)}) copy-start(f32[40,1024]{1,0:T(8,128)} %param.19) | copy-start | bytes 491524
  378.0 29.3 %copy-start.21 = (f32[40,1024]{1,0:T(8,128)S(1)}, f32[40,1024]{1,0:T(8,128)}, u32[]{:S(2)}) copy-start(f32[40,1024]{1,0:T(8,128)} %param.25) | copy-start | bytes 491524
  378.0 29.3 %copy-start.22 = (f32[40,1024]{1,0:T(8,128)S(1)}, f32[40,1024]{1,0:T(8,128)}, u32[]{:S(2)}) copy-start(f32[40,1024]{1,0:T(8,128)} %param.22) | copy-start | bytes 491524
  395.0 12.3 %collective-permute-start.23 = (f32[40,1024]{1,0:T(8,128)S(1)}, f32[40,1024]{1,0:T(8,128)S(1)}, u32[]{:S(2)}, u32[]{:S(2)}) collective-permute-start(f32[40,1024]{1,0:T(8,128)S(1)} %slice.208), channel_id=1, source_target_pairs={{0,0},{1,4},{2,8},{3,12},{4,1},{5,5},{6,9},{7,13},{8,64},{9,68},{1... | collective-permute-start | bytes 491528 | tf_op jit(solution)/shard_map/ppermute | solution.py:870
  (15 other events, 75.7 us)
Sparse Core Ops, SparseCore 0:
  24.3 34.8 all-gather.7
  61.4 97.0 all-gather.5
  218.4 110.6 reduce-scatter.3
  332.0 36.9 reduce-scatter.5
  371.3 22.7 reduce-scatter.7

commit v5 on v4

--- a/solution.py
+++ b/solution.py
@@ -66,6 +66,51 @@
 
 def dot_nn(a, b):
     return lax.dot_general(a, b, (((1,), (0,)), ((), ())), preferred_element_type=f32)
+
+
+LAST_DOC = 13
+
+
+def tables_kernel(docs_ref, live_ref, freq_ref, cos_ref, sin_ref, lens_ref):
+    docs = docs_ref[...]
+    shape = docs.shape
+    start = jnp.zeros(shape, f32)
+    for number in range(1, LAST_DOC + 1):
+        before = jnp.sum(jnp.where(docs < number, 1.0, 0.0))
+        start = jnp.where(docs == number, before, start)
+    at = lax.broadcasted_iota(jnp.int32, shape, 0) * shape[1] + lax.broadcasted_iota(
+        jnp.int32, shape, 1
+    )
+    within = at.astype(f32) - start
+    lens_ref[...] = jnp.where(live_ref[...] == 1, within.astype(jnp.int32), 0)
+
+    left = lax.broadcasted_iota(jnp.int32, (HD, HD), 1) < HD // 2
+    for i in range(0, shape[0], 2):
+        cols = [jnp.broadcast_to(within[i + n : i + n + 1, :], (HD, HD)).T for n in range(2)]
+        angle = jnp.where(left, cols[0], cols[1]) * freq_ref[...]
+        for ref, values, flip in ((cos_ref, jnp.cos(angle), False), (sin_ref, jnp.sin(angle), True)):
+            turned = pltpu.roll(values, HD // 2, 1)
+            for n in range(2):
+                lower, upper = (values, turned) if n == 0 else (turned, values)
+                ref[(i + n) * HD : (i + n + 1) * HD, :] = jnp.where(
+                    left, -lower if flip else lower, upper
+                )
+
+
+def tables(docs, live, freq):
+    span = docs.size
+    table = jax.ShapeDtypeStruct((span, HD), f32)
+    return pl.pallas_call(
+        tables_kernel,
+        in_specs=[vmem()] * 3,
+        out_specs=[vmem()] * 3,
+        out_shape=[table, table, jax.ShapeDtypeStruct(docs.shape, jnp.int32)],
+        compiler_params=pltpu.CompilerParams(vmem_limit_bytes=VMEM_BYTES),
+        cost_estimate=pl.CostEstimate(
+            flops=100 * span * HD, bytes_accessed=3 * span * HD * 4, transcendentals=span * HD
+        ),
+        name="tables",
+    )(docs, live, freq)
 
 
 N_GROUPS = 4
@@ -648,9 +693,10 @@
     return pair, ring
 
 
-def second_moves(pair, ring):
+def second_moves(pair, ring, after):
     one = jnp.concatenate([pair] + [shift(pair, "y", b) for b in (1, 2, 3)], axis=0)
     two = jnp.concatenate([ring, shift(ring, "xh", 1)], axis=0)
+    one, two, _ = lax.optimization_barrier((one, two, after))
     return [one, two, shift(one, "core", 1), shift(two, "core", 1)]
 
 
@@ -784,29 +830,18 @@
         x = x.reshape(n_ctx, 2, half)
         return jnp.concatenate([x[:, 0], x[::-1, 1]], axis=0)
 
-    docs = natural(segments[0])
-    live = natural(pad_mask[0])
-    at = jnp.arange(span, dtype=jnp.int32).reshape(2 * n_ctx, half)
-    start = jnp.zeros_like(docs)
-    for number in range(1, 14):
-        before = jnp.sum((docs < number).astype(jnp.int32))
-        start = jnp.where(docs == number, before, start)
-    place_in = at - start
-    lens = jnp.where(live == 1, place_in, 0)
-    first_key = (at - lens).reshape(span // BQ, BQ)
+    halves = jnp.arange(HD // 2, dtype=f32)
+    inverse = ROPE_BASE ** (-2.0 * halves / HD)
+    cos, sin, lens = tables(
+        natural(segments[0]), natural(pad_mask[0]), jnp.concatenate([inverse, inverse])[None]
+    )
+    first_key = (jnp.arange(span, dtype=jnp.int32).reshape(lens.shape) - lens).reshape(span // BQ, BQ)
     klo = jnp.stack(
         [jnp.min(first_key, axis=1) // BK, (jnp.max(first_key, axis=1) + BK - 1) // BK]
     )
     lens = lens.reshape(span // BQ, BQ)
-    halves = jnp.arange(HD // 2, dtype=f32)
-    inverse = ROPE_BASE ** (-2.0 * halves / HD)
-    angle = place_in.reshape(span, 1).astype(f32) * inverse[None, :]
-    cos_half = jnp.cos(angle)
-    sin_half = jnp.sin(angle)
-    cos = jnp.concatenate([cos_half, cos_half], axis=1)
-    sin = jnp.concatenate([-sin_half, sin_half], axis=1)
-
-    groups = second_moves(pair, ring)
+
+    groups = second_moves(pair, ring, (cos, klo, lens))
     place = places_of_groups()
     q, k, v, query_raw, key_raw, inv = project(
         place, groups, w_scaled, cos, sin, gain_query, gain_key
@@ -842,17 +877,15 @@
     dw_head = jnp.concatenate([dw_head, grad_gains], axis=2).astype(bf16)
     dw_head = dw_head.reshape(n_ctx, n_dev // n_ctx, owned, PAD_COLS).transpose(1, 0, 2, 3)
     plane = sum_over_core(da_near, da_far)
-    dw_head, _, _ = lax.optimization_barrier((dw_head, grads, plane))
-    dw_head = lax.psum_scatter(
-        dw_head.reshape(-1, PAD_COLS), SHARD, scatter_dimension=0, tiled=True
-    )
-    grads, dw_head = lax.optimization_barrier((grads, dw_head))
-    dw_head = lax.all_to_all(
-        dw_head.reshape(n_ctx, owned, PAD_COLS), CTX, 0, 0, tiled=True
-    ).astype(f32)
+    dw_head, _ = lax.optimization_barrier((dw_head, plane))
+    dw_head = lax.all_to_all(dw_head, SHARD, 0, 0, tiled=True)
+    dw_head = jnp.sum(dw_head.astype(f32), axis=0).astype(bf16)
+    one, two = first_sums(plane)
+    dw_head, _, _ = lax.optimization_barrier((dw_head, one, two))
+    dw_head = lax.all_to_all(dw_head, CTX, 0, 0, tiled=True).astype(f32)
     owned_gain_grad = jnp.sum(dw_head[:, 0, HEAD_COLS : HEAD_COLS + owned_gains], axis=0)
 
-    grad_a = second_sums(*first_sums(plane))
+    grad_a = second_sums(one, two)
     inputs = tokens[0].astype(f32)
     input_grad = grad_residual + rms_back(inputs, gain_one, grad_a)[0]
 

time: 422 us -> 410 us (0.972)
  other arithmetic: 52.5 us -> 30.4 us
  starting transfers between devices: 42.4 us -> 51.1 us
  Pallas kernels: 124 us -> 129 us
    ppermute x22, waiting for transfers between devices: 21.8 us -> 65.5 us  [shift(): return lax.ppermute(x, axis, [(i, (i + step) % n) for i in range(n)])]
    reduce_scatter x1, waiting for transfers between devices: 35.6 us -> 0.02 us  [body(): grads = lax.psum_scatter(grads, AXIS_YZ, scatter_dimension=0, tiled=True)]
    reduce_scatter x1 -> x0, waiting for transfers between devices: 19.1 us -> none  [body(): lax.psum_scatter(dw_head.reshape(-1, PAD_COLS), SHARD, scatter_dimension=...]
    neg x1 -> x0, other arithmetic: 9.8 us -> none  [body(): sin = jnp.concatenate([-sin_half, sin_half], axis=1)]
    convert_element_type x2 -> x1, other arithmetic: 8.42 us -> 0.02 us  [body(): dw_head = lax.all_to_all(dw_head, CTX, 0, 0, tiled=True).astype(f32)]
    all_gather x1, waiting for transfers between devices: 0.01 us -> 8.16 us  [gathered(): return lax.all_gather(x, AXIS_CYZ, axis=0, tiled=True)]
    all_to_all x1 -> x2, waiting for transfers between devices: 6.88 us -> 1.91 us  [the longest x1 1.9 us: body(): dw_head = lax.all_to_all(dw_head, CTX, 0, 0, tiled=True).astype(f32)]
    all_to_all x1 -> x2, starting transfers between devices: 6.45 us -> 11.2 us  [the longest x1 7.04 us: body(): dw_head = lax.all_to_all(dw_head, SHARD, 0, 0, tiled=True)]
  transfers between devices with their start and end apart: 32 -> 32, of which waited for: 14 -> 18; matrix products, arithmetic and copies ran while one was open for 17% -> 11% of each run, Pallas kernels for 24% -> 26%
where the time goes in v5:
time: 410 us; the launch traced here: 403 us
  Pallas kernels  129 us (31%)
  waiting for transfers between devices  117 us (29%)
  starting transfers between devices  51.1 us (12%)
  blocking collectives  34.4 us (8%)
  other arithmetic  30.4 us (7%)
  local copies, waits for them, and re-layouts  25.4 us (6%)
  between operations  15 us (4%)
    ppermute x22, waiting for transfers between devices, shift(): return lax.ppermute(x, axis, [(i, (i + step) % n) for i in range(n)])  65.5 us
    pallas_call x1, Pallas kernels, attend_back(): pl.pallas_call(attend_back_kernel, in_specs=[pl.BlockSpec(memory_space=pl...  28 us
    pallas_call x1, Pallas kernels, middle(): pl.pallas_call(middle_kernel, grid=(N_CHUNKS + 2,), in_specs=[pl.BlockSpe...  25.9 us
    ppermute x22, starting transfers between devices, shift(): return lax.ppermute(x, axis, [(i, (i + step) % n) for i in range(n)])  25.7 us
    pallas_call x1, Pallas kernels, project_back(): pl.pallas_call(project_back_kernel, grid_spec=pltpu.PrefetchScalarGridSpe...  24.4 us
    all_gather x1, blocking collectives, body(): own_rest = lax.all_gather(own_rest, AXIS_X, axis=0, tiled=False)  19.3 us
    all_to_all x1, waiting for transfers between devices, body(): mixed = lax.all_to_all(o_send, CTX, 0, 0, tiled=True)  18.5 us
    pallas_call x1, Pallas kernels, attend(): pl.pallas_call(attend_kernel, in_specs=[pl.BlockSpec(memory_space=pltpu.S...  17.7 us
  transfers between devices with their start and end apart: 32, of which 18 were waited for; matrix products, arithmetic and copies ran while one was open for 11% of the time, Pallas kernels for 26%

profile of v5, /device:TPU:96, one launch (start us, length us, event | category | flops | bytes accessed | tf_op | source)
XLA Modules:
  0.0 402.7 jit_solution(3715312016495796370)
XLA Ops:
  9.0 15.1 %all_to_all.25 = bf16[16,8,512]{2,1,0:T(8,128)(2,1)} all-to-all(bf16[16,8,512]{2,1,0:T(8,128)(2,1)S(1)} %maximum_bitcast_fusion.1), channel_id=1, replica_groups=mesh['xh'=2,'y'=4,'core'=2,'xl'=2,'z'=4] {'xh','y','core'}, dimensions={0} | all-to-all | bytes 262144 | tf_op jit(solution)/shard_map/all_to_all | solution.py:800
  25.1 1.9 collective-permute-start
  31.2 3.1 collective-permute-done
  34.3 19.3 %all-gather = bf16[352,1024]{1,0:T(8,128)(2,1)S(1)} all-gather(bf16[88,1024]{1,0:T(8,128)(2,1)S(1)} %pad_maximum_fusion.7), channel_id=2, replica_groups=mesh['xh'=2,'y'=4,'core'=2,'xl'=2,'z'=4] {'xh','xl'}, dimensions={0}, use_global_device_ids=true | all-gather | bytes 901120 | tf_op jit(solution)/shard_map/all_gather | solution.py:807
  55.0 3.3 collective-permute-start.7
  61.5 4.4 %tables.1 = (f32[4096,128]{1,0:T(8,128)S(1)}, f32[4096,128]{1,0:T(8,128)S(1)}, s32[32,128]{1,0:T(8,128)S(1)}) custom-call(s32[32,128]{1,0:T(8,128)S(1)} %get-tuple-element.124.docs_ref, s32[32,128]{1,0:T(8,128)S(1)} %get-tuple-element.125.live_ref, f32[1,128]{1,0:T(1,128)S(1)} %maximum_bitcast_fusion.2.freq_ref), custom_call_target="tpu_custom_call" | custom-call | flops 52428800 | bytes 6291456 | tf_op jit(solution)/shard_map/tables/pallas_call | solution.py:103
  69.1 7.2 %collective-permute-done.7 = bf16[2,128,1024]{2,1,0:T(8,128)(2,1)S(1)} collective-permute-done((bf16[2,128,1024]{2,1,0:T(8,128)(2,1)S(1)}, bf16[2,128,1024]{2,1,0:T(8,128)(2,1)S(1)}, u32[]{:S(2)}, u32[]{:S(2)}) %collective-permute-start.7) | collective-permute-done | bytes 524320 | tf_op jit(solution)/shard_map/ppermute | solution.py:686
  77.9 7.5 %collective-permute-done.5 = bf16[2,128,1024]{2,1,0:T(8,128)(2,1)} collective-permute-done((bf16[2,128,1024]{2,1,0:T(8,128)(2,1)S(1)}, bf16[2,128,1024]{2,1,0:T(8,128)(2,1)}, u32[]{:S(2)}, u32[]{:S(2)}) %collective-permute-start.5) | collective-permute-done | bytes 524320 | tf_op jit(solution)/shard_map/ppermute | solution.py:686
  85.5 1.8 pad_maximum_fusion.x0
  87.3 3.5 pad_maximum_fusion.1.x1
  95.1 3.2 collective-permute-done.10.x3
  98.3 13.7 %project.1 = (bf16[4096,128]{1,0:T(8,128)(2,1)S(1)}, bf16[4096,128]{1,0:T(8,128)(2,1)S(1)}, bf16[4096,128]{1,0:T(8,128)(2,1)S(1)}, bf16[4096,128]{1,0:T(8,128)(2...) custom-call(s32[32]{0:T(128)S(1)} %stack.137.place_ref, bf16[8,128,1024]{2,1,0:T(8,128)(2,1)} %copy-done.14, ...), custom_call_target="tpu_custom_call" | custom-call | tf_op jit(solution)/shard_map/project/pallas_call | solution.py:193
  112.9 17.7 %attend.1 = (bf16[16,256,128]{2,1,0:T(8,128)(2,1)}, f32[4096,128]{1,0:T(8,128)}, f32[8,512]{1,0:T(8,128)S(1)}) custom-call(s32[2,8]{1,0:T(2,128)S(1)} %pad_add_fusion.2.bounds_ref, bf16[4096,128]{1,0:T(8,128)(2,1)S(1)} %get-tuple-element.59.q_ref, bf16[4096,128]{1,0:T(8,128)(2,1)S(1)} %get-tuple-element.60.k_ref, ...), custom_call_target="tpu_custom_call" | custom-call | tf_op jit(solution)/shard_map/attend/pallas_call | solution.py:374
  131.7 5.2 %all-to-all-start.1 = ((bf16[16,256,128]{2,1,0:T(8,128)(2,1)}), bf16[16,256,128]{2,1,0:T(8,128)(2,1)S(1)}, u32[]{:S(2)}, u32[]{:S(2)}) async-start(bf16[16,256,128]{2,1,0:T(8,128)(2,1)} %get-tuple-element.62), calls=%async_computation.1 | async-start | bytes 2097152 | tf_op jit(solution)/shard_map/all_to_all | solution.py:850
  137.0 1.8 fusion.shuffle_ref
  138.8 18.5 %all-to-all-done.1.mixed_ref = bf16[16,256,128]{2,1,0:T(8,128)(2,1)S(1)} async-done(((bf16[16,256,128]{2,1,0:T(8,128)(2,1)}), bf16[16,256,128]{2,1,0:T(8,128)(2,1)S(1)}, u32[]{:S(2)}, u32[]{:S(2)}) %all-to-all-start.1) | async-done | bytes 1048608 | tf_op jit(solution)/shard_map/all_to_all | solution.py:850
  157.3 8.2 %all-gather.6.cloned.1.call-done = bf16[11264,1024]{1,0:T(8,128)(2,1)} async-done(((bf16[352,1024]{1,0:T(8,128)(2,1)}), bf16[11264,1024]{1,0:T(8,128)(2,1)}) %all-gather.6.cloned.1.call-update) | async-done | bytes 23068688 | tf_op jit(solution)/shard_map/all_gather | solution.py:681
  165.5 25.9 %middle.1 = (f32[256,1024]{1,0:T(8,128)}, f32[256,1024]{1,0:T(8,128)}, bf16[16,256,128]{2,1,0:T(8,128)(2,1)}, bf16[2,256,3072]{2,1,0:T(8,128)(2,1)}, bf16[256,7168]{1,0:T(8,128)(2,1)}, /*index=5*/f32[1,1024]{1,0:T(1,128)}) custom-call(bf16[32,352,1024]{2,1,0:T(8,128)(2,1)} %bitcast.176, bf16[16,256,128]{2,1,0:T(8,128)(2,1)} %copy-done.19, ...), custom_call_target="tpu_custom_call" | custom-call | tf_op jit(solution)/shard_map/middle/pallas_call | solution.py:560
  191.7 3.2 dynamic-slice_bitcast_fusion
  195.1 5.1 %all-to-all-start.2 = ((bf16[16,256,128]{2,1,0:T(8,128)(2,1)}), bf16[16,256,128]{2,1,0:T(8,128)(2,1)}, u32[]{:S(2)}, u32[]{:S(2)}) async-start(bf16[16,256,128]{2,1,0:T(8,128)(2,1)} %get-tuple-element.65), calls=%async_computation.2 | async-start | bytes 2097152 | tf_op jit(solution)/shard_map/all_to_all | solution.py:861
  200.7 8.6 %grad_ffn.1.grads_ref = bf16[16,352,1024]{2,1,0:T(8,128)(2,1)} custom-call(bf16[256,3072]{1,0:T(8,128)(2,1)S(1)} %get-tuple-element.104.left_a, bf16[256,3072]{1,0:T(8,128)(2,1)S(1)} %collective-permute-done.11.left_b, bf16[256,7168]{1,0:T(8,128)(2,1)} %get-tuple-element.67.right_a.drb_a, bf16[256,7168]{1,0:T(8,128)(2,1)} %collective-permute-done.12.right_b.drb_b), custom_call_target="tpu_custom_call" | custom-call | tf_op jit(solution)/shard_map/grad_ffn/pallas_call | solution.py:612
  209.3 6.3 %grad_out.1 = bf16[16,352,1024]{2,1,0:T(8,128)(2,1)} custom-call(s32[1]{0:T(128)} %bitcast.66.core_ref, bf16[256,3072]{1,0:T(8,128)(2,1)S(1)} %get-tuple-element.104.left_a, bf16[256,3072]{1,0:T(8,128)(2,1)S(1)} %collective-permute-done.11.left_b, bf16[256,7168]{1,0:T(8,128)(2,1)} %get-tuple-element.67.right_a.drb_a, ...), custom_call_target="tpu_custom_call", output_to_operand_aliasing={{}: (7, {})} | custom-call | tf_op jit(solution)/shard_map/grad_out/pallas_call | solution.py:654
  215.6 2.7 all-to-all-done.2.do_ref
  220.1 28.0 %attend_back.1 = (f32[4096,128]{1,0:T(8,128)}, f32[4096,128]{1,0:T(8,128)}, f32[4096,128]{1,0:T(8,128)}) custom-call(s32[2,8]{1,0:T(2,128)S(1)} %pad_add_fusion.2.bounds_ref, bf16[4096,128]{1,0:T(8,128)(2,1)S(1)} %copy-done.3, bf16[4096,128]{1,0:T(8,128)(2,1)S(1)} %copy-done.5, bf16[4096,128]{1,0:T(8,128)(2,1)S(1)} %copy-done.7, ...), custom_call_target="tpu_custom_call" | custom-call | tf_op jit(solution)/shard_map/attend_back/pallas_call | solution.py:441
  248.2 24.4 %project_back.1 = (bf16[16,128,1024]{2,1,0:T(8,128)(2,1)}, bf16[16,128,1024]{2,1,0:T(8,128)(2,1)}, f32[1024,384]{1,0:T(8,128)}, f32[8,128]{1,0:T(8,128)}) custom-call(s32[32]{0:T(128)} %copy-done.11, bf16[8,128,1024]{2,1,0:T(8,128)(2,1)} %copy-done.14, bf16[8,128,1024]{2,1,0:T(8,128)(2,1)} %pad_maximum_fusion.1.x1, ...), custom_call_target="tpu_custom_call" | custom-call | tf_op jit(solution)/shard_map/project_back/pallas_call | solution.py:263
  273.4 1.9 multiply_convert_fusion
  275.3 4.7 %collective-permute-done.14 = bf16[16,128,1024]{2,1,0:T(8,128)(2,1)S(1)} collective-permute-done((bf16[16,128,1024]{2,1,0:T(8,128)(2,1)}, bf16[16,128,1024]{2,1,0:T(8,128)(2,1)S(1)}, u32[]{:S(2)}, u32[]{:S(2)}) %collective-permute-start.14) | collective-permute-done | bytes 4194336 | tf_op jit(solution)/shard_map/ppermute | solution.py:686
  280.1 3.6 add_convert_fusion
  283.6 1.9 copy-done.15
  286.8 1.8 collective-permute-start.15
  291.5 2.4 slice.199
  294.0 7.0 %all-to-all-start.3 = ((bf16[8,16,8,512]{3,2,1,0:T(8,128)(2,1)}), bf16[8,16,8,512]{3,2,1,0:T(8,128)(2,1)S(1)}, u32[]{:S(2)}, u32[]{:S(2)}) async-start(bf16[8,16,8,512]{3,2,1,0:T(8,128)(2,1)} %maximum_bitcast_fusion), calls=%async_computation.3 | async-start | bytes 2097152 | tf_op jit(solution)/shard_map/all_to_all | solution.py:881
  301.0 2.6 collective-permute-start.19
  303.6 7.8 %collective-permute-done.15 = bf16[2,128,1024]{2,1,0:T(8,128)(2,1)} collective-permute-done((bf16[2,128,1024]{2,1,0:T(8,128)(2,1)}, bf16[2,128,1024]{2,1,0:T(8,128)(2,1)}, u32[]{:S(2)}, u32[]{:S(2)}) %collective-permute-start.15) | collective-permute-done | bytes 524320 | tf_op jit(solution)/shard_map/ppermute | solution.py:686
  311.5 6.5 %collective-permute-done.17 = bf16[2,128,1024]{2,1,0:T(8,128)(2,1)} collective-permute-done((bf16[2,128,1024]{2,1,0:T(8,128)(2,1)}, bf16[2,128,1024]{2,1,0:T(8,128)(2,1)}, u32[]{:S(2)}, u32[]{:S(2)}) %collective-permute-start.17) | collective-permute-done | bytes 524320 | tf_op jit(solution)/shard_map/ppermute | solution.py:686
  317.9 7.4 %collective-permute-done.16 = bf16[2,128,1024]{2,1,0:T(8,128)(2,1)} collective-permute-done((bf16[2,128,1024]{2,1,0:T(8,128)(2,1)}, bf16[2,128,1024]{2,1,0:T(8,128)(2,1)}, u32[]{:S(2)}, u32[]{:S(2)}) %collective-permute-start.16) | collective-permute-done | bytes 524320 | tf_op jit(solution)/shard_map/ppermute | solution.py:686
  325.3 1.9 add_convert_fusion.2
  327.2 2.7 collective-permute-start.18
  330.1 13.1 %collective-permute-done.18 = bf16[128,1024]{1,0:T(8,128)(2,1)S(1)} collective-permute-done((bf16[128,1024]{1,0:T(8,128)(2,1)S(1)}, bf16[128,1024]{1,0:T(8,128)(2,1)S(1)}, u32[]{:S(2)}, u32[]{:S(2)}) %collective-permute-start.18) | collective-permute-done | bytes 262176 | tf_op jit(solution)/shard_map/ppermute | solution.py:686
  345.8 4.2 %all-to-all-start.4 = ((bf16[16,8,512]{2,1,0:T(8,128)(2,1)}), bf16[16,8,512]{2,1,0:T(8,128)(2,1)S(1)}, u32[]{:S(2)}, u32[]{:S(2)}) async-start(bf16[16,8,512]{2,1,0:T(8,128)(2,1)} %reduce_sum.69), calls=%async_computation.4 | async-start | bytes 262144 | tf_op jit(solution)/shard_map/all_to_all | solution.py:885
  350.9 3.1 collective-permute-start.20
  354.0 2.3 collective-permute-start.21
  356.4 1.9 all-to-all-done.4
  361.7 4.7 %collective-permute-done.20 = bf16[128,1024]{1,0:T(8,128)(2,1)} collective-permute-done((bf16[128,1024]{1,0:T(8,128)(2,1)}, bf16[128,1024]{1,0:T(8,128)(2,1)}, u32[]{:S(2)}, u32[]{:S(2)}) %collective-permute-start.20) | collective-permute-done | bytes 262176 | tf_op jit(solution)/shard_map/ppermute | solution.py:686
  366.4 3.0 collective-permute-done.22
  372.4 9.1 %reduce-scatter.5.cloned.1.call-done = bf16[88,1024]{1,0:T(8,128)(2,1)} async-done(((bf16[352,1024]{1,0:T(8,128)(2,1)}), bf16[88,1024]{1,0:T(8,128)(2,1)}) %reduce-scatter.5.cloned.1.call-update) | async-done | bytes 180240 | tf_op jit(solution)/shard_map/reduce_scatter | solution.py:902
  382.4 1.9 collective-permute-start.23
  386.5 8.2 %collective-permute-done.23 = f32[40,1024]{1,0:T(8,128)S(1)} collective-permute-done((f32[40,1024]{1,0:T(8,128)S(1)}, f32[40,1024]{1,0:T(8,128)S(1)}, u32[]{:S(2)}, u32[]{:S(2)}) %collective-permute-start.23) | collective-permute-done | bytes 163872 | tf_op jit(solution)/shard_map/ppermute | solution.py:903
  (193 shorter events, 44.1 us)
Async XLA Ops:
  7.2 84.8 %all-gather.8.cloned.1.call-start = ((), (), s32[]{:S(2)}) async-start(), calls=%async_computation.10 | async-start | bytes 1179648 | tf_op jit(solution)/shard_map/all_gather | solution.py:801
  24.1 141.3 %all-gather.6.cloned.1.call-start = ((), (), s32[]{:S(2)}) async-start(), calls=%async_computation.9 | async-start | bytes 23789568 | tf_op jit(solution)/shard_map/all_gather | solution.py:681
  25.1 9.2 %collective-permute-start = (bf16[40,1024]{1,0:T(8,128)(2,1)S(1)}, bf16[40,1024]{1,0:T(8,128)(2,1)S(1)}, u32[]{:S(2)}, u32[]{:S(2)}) collective-permute-start(bf16[40,1024]{1,0:T(8,128)(2,1)S(1)} %convert_element_type.105), channel_id=1, source_target_pairs={{0,0},{4,1},{8,2},{12,3},{1,4},{5,5},{9,6},{13,7},{64,8},{68,9},{7... | collective-permute-start | bytes 245768 | tf_op jit(solution)/shard_map/ppermute | solution.py:803
  28.1 25.6 %collective-permute-start.4 = (bf16[1,128,1024]{2,1,0:T(8,128)(2,1)S(1)}, bf16[1,128,1024]{2,1,0:T(8,128)(2,1)S(1)}, u32[]{:S(2)}, u32[]{:S(2)}) collective-permute-start(bf16[1,128,1024]{2,1,0:T(8,128)(2,1)S(1)} %get-tuple-element.110), channel_id=1, source_target_pairs={{0,48},{16,0},{32,16},{48,32},{1,49},{17,1},{33,17},{49,33},{2,50}... | collective-permute-start | bytes 786440 | tf_op jit(solution)/shard_map/ppermute | solution.py:686
  29.2 24.4 %collective-permute-start.3 = (bf16[1,128,1024]{2,1,0:T(8,128)(2,1)S(1)}, bf16[1,128,1024]{2,1,0:T(8,128)(2,1)S(1)}, u32[]{:S(2)}, u32[]{:S(2)}) collective-permute-start(bf16[1,128,1024]{2,1,0:T(8,128)(2,1)S(1)} %get-tuple-element.110), channel_id=1, source_target_pairs={{0,32},{16,48},{32,0},{48,16},{1,33},{17,49},{33,1},{49,17},{2,34}... | collective-permute-start | bytes 786440 | tf_op jit(solution)/shard_map/ppermute | solution.py:686
  30.4 23.3 %collective-permute-start.2 = (bf16[1,128,1024]{2,1,0:T(8,128)(2,1)S(1)}, bf16[1,128,1024]{2,1,0:T(8,128)(2,1)S(1)}, u32[]{:S(2)}, u32[]{:S(2)}) collective-permute-start(bf16[1,128,1024]{2,1,0:T(8,128)(2,1)S(1)} %get-tuple-element.110), channel_id=1, source_target_pairs={{0,16},{16,32},{32,48},{48,0},{1,17},{17,33},{33,49},{49,1},{2,18}... | collective-permute-start | bytes 786440 | tf_op jit(solution)/shard_map/ppermute | solution.py:686
  30.4 23.2 %collective-permute-start.1 = (bf16[1,128,1024]{2,1,0:T(8,128)(2,1)S(1)}, bf16[1,128,1024]{2,1,0:T(8,128)(2,1)S(1)}, u32[]{:S(2)}, u32[]{:S(2)}) collective-permute-start(bf16[1,128,1024]{2,1,0:T(8,128)(2,1)S(1)} %get-tuple-element.111), channel_id=1, source_target_pairs={{0,64},{64,0},{1,65},{65,1},{2,66},{66,2},{3,67},{67,3},{4,68},{68... | collective-permute-start | bytes 786440 | tf_op jit(solution)/shard_map/ppermute | solution.py:686
  55.0 21.3 %collective-permute-start.7 = (bf16[2,128,1024]{2,1,0:T(8,128)(2,1)S(1)}, bf16[2,128,1024]{2,1,0:T(8,128)(2,1)S(1)}, u32[]{:S(2)}, u32[]{:S(2)}) collective-permute-start(bf16[2,128,1024]{2,1,0:T(8,128)(2,1)S(1)} %pad_maximum_fusion.5), channel_id=1, source_target_pairs={{0,48},{16,0},{32,16},{48,32},{1,49},{17,1},{33,17},{49,33},{2,50}... | collective-permute-start | bytes 1572872 | tf_op jit(solution)/shard_map/ppermute | solution.py:686
  58.4 18.0 %collective-permute-start.6 = (bf16[2,128,1024]{2,1,0:T(8,128)(2,1)S(1)}, bf16[2,128,1024]{2,1,0:T(8,128)(2,1)S(1)}, u32[]{:S(2)}, u32[]{:S(2)}) collective-permute-start(bf16[2,128,1024]{2,1,0:T(8,128)(2,1)S(1)} %pad_maximum_fusion.5), channel_id=1, source_target_pairs={{0,32},{16,48},{32,0},{48,16},{1,33},{17,49},{33,1},{49,17},{2,34}... | collective-permute-start | bytes 1572872 | tf_op jit(solution)/shard_map/ppermute | solution.py:686
  59.2 26.3 %collective-permute-start.5 = (bf16[2,128,1024]{2,1,0:T(8,128)(2,1)S(1)}, bf16[2,128,1024]{2,1,0:T(8,128)(2,1)}, u32[]{:S(2)}, u32[]{:S(2)}) collective-permute-start(bf16[2,128,1024]{2,1,0:T(8,128)(2,1)S(1)} %pad_maximum_fusion.5), channel_id=1, source_target_pairs={{0,16},{16,32},{32,48},{48,0},{1,17},{17,33},{33,49},{49,1},{2,18}... | collective-permute-start | bytes 1572872 | tf_op jit(solution)/shard_map/ppermute | solution.py:686
  59.8 27.5 %collective-permute-start.8 = (bf16[4,128,1024]{2,1,0:T(8,128)(2,1)S(1)}, bf16[4,128,1024]{2,1,0:T(8,128)(2,1)}, u32[]{:S(2)}, u32[]{:S(2)}) collective-permute-start(bf16[4,128,1024]{2,1,0:T(8,128)(2,1)S(1)} %pad_maximum_fusion.2), channel_id=1, source_target_pairs={{0,64},{64,0},{1,65},{65,1},{2,66},{66,2},{3,67},{67,3},{4,68},{68... | collective-permute-start | bytes 3145736 | tf_op jit(solution)/shard_map/ppermute | solution.py:686
  90.8 4.3 %collective-permute-start.9 = (bf16[8,128,1024]{2,1,0:T(8,128)(2,1)S(1)}, bf16[8,128,1024]{2,1,0:T(8,128)(2,1)}, u32[]{:S(2)}, u32[]{:S(2)}) collective-permute-start(bf16[8,128,1024]{2,1,0:T(8,128)(2,1)S(1)} %pad_maximum_fusion.x0), channel_id=1, source_target_pairs={{0,8},{8,0},{1,9},{9,1},{2,10},{10,2},{3,11},{11,3},{4,12},{12,4},... | collective-permute-start | bytes 6291464 | tf_op jit(solution)/shard_map/ppermute | solution.py:686
  90.8 7.5 %collective-permute-start.10 = (bf16[8,128,1024]{2,1,0:T(8,128)(2,1)}, bf16[8,128,1024]{2,1,0:T(8,128)(2,1)}, u32[]{:S(2)}, u32[]{:S(2)}) collective-permute-start(bf16[8,128,1024]{2,1,0:T(8,128)(2,1)} %pad_maximum_fusion.1.x1), channel_id=1, source_target_pairs={{0,8},{8,0},{1,9},{9,1},{2,10},{10,2},{3,11},{11,3},{4,12},{12,4},... | collective-permute-start | bytes 6291464 | tf_op jit(solution)/shard_map/ppermute | solution.py:686
  93.8 18.1 %copy-start.17 = (bf16[16,2,4,8,384]{4,3,2,1,0:T(8,128)(2,1)}, bf16[16,2,4,8,384]{4,3,2,1,0:T(8,128)(2,1)S(1)}, u32[]{:S(2)}) copy-start(bf16[16,2,4,8,384]{4,3,2,1,0:T(8,128)(2,1)S(1)} %copy.60) | copy-start | bytes 2359300
  94.0 17.9 %copy-start.12 = (f32[1,128]{1,0:T(1,128)}, f32[1,128]{1,0:T(1,128)S(1)}, u32[]{:S(2)}) copy-start(f32[1,128]{1,0:T(1,128)S(1)} %get-tuple-element.120.gk_ref) | copy-start | bytes 1540
  94.0 17.9 %copy-start.13 = (f32[1,128]{1,0:T(1,128)}, f32[1,128]{1,0:T(1,128)S(1)}, u32[]{:S(2)}) copy-start(f32[1,128]{1,0:T(1,128)S(1)} %get-tuple-element.121.gq_ref) | copy-start | bytes 1540
  112.9 17.7 %copy-start.4 = (bf16[4096,128]{1,0:T(8,128)(2,1)}, bf16[4096,128]{1,0:T(8,128)(2,1)S(1)}, u32[]{:S(2)}) copy-start(bf16[4096,128]{1,0:T(8,128)(2,1)S(1)} %get-tuple-element.60.k_ref) | copy-start | bytes 3145732
  112.9 17.7 %copy-start.6 = (bf16[4096,128]{1,0:T(8,128)(2,1)}, bf16[4096,128]{1,0:T(8,128)(2,1)S(1)}, u32[]{:S(2)}) copy-start(bf16[4096,128]{1,0:T(8,128)(2,1)S(1)} %get-tuple-element.61.v_ref) | copy-start | bytes 3145732
  112.9 17.7 %copy-start.10 = (bf16[4096,128]{1,0:T(8,128)(2,1)}, bf16[4096,128]{1,0:T(8,128)(2,1)S(1)}, u32[]{:S(2)}) copy-start(bf16[4096,128]{1,0:T(8,128)(2,1)S(1)} %get-tuple-element.75.kraw_ref) | copy-start | bytes 3145732
  131.7 25.6 %all-to-all-start.1 = ((bf16[16,256,128]{2,1,0:T(8,128)(2,1)}), bf16[16,256,128]{2,1,0:T(8,128)(2,1)S(1)}, u32[]{:S(2)}, u32[]{:S(2)}) async-start(bf16[16,256,128]{2,1,0:T(8,128)(2,1)} %get-tuple-element.62), calls=%async_computation.1 | async-start | bytes 2097152 | tf_op jit(solution)/shard_map/all_to_all | solution.py:850
  191.3 9.4 %collective-permute-start.12 = (bf16[256,7168]{1,0:T(8,128)(2,1)}, bf16[256,7168]{1,0:T(8,128)(2,1)}, u32[]{:S(2)}, u32[]{:S(2)}) collective-permute-start(bf16[256,7168]{1,0:T(8,128)(2,1)} %get-tuple-element.67.right_a.drb_a), channel_id=1, source_target_pairs={{0,8},{8,0},{1,9},{9,1},{2,10},{10,2},{3,11},{11,3},{4,12},{12,4},... | collective-permute-start | bytes 11010056 | tf_op jit(solution)/shard_map/ppermute | solution.py:686
  194.9 5.8 %collective-permute-start.11 = (bf16[256,3072]{1,0:T(8,128)(2,1)}, bf16[256,3072]{1,0:T(8,128)(2,1)S(1)}, u32[]{:S(2)}, u32[]{:S(2)}) collective-permute-start(bf16[256,3072]{1,0:T(8,128)(2,1)} %get-tuple-element.103), channel_id=1, source_target_pairs={{0,8},{8,0},{1,9},{9,1},{2,10},{10,2},{3,11},{11,3},{4,12},{12,4},... | collective-permute-start | bytes 4718600 | tf_op jit(solution)/shard_map/ppermute | solution.py:686
  195.1 23.1 %all-to-all-start.2 = ((bf16[16,256,128]{2,1,0:T(8,128)(2,1)}), bf16[16,256,128]{2,1,0:T(8,128)(2,1)}, u32[]{:S(2)}, u32[]{:S(2)}) async-start(bf16[16,256,128]{2,1,0:T(8,128)(2,1)} %get-tuple-element.65), calls=%async_computation.2 | async-start | bytes 2097152 | tf_op jit(solution)/shard_map/all_to_all | solution.py:861
  200.2 158.1 %reduce-scatter.3.cloned.1.call-start = ((), (), s32[]{:S(2)}) async-start(), calls=%async_computation.7 | async-start | bytes 12255232 | tf_op jit(solution)/shard_map/reduce_scatter | solution.py:864
  200.3 9.0 %collective-permute-start.13 = (bf16[256,1024]{1,0:T(8,128)(2,1)}, bf16[256,1024]{1,0:T(8,128)(2,1)S(1)}, u32[]{:S(2)}, u32[]{:S(2)}) collective-permute-start(bf16[256,1024]{1,0:T(8,128)(2,1)} %bitcast.174), channel_id=1, source_target_pairs={{0,8},{8,0},{1,9},{9,1},{2,10},{10,2},{3,11},{11,3},{4,12},{12,4},... | collective-permute-start | bytes 1572872 | tf_op jit(solution)/shard_map/ppermute | solution.py:686
  248.2 24.5 %copy-start.33 = (f32[1,1024]{1,0:T(1,128)S(1)}, f32[1,1024]{1,0:T(1,128)}, u32[]{:S(2)}) copy-start(f32[1,1024]{1,0:T(1,128)} %get-tuple-element.80) | copy-start | bytes 12292
  248.2 25.3 %copy-start.18 = (bf16[16,2,4,8,384]{4,3,2,1,0:T(8,128)(2,1)S(1)}, bf16[16,2,4,8,384]{4,3,2,1,0:T(8,128)(2,1)}, u32[]{:S(2)}) copy-start(bf16[16,2,4,8,384]{4,3,2,1,0:T(8,128)(2,1)} %copy-done.17) | copy-start | bytes 2359300
  272.6 7.4 %collective-permute-start.14 = (bf16[16,128,1024]{2,1,0:T(8,128)(2,1)}, bf16[16,128,1024]{2,1,0:T(8,128)(2,1)S(1)}, u32[]{:S(2)}, u32[]{:S(2)}) collective-permute-start(bf16[16,128,1024]{2,1,0:T(8,128)(2,1)} %get-tuple-element.78), channel_id=1, source_target_pairs={{0,8},{8,0},{1,9},{9,1},{2,10},{10,2},{3,11},{11,3},{4,12},{12,4},... | collective-permute-start | bytes 12582920 | tf_op jit(solution)/shard_map/ppermute | solution.py:686
  286.8 24.7 %collective-permute-start.15 = (bf16[2,128,1024]{2,1,0:T(8,128)(2,1)}, bf16[2,128,1024]{2,1,0:T(8,128)(2,1)}, u32[]{:S(2)}, u32[]{:S(2)}) collective-permute-start(bf16[2,128,1024]{2,1,0:T(8,128)(2,1)} %get-tuple-element.100), channel_id=1, source_target_pairs={{0,48},{16,0},{32,16},{48,32},{1,49},{17,1},{33,17},{49,33},{2,50}... | collective-permute-start | bytes 1572872 | tf_op jit(solution)/shard_map/ppermute | solution.py:686
  288.6 29.4 %collective-permute-start.17 = (bf16[2,128,1024]{2,1,0:T(8,128)(2,1)}, bf16[2,128,1024]{2,1,0:T(8,128)(2,1)}, u32[]{:S(2)}, u32[]{:S(2)}) collective-permute-start(bf16[2,128,1024]{2,1,0:T(8,128)(2,1)} %get-tuple-element.101), channel_id=1, source_target_pairs={{0,16},{16,32},{32,48},{48,0},{1,17},{17,33},{33,49},{49,1},{2,18}... | collective-permute-start | bytes 1572872 | tf_op jit(solution)/shard_map/ppermute | solution.py:686
  288.8 36.5 %collective-permute-start.16 = (bf16[2,128,1024]{2,1,0:T(8,128)(2,1)}, bf16[2,128,1024]{2,1,0:T(8,128)(2,1)}, u32[]{:S(2)}, u32[]{:S(2)}) collective-permute-start(bf16[2,128,1024]{2,1,0:T(8,128)(2,1)} %get-tuple-element.102), channel_id=1, source_target_pairs={{0,32},{16,48},{32,0},{48,16},{1,33},{17,49},{33,1},{49,17},{2,34}... | collective-permute-start | bytes 1572872 | tf_op jit(solution)/shard_map/ppermute | solution.py:686
  294.0 49.3 %all-to-all-start.3 = ((bf16[8,16,8,512]{3,2,1,0:T(8,128)(2,1)}), bf16[8,16,8,512]{3,2,1,0:T(8,128)(2,1)S(1)}, u32[]{:S(2)}, u32[]{:S(2)}) async-start(bf16[8,16,8,512]{3,2,1,0:T(8,128)(2,1)} %maximum_bitcast_fusion), calls=%async_computation.3 | async-start | bytes 2097152 | tf_op jit(solution)/shard_map/all_to_all | solution.py:881
  301.0 28.9 %copy-start.16 = (bf16[1,256,1024]{2,1,0:T(8,128)(2,1)S(1)}, bf16[1,256,1024]{2,1,0:T(8,128)(2,1)}, u32[]{:S(2)}) copy-start(bf16[1,256,1024]{2,1,0:T(8,128)(2,1)} %param.14) | copy-start | bytes 1572868
  301.0 43.1 %collective-permute-start.19 = (bf16[4,128,1024]{2,1,0:T(8,128)(2,1)}, bf16[4,128,1024]{2,1,0:T(8,128)(2,1)S(1)}, u32[]{:S(2)}, u32[]{:S(2)}) collective-permute-start(bf16[4,128,1024]{2,1,0:T(8,128)(2,1)} %slice.199), channel_id=1, source_target_pairs={{0,64},{64,0},{1,65},{65,1},{2,66},{66,2},{3,67},{67,3},{4,68},{68... | collective-permute-start | bytes 3145736 | tf_op jit(solution)/shard_map/ppermute | solution.py:686
  327.2 16.0 %collective-permute-start.18 = (bf16[128,1024]{1,0:T(8,128)(2,1)S(1)}, bf16[128,1024]{1,0:T(8,128)(2,1)S(1)}, u32[]{:S(2)}, u32[]{:S(2)}) collective-permute-start(bf16[128,1024]{1,0:T(8,128)(2,1)S(1)} %slice_bitcast_fusion.5), channel_id=1, source_target_pairs={{0,64},{64,0},{1,65},{65,1},{2,66},{66,2},{3,67},{67,3},{4,68},{68... | collective-permute-start | bytes 786440 | tf_op jit(solution)/shard_map/ppermute | solution.py:686
  345.8 12.5 %all-to-all-start.4 = ((bf16[16,8,512]{2,1,0:T(8,128)(2,1)}), bf16[16,8,512]{2,1,0:T(8,128)(2,1)S(1)}, u32[]{:S(2)}, u32[]{:S(2)}) async-start(bf16[16,8,512]{2,1,0:T(8,128)(2,1)} %reduce_sum.69), calls=%async_computation.4 | async-start | bytes 262144 | tf_op jit(solution)/shard_map/all_to_all | solution.py:885
  350.0 31.6 %reduce-scatter.5.cloned.1.call-start = ((), (), s32[]{:S(2)}) async-start(), calls=%async_computation.8 | async-start | bytes 901120 | tf_op jit(solution)/shard_map/reduce_scatter | solution.py:902
  350.9 15.5 %collective-permute-start.20 = (bf16[128,1024]{1,0:T(8,128)(2,1)}, bf16[128,1024]{1,0:T(8,128)(2,1)}, u32[]{:S(2)}, u32[]{:S(2)}) collective-permute-start(bf16[128,1024]{1,0:T(8,128)(2,1)} %get-tuple-element.107), channel_id=1, source_target_pairs={{0,48},{16,0},{32,16},{48,32},{1,49},{17,1},{33,17},{49,33},{2,50}... | collective-permute-start | bytes 786440 | tf_op jit(solution)/shard_map/ppermute | solution.py:686
  354.0 15.4 %collective-permute-start.22 = (bf16[128,1024]{1,0:T(8,128)(2,1)}, bf16[128,1024]{1,0:T(8,128)(2,1)}, u32[]{:S(2)}, u32[]{:S(2)}) collective-permute-start(bf16[128,1024]{1,0:T(8,128)(2,1)} %get-tuple-element.108), channel_id=1, source_target_pairs={{0,16},{16,32},{32,48},{48,0},{1,17},{17,33},{33,49},{49,1},{2,18}... | collective-permute-start | bytes 786440 | tf_op jit(solution)/shard_map/ppermute | solution.py:686
  354.0 15.4 %collective-permute-start.21 = (bf16[128,1024]{1,0:T(8,128)(2,1)}, bf16[128,1024]{1,0:T(8,128)(2,1)}, u32[]{:S(2)}, u32[]{:S(2)}) collective-permute-start(bf16[128,1024]{1,0:T(8,128)(2,1)} %get-tuple-element.109), channel_id=1, source_target_pairs={{0,32},{16,48},{32,0},{48,16},{1,33},{17,49},{33,1},{49,17},{2,34}... | collective-permute-start | bytes 786440 | tf_op jit(solution)/shard_map/ppermute | solution.py:686
  371.1 14.2 %copy-start.21 = (f32[8,10240]{1,0:T(8,128)S(1)}, f32[8,10240]{1,0:T(8,128)}, u32[]{:S(2)}) copy-start(f32[8,10240]{1,0:T(8,128)} %param.18) | copy-start | bytes 983044
  371.1 14.2 %copy-start.26 = (f32[8,10240]{1,0:T(8,128)S(1)}, f32[8,10240]{1,0:T(8,128)}, u32[]{:S(2)}) copy-start(f32[8,10240]{1,0:T(8,128)} %param.24) | copy-start | bytes 983044
  371.1 14.2 %copy-start.27 = (f32[8,10240]{1,0:T(8,128)S(1)}, f32[8,10240]{1,0:T(8,128)}, u32[]{:S(2)}) copy-start(f32[8,10240]{1,0:T(8,128)} %param.21) | copy-start | bytes 983044
  371.1 14.2 %copy-start.30 = (f32[8,8,128]{2,1,0:T(8,128)S(1)}, f32[8,8,128]{2,1,0:T(8,128)}, u32[]{:S(2)}) copy-start(f32[8,8,128]{2,1,0:T(8,128)} %get-tuple-element.86) | copy-start | bytes 98308
  372.4 22.3 %copy-start.23 = (f32[40,1024]{1,0:T(8,128)S(1)}, f32[40,1024]{1,0:T(8,128)}, u32[]{:S(2)}) copy-start(f32[40,1024]{1,0:T(8,128)} %param.19) | copy-start | bytes 491524
  372.4 22.3 %copy-start.28 = (f32[40,1024]{1,0:T(8,128)S(1)}, f32[40,1024]{1,0:T(8,128)}, u32[]{:S(2)}) copy-start(f32[40,1024]{1,0:T(8,128)} %param.25) | copy-start | bytes 491524
  372.4 22.4 %copy-start.29 = (f32[40,1024]{1,0:T(8,128)S(1)}, f32[40,1024]{1,0:T(8,128)}, u32[]{:S(2)}) copy-start(f32[40,1024]{1,0:T(8,128)} %param.22) | copy-start | bytes 491524
  382.4 12.3 %collective-permute-start.23 = (f32[40,1024]{1,0:T(8,128)S(1)}, f32[40,1024]{1,0:T(8,128)S(1)}, u32[]{:S(2)}, u32[]{:S(2)}) collective-permute-start(f32[40,1024]{1,0:T(8,128)S(1)} %slice.210), channel_id=1, source_target_pairs={{0,0},{1,4},{2,8},{3,12},{4,1},{5,5},{6,9},{7,13},{8,64},{9,68},{1... | collective-permute-start | bytes 491528 | tf_op jit(solution)/shard_map/ppermute | solution.py:903
  (22 other events, 77.1 us)
Sparse Core Ops, SparseCore 0:
  24.3 34.8 all-gather.7
  61.4 103.9 all-gather.5
  218.4 109.3 reduce-scatter.2
  360.6 20.9 reduce-scatter.4
